TPU v7x, 32 devices: a whole 2x2x4 slice. The times are simulated.
32 devices in a mesh: segment: 2 (over x), tm: 4 (over z), space: 4 (over y, core).
Axes of the slice: x: 2, y: 2, z: 4, core: 2. Of those that a mesh axis runs over, the one named last changes fastest.
Arguments:
- video_clips: float32 [2, 8, 16, 32, 128], P(None, 'tm', 'space'), may hold values from -6 to 6
- conv_weights: float32 [2, 3456, 128], P('segment'), may hold values from -0.109375 to 0.109375
Outputs:
- weight_grads: float32 [2, 3456, 128], P('segment')
All inputs are finite; a program needn't handle non-finite values.
Results may differ from a plain program's by a relative error of at most 0.000091.
Values sent between devices are 32-bit elements; how exact they have to be, the bound alone decides.
No kernel may reach another device: no remote copies, remote signals or barrier semaphores. Data moves between devices by JAX's collectives and lax.ppermute only.
A program may use at most 64 MiB of HBM per device.

v0:
```python
import jax
import jax.numpy as jnp
from jax import lax
from jax.sharding import PartitionSpec as P

highest = lax.Precision.HIGHEST


def from_behind(block, axis, distance):
    devices = range(lax.axis_size(axis))
    route = [(i - distance, i) for i in devices if i - distance in devices]
    return lax.ppermute(block, axis, route)


def with_halo(block, sides, width):
    for axis, dim in sides:
        count = lax.axis_size(axis)
        forward = [(i, i + 1) for i in range(count - 1)]
        backward = [(target, source) for source, target in forward]
        low = lax.ppermute(
            lax.slice_in_dim(block, block.shape[dim] - width, None, axis=dim), axis, forward
        )
        high = lax.ppermute(lax.slice_in_dim(block, 0, width, axis=dim), axis, backward)
        block = jnp.concatenate([low, block, high], axis=dim)
    return block


def segment_pass(values, direction):
    return from_behind(values, "segment", direction)


def extend(field_in, direction):
    boundary = field_in if direction == 1 else field_in
    arrived = from_behind(boundary, "tm", direction)
    if direction == 1:
        joined = jnp.concatenate([arrived, field_in], axis=1)
    else:
        joined = jnp.concatenate([field_in, arrived], axis=1)
    rimmed = with_halo(joined, (("space", 2),), 1)
    return jnp.pad(rimmed, ((0, 0), (0, 0), (0, 0), (1, 1), (0, 0)))


def patches_at(extended, offset, reverse, frames, height, columns):
    pieces = []
    for row_step in range(3):
        for col_step in range(3):
            if reverse:
                pieces.append(
                    extended[
                        :,
                        2 - offset : 2 - offset + frames,
                        2 - row_step : 2 - row_step + height,
                        2 - col_step : 2 - col_step + columns,
                    ]
                )
            else:
                pieces.append(
                    extended[
                        :,
                        offset : offset + frames,
                        row_step : row_step + height,
                        col_step : col_step + columns,
                    ]
                )
    gathered = jnp.concatenate(pieces, axis=-1)
    return gathered.reshape(-1, gathered.shape[-1])


def apply_conv(extended, weight, shape_out, reverse):
    clip_count, frames, height, columns, channels = shape_out
    summed = None
    for offset in range(3):
        patches = patches_at(extended, offset, reverse, frames, height, columns)
        weight_block = weight[offset * 9 * channels : (offset + 1) * 9 * channels]
        if reverse:
            weight_block = (
                weight_block.reshape(9, channels, channels)
                .transpose(0, 2, 1)
                .reshape(9 * channels, channels)
            )
        partial_value = jnp.dot(
            patches, weight_block, precision=highest, preferred_element_type=jnp.float32
        )
        summed = partial_value if summed is None else summed + partial_value
    return summed.reshape(shape_out)


def weight_terms(extended, grad_out, offset):
    clip_count, frames, height, columns, channels = grad_out.shape
    patches = patches_at(extended, offset, False, frames, height, columns)
    flattened = grad_out.reshape(-1, channels)
    return lax.dot_general(
        patches,
        flattened,
        (((0,), (0,)), ((), ())),
        precision=highest,
        preferred_element_type=jnp.float32,
    )


def summed_grads(pairs):
    stacked = jnp.stack(
        [
            jnp.concatenate([weight_terms(ext, grad, offset) for offset in range(3)], axis=0)
            for ext, grad in pairs
        ]
    )
    return lax.psum(stacked, ("tm", "space"))


def silu_slope(values):
    sigmoid = jax.nn.sigmoid(values)
    return sigmoid * (1.0 + values * (1.0 - sigmoid))


def local(video_clips, conv_weights):
    clip_count, frames, height, columns, channels = video_clips.shape
    cell_count = (
        clip_count * frames * lax.axis_size("tm") * height * lax.axis_size("space") * columns
    )
    factor = float(cell_count) ** (-0.5)
    weight = conv_weights[0]
    encoding = lax.axis_index("segment") == 0
    received = jnp.zeros_like(video_clips[:1])
    ext_list = []
    out_list = []
    for tick_index in range(clip_count + 1):
        if tick_index < clip_count:
            own_clip = video_clips[tick_index : tick_index + 1]
        else:
            own_clip = jnp.zeros_like(received)
        inputs = jnp.where(encoding, own_clip, received)
        extended = extend(inputs, 1)
        result = apply_conv(extended, weight, inputs.shape, False)
        ext_list.append(extended)
        out_list.append(result)
        if tick_index < clip_count:
            received = segment_pass(jax.nn.silu(result), 1)
    own_ext = jnp.where(
        encoding, jnp.concatenate(ext_list[:-1], axis=0), jnp.concatenate(ext_list[1:], axis=0)
    )
    produced = jnp.where(
        encoding, jnp.concatenate(out_list[:-1], axis=0), jnp.concatenate(out_list[1:], axis=0)
    )
    cotangent = jnp.where(encoding, 0.0, (produced - video_clips) * factor)
    grad_latent = apply_conv(extend(cotangent, -1), weight, video_clips.shape, True)
    returned = segment_pass(grad_latent, -1)
    grad_out = jnp.where(encoding, returned * silu_slope(produced), cotangent)
    return summed_grads([(own_ext, grad_out)])


def solution(mesh):
    return jax.shard_map(
        local,
        mesh=mesh,
        in_specs=(P(None, "tm", "space", None, None), P("segment", None, None)),
        out_specs=P("segment", None, None),
        check_vma=False,
    )
```

profile of v0, /device:TPU:0, one launch (start us, length us, event | category | flops | bytes accessed | tf_op | source)
XLA Modules:
  0.0 238.6 jit_solution(2863225284892522858)
XLA Ops:
  7.5 4.9 %collective-permute-start = (f32[1,2,4,32,128]{4,3,2,1,0:T(8,128)S(1)}, f32[1,2,4,32,128]{4,3,2,1,0:T(8,128)S(1)}, u32[]{:S(2)}, u32[]{:S(2)}) collective-permute-start(f32[1,2,4,32,128]{4,3,2,1,0:T(8,128)S(1)} %slice_select_fusion.1), channel_id=1, source_target_pairs={{0,4},{4,8},{8,12},{1,5},{5,9},{9,13},{2,6},{6,10},{10,14},{3,7},{... | collective-permute-start | bytes 393224 | tf_op jit(solution)/shard_map/ppermute | solution.py:12
  12.4 2.7 %collective-permute-done = f32[1,2,4,32,128]{4,3,2,1,0:T(8,128)S(1)} collective-permute-done((f32[1,2,4,32,128]{4,3,2,1,0:T(8,128)S(1)}, f32[1,2,4,32,128]{4,3,2,1,0:T(8,128)S(1)}, u32[]{:S(2)}, u32[]{:S(2)}) %collective-permute-start) | collective-permute-done | bytes 131104 | tf_op jit(solution)/shard_map/ppermute | solution.py:12
  17.8 3.6 %collective-permute-done.2 = f32[1,4,1,32,128]{4,3,2,1,0:T(8,128)S(1)} collective-permute-done((f32[1,4,1,32,128]{4,3,2,1,0:T(8,128)S(1)}, f32[1,4,1,32,128]{4,3,2,1,0:T(8,128)S(1)}, u32[]{:S(2)}, u32[]{:S(2)}) %collective-permute-start.2) | collective-permute-done | bytes 65568 | tf_op jit(solution)/shard_map/ppermute | solution.py:23
  26.7 3.4 %collective-permute-start.3 = (f32[1,2,4,32,128]{4,3,2,1,0:T(8,128)S(1)}, f32[1,2,4,32,128]{4,3,2,1,0:T(8,128)S(1)}, u32[]{:S(2)}, u32[]{:S(2)}) collective-permute-start(f32[1,2,4,32,128]{4,3,2,1,0:T(8,128)S(1)} %divide_multiply_fusion.1), channel_id=1, source_target_pairs={{0,16},{1,17},{2,18},{3,19},{4,20},{5,21},{6,22},{7,23},{8,24},{9,... | collective-permute-start | bytes 393224 | tf_op jit(solution)/shard_map/ppermute | solution.py:12
  30.1 2.5 %collective-permute-done.3 = f32[1,2,4,32,128]{4,3,2,1,0:T(8,128)S(1)} collective-permute-done((f32[1,2,4,32,128]{4,3,2,1,0:T(8,128)S(1)}, f32[1,2,4,32,128]{4,3,2,1,0:T(8,128)S(1)}, u32[]{:S(2)}, u32[]{:S(2)}) %collective-permute-start.3) | collective-permute-done | bytes 131104 | tf_op jit(solution)/shard_map/ppermute | solution.py:12
  32.6 4.4 %collective-permute-start.4 = (f32[1,2,4,32,128]{4,3,2,1,0:T(8,128)S(1)}, f32[1,2,4,32,128]{4,3,2,1,0:T(8,128)S(1)}, u32[]{:S(2)}, u32[]{:S(2)}) collective-permute-start(f32[1,2,4,32,128]{4,3,2,1,0:T(8,128)S(1)} %slice_select_fusion), channel_id=1, source_target_pairs={{0,4},{4,8},{8,12},{1,5},{5,9},{9,13},{2,6},{6,10},{10,14},{3,7},{... | collective-permute-start | bytes 393224 | tf_op jit(solution)/shard_map/ppermute | solution.py:12
  37.0 2.7 %collective-permute-done.4 = f32[1,2,4,32,128]{4,3,2,1,0:T(8,128)S(1)} collective-permute-done((f32[1,2,4,32,128]{4,3,2,1,0:T(8,128)S(1)}, f32[1,2,4,32,128]{4,3,2,1,0:T(8,128)S(1)}, u32[]{:S(2)}, u32[]{:S(2)}) %collective-permute-start.4) | collective-permute-done | bytes 131104 | tf_op jit(solution)/shard_map/ppermute | solution.py:12
  39.8 3.1 %collective-permute-start.5 = (f32[1,4,1,32,128]{4,3,2,1,0:T(8,128)S(1)}, f32[1,4,1,32,128]{4,3,2,1,0:T(8,128)S(1)}, u32[]{:S(2)}, u32[]{:S(2)}) collective-permute-start(f32[1,4,1,32,128]{4,3,2,1,0:T(8,128)S(1)} %get-tuple-element.144), channel_id=1, source_target_pairs={{0,1},{1,2},{2,3},{4,5},{5,6},{6,7},{8,9},{9,10},{10,11},{12,13},{... | collective-permute-start | bytes 196616 | tf_op jit(solution)/shard_map/ppermute | solution.py:20
  44.2 2.8 %collective-permute-done.6 = f32[1,4,1,32,128]{4,3,2,1,0:T(8,128)S(1)} collective-permute-done((f32[1,4,1,32,128]{4,3,2,1,0:T(8,128)S(1)}, f32[1,4,1,32,128]{4,3,2,1,0:T(8,128)S(1)}, u32[]{:S(2)}, u32[]{:S(2)}) %collective-permute-start.6) | collective-permute-done | bytes 65568 | tf_op jit(solution)/shard_map/ppermute | solution.py:23
  51.0 4.4 %collective-permute-start.7 = (f32[1,2,4,32,128]{4,3,2,1,0:T(8,128)S(1)}, f32[1,2,4,32,128]{4,3,2,1,0:T(8,128)S(1)}, u32[]{:S(2)}, u32[]{:S(2)}) collective-permute-start(f32[1,2,4,32,128]{4,3,2,1,0:T(8,128)S(1)} %divide_multiply_fusion), channel_id=1, source_target_pairs={{0,16},{1,17},{2,18},{3,19},{4,20},{5,21},{6,22},{7,23},{8,24},{9,... | collective-permute-start | bytes 393224 | tf_op jit(solution)/shard_map/ppermute | solution.py:12
  55.3 2.5 %collective-permute-done.7 = f32[1,2,4,32,128]{4,3,2,1,0:T(8,128)S(1)} collective-permute-done((f32[1,2,4,32,128]{4,3,2,1,0:T(8,128)S(1)}, f32[1,2,4,32,128]{4,3,2,1,0:T(8,128)S(1)}, u32[]{:S(2)}, u32[]{:S(2)}) %collective-permute-start.7) | collective-permute-done | bytes 131104 | tf_op jit(solution)/shard_map/ppermute | solution.py:12
  57.9 4.4 %collective-permute-start.8 = (f32[1,2,4,32,128]{4,3,2,1,0:T(8,128)S(1)}, f32[1,2,4,32,128]{4,3,2,1,0:T(8,128)S(1)}, u32[]{:S(2)}, u32[]{:S(2)}) collective-permute-start(f32[1,2,4,32,128]{4,3,2,1,0:T(8,128)S(1)} %broadcast_select_fusion), channel_id=1, source_target_pairs={{0,4},{4,8},{8,12},{1,5},{5,9},{9,13},{2,6},{6,10},{10,14},{3,7},{... | collective-permute-start | bytes 393224 | tf_op jit(solution)/shard_map/ppermute | solution.py:12
  62.2 2.7 %collective-permute-done.8 = f32[1,2,4,32,128]{4,3,2,1,0:T(8,128)S(1)} collective-permute-done((f32[1,2,4,32,128]{4,3,2,1,0:T(8,128)S(1)}, f32[1,2,4,32,128]{4,3,2,1,0:T(8,128)S(1)}, u32[]{:S(2)}, u32[]{:S(2)}) %collective-permute-start.8) | collective-permute-done | bytes 131104 | tf_op jit(solution)/shard_map/ppermute | solution.py:12
  67.0 4.4 %collective-permute-start.9 = (f32[1,4,1,32,128]{4,3,2,1,0:T(8,128)}, f32[1,4,1,32,128]{4,3,2,1,0:T(8,128)}, u32[]{:S(2)}, u32[]{:S(2)}) collective-permute-start(f32[1,4,1,32,128]{4,3,2,1,0:T(8,128)} %get-tuple-element.140), channel_id=1, source_target_pairs={{0,1},{1,2},{2,3},{4,5},{5,6},{6,7},{8,9},{9,10},{10,11},{12,13},{... | collective-permute-start | bytes 196616 | tf_op jit(solution)/shard_map/ppermute | solution.py:20
  72.5 2.1 copy.3
  74.6 2.1 copy.4
  86.5 8.8 %collective-permute-done.11 = f32[2,2,4,32,128]{4,3,2,1,0:T(8,128)S(1)} collective-permute-done((f32[2,2,4,32,128]{4,3,2,1,0:T(8,128)S(1)}, f32[2,2,4,32,128]{4,3,2,1,0:T(8,128)S(1)}, u32[]{:S(2)}, u32[]{:S(2)}) %collective-permute-start.11) | collective-permute-done | bytes 262176 | tf_op jit(solution)/shard_map/ppermute | solution.py:12
  95.3 2.3 collective-permute-start.12
  111.2 6.6 %collective-permute-done.14 = f32[2,2,4,32,128]{4,3,2,1,0:T(8,128)S(1)} collective-permute-done((f32[2,2,4,32,128]{4,3,2,1,0:T(8,128)S(1)}, f32[2,2,4,32,128]{4,3,2,1,0:T(8,128)S(1)}, u32[]{:S(2)}, u32[]{:S(2)}) %collective-permute-start.14) | collective-permute-done | bytes 262176 | tf_op jit(solution)/shard_map/ppermute | solution.py:12
  118.0 3.9 %convolution_bitcast_fusion.2 = f32[1152,128]{1,0:T(8,128)S(1)} fusion(f32[2,2,4,32,1152]{4,3,2,1,0:T(8,128)S(1)} %get-tuple-element.8, f32[2,2,4,32,128]{4,3,2,1,0:T(8,128)S(1)} %multiply_select_fusion), kind=kOutput, calls=%fused_computation.2 | convolution fusion | flops 905969664 | bytes 3211264 | tf_op jit(solution)/shard_map/dot_general | solution.py:92
  121.9 3.9 %convolution_bitcast_fusion.1 = f32[1152,128]{1,0:T(8,128)S(1)} fusion(f32[2,2,4,32,1152]{4,3,2,1,0:T(8,128)S(1)} %get-tuple-element.10, f32[2,2,4,32,128]{4,3,2,1,0:T(8,128)S(1)} %multiply_select_fusion), kind=kOutput, calls=%fused_computation.1 | convolution fusion | flops 905969664 | bytes 3211264 | tf_op jit(solution)/shard_map/dot_general | solution.py:92
  125.9 3.9 %convolution_bitcast_fusion = f32[1152,128]{1,0:T(8,128)S(1)} fusion(f32[2,2,4,32,1152]{4,3,2,1,0:T(8,128)S(1)} %get-tuple-element.9, f32[2,2,4,32,128]{4,3,2,1,0:T(8,128)S(1)} %multiply_select_fusion), kind=kOutput, calls=%fused_computation | convolution fusion | flops 905969664 | bytes 3211264 | tf_op jit(solution)/shard_map/dot_general | solution.py:92
  131.1 97.8 %all-reduce.6.cloned.1.call-done = f32[1,3456,128]{2,1,0:T(8,128)} async-done(((f32[1,3456,128]{2,1,0:T(8,128)}), f32[1,3456,128]{2,1,0:T(8,128)}) %all-reduce.6.cloned.1.call-update) | async-done | bytes 1769488 | tf_op jit(solution)/shard_map/psum | solution.py:108
  228.9 2.8 %copy.130 = f32[1,3456,128]{2,1,0:T(8,128)} copy(f32[1,3456,128]{2,1,0:T(8,128)} %all-reduce.6.cloned.1.call-done) | data formatting | bytes 3538944
  (119 shorter events, 41.5 us)
Async XLA Ops:
  6.5 222.4 %all-reduce.6.cloned.1.call-start = ((), (), s32[]{:S(2)}) async-start(), calls=%async_computation | async-start | bytes 3538944 | tf_op jit(solution)/shard_map/psum | solution.py:108
  7.5 7.7 %collective-permute-start = (f32[1,2,4,32,128]{4,3,2,1,0:T(8,128)S(1)}, f32[1,2,4,32,128]{4,3,2,1,0:T(8,128)S(1)}, u32[]{:S(2)}, u32[]{:S(2)}) collective-permute-start(f32[1,2,4,32,128]{4,3,2,1,0:T(8,128)S(1)} %slice_select_fusion.1), channel_id=1, source_target_pairs={{0,4},{4,8},{8,12},{1,5},{5,9},{9,13},{2,6},{6,10},{10,14},{3,7},{... | collective-permute-start | bytes 393224 | tf_op jit(solution)/shard_map/ppermute | solution.py:12
  15.1 2.6 %collective-permute-start.1 = (f32[1,4,1,32,128]{4,3,2,1,0:T(8,128)S(1)}, f32[1,4,1,32,128]{4,3,2,1,0:T(8,128)S(1)}, u32[]{:S(2)}, u32[]{:S(2)}) collective-permute-start(f32[1,4,1,32,128]{4,3,2,1,0:T(8,128)S(1)} %get-tuple-element.148), channel_id=1, source_target_pairs={{0,1},{1,2},{2,3},{4,5},{5,6},{6,7},{8,9},{9,10},{10,11},{12,13},{... | collective-permute-start | bytes 196616 | tf_op jit(solution)/shard_map/ppermute | solution.py:20
  16.4 4.9 %collective-permute-start.2 = (f32[1,4,1,32,128]{4,3,2,1,0:T(8,128)S(1)}, f32[1,4,1,32,128]{4,3,2,1,0:T(8,128)S(1)}, u32[]{:S(2)}, u32[]{:S(2)}) collective-permute-start(f32[1,4,1,32,128]{4,3,2,1,0:T(8,128)S(1)} %get-tuple-element.149), channel_id=1, source_target_pairs={{1,0},{2,1},{3,2},{5,4},{6,5},{7,6},{9,8},{10,9},{11,10},{13,12},{... | collective-permute-start | bytes 196616 | tf_op jit(solution)/shard_map/ppermute | solution.py:23
  21.8 1.5 copy-start
  25.5 7.1 %copy-start.1 = (f32[2,2,4,32,128]{4,3,2,1,0:T(8,128)S(1)}, f32[2,2,4,32,128]{4,3,2,1,0:T(8,128)}, u32[]{:S(2)}) copy-start(f32[2,2,4,32,128]{4,3,2,1,0:T(8,128)} %param.2) | copy-start | bytes 786436
  26.6 3.5 %copy-start.6 = (f32[256,128]{1,0:T(8,128)}, f32[256,128]{1,0:T(8,128)S(1)}, u32[]{:S(2)}) copy-start(f32[256,128]{1,0:T(8,128)S(1)} %convolution_add_fusion.6) | copy-start | bytes 393220
  26.7 5.9 %collective-permute-start.3 = (f32[1,2,4,32,128]{4,3,2,1,0:T(8,128)S(1)}, f32[1,2,4,32,128]{4,3,2,1,0:T(8,128)S(1)}, u32[]{:S(2)}, u32[]{:S(2)}) collective-permute-start(f32[1,2,4,32,128]{4,3,2,1,0:T(8,128)S(1)} %divide_multiply_fusion.1), channel_id=1, source_target_pairs={{0,16},{1,17},{2,18},{3,19},{4,20},{5,21},{6,22},{7,23},{8,24},{9,... | collective-permute-start | bytes 393224 | tf_op jit(solution)/shard_map/ppermute | solution.py:12
  32.6 7.1 %collective-permute-start.4 = (f32[1,2,4,32,128]{4,3,2,1,0:T(8,128)S(1)}, f32[1,2,4,32,128]{4,3,2,1,0:T(8,128)S(1)}, u32[]{:S(2)}, u32[]{:S(2)}) collective-permute-start(f32[1,2,4,32,128]{4,3,2,1,0:T(8,128)S(1)} %slice_select_fusion), channel_id=1, source_target_pairs={{0,4},{4,8},{8,12},{1,5},{5,9},{9,13},{2,6},{6,10},{10,14},{3,7},{... | collective-permute-start | bytes 393224 | tf_op jit(solution)/shard_map/ppermute | solution.py:12
  39.8 4.5 %collective-permute-start.5 = (f32[1,4,1,32,128]{4,3,2,1,0:T(8,128)S(1)}, f32[1,4,1,32,128]{4,3,2,1,0:T(8,128)S(1)}, u32[]{:S(2)}, u32[]{:S(2)}) collective-permute-start(f32[1,4,1,32,128]{4,3,2,1,0:T(8,128)S(1)} %get-tuple-element.144), channel_id=1, source_target_pairs={{0,1},{1,2},{2,3},{4,5},{5,6},{6,7},{8,9},{9,10},{10,11},{12,13},{... | collective-permute-start | bytes 196616 | tf_op jit(solution)/shard_map/ppermute | solution.py:20
  42.9 4.1 %collective-permute-start.6 = (f32[1,4,1,32,128]{4,3,2,1,0:T(8,128)S(1)}, f32[1,4,1,32,128]{4,3,2,1,0:T(8,128)S(1)}, u32[]{:S(2)}, u32[]{:S(2)}) collective-permute-start(f32[1,4,1,32,128]{4,3,2,1,0:T(8,128)S(1)} %get-tuple-element.145), channel_id=1, source_target_pairs={{1,0},{2,1},{3,2},{5,4},{6,5},{7,6},{9,8},{10,9},{11,10},{13,12},{... | collective-permute-start | bytes 196616 | tf_op jit(solution)/shard_map/ppermute | solution.py:23
  50.9 16.0 %copy-start.8 = (f32[256,128]{1,0:T(8,128)}, f32[256,128]{1,0:T(8,128)S(1)}, u32[]{:S(2)}) copy-start(f32[256,128]{1,0:T(8,128)S(1)} %convolution_add_fusion.4) | copy-start | bytes 393220
  51.0 6.9 %collective-permute-start.7 = (f32[1,2,4,32,128]{4,3,2,1,0:T(8,128)S(1)}, f32[1,2,4,32,128]{4,3,2,1,0:T(8,128)S(1)}, u32[]{:S(2)}, u32[]{:S(2)}) collective-permute-start(f32[1,2,4,32,128]{4,3,2,1,0:T(8,128)S(1)} %divide_multiply_fusion), channel_id=1, source_target_pairs={{0,16},{1,17},{2,18},{3,19},{4,20},{5,21},{6,22},{7,23},{8,24},{9,... | collective-permute-start | bytes 393224 | tf_op jit(solution)/shard_map/ppermute | solution.py:12
  57.9 7.1 %collective-permute-start.8 = (f32[1,2,4,32,128]{4,3,2,1,0:T(8,128)S(1)}, f32[1,2,4,32,128]{4,3,2,1,0:T(8,128)S(1)}, u32[]{:S(2)}, u32[]{:S(2)}) collective-permute-start(f32[1,2,4,32,128]{4,3,2,1,0:T(8,128)S(1)} %broadcast_select_fusion), channel_id=1, source_target_pairs={{0,4},{4,8},{8,12},{1,5},{5,9},{9,13},{2,6},{6,10},{10,14},{3,7},{... | collective-permute-start | bytes 393224 | tf_op jit(solution)/shard_map/ppermute | solution.py:12
  65.0 2.0 copy-start.10
  65.7 12.1 %collective-permute-start.10 = (f32[1,4,1,32,128]{4,3,2,1,0:T(8,128)}, f32[1,4,1,32,128]{4,3,2,1,0:T(8,128)S(1)}, u32[]{:S(2)}, u32[]{:S(2)}) collective-permute-start(f32[1,4,1,32,128]{4,3,2,1,0:T(8,128)} %get-tuple-element.141), channel_id=1, source_target_pairs={{1,0},{2,1},{3,2},{5,4},{6,5},{7,6},{9,8},{10,9},{11,10},{13,12},{... | collective-permute-start | bytes 196616 | tf_op jit(solution)/shard_map/ppermute | solution.py:23
  67.0 10.8 %collective-permute-start.9 = (f32[1,4,1,32,128]{4,3,2,1,0:T(8,128)}, f32[1,4,1,32,128]{4,3,2,1,0:T(8,128)}, u32[]{:S(2)}, u32[]{:S(2)}) collective-permute-start(f32[1,4,1,32,128]{4,3,2,1,0:T(8,128)} %get-tuple-element.140), channel_id=1, source_target_pairs={{0,1},{1,2},{2,3},{4,5},{5,6},{6,7},{8,9},{9,10},{10,11},{12,13},{... | collective-permute-start | bytes 196616 | tf_op jit(solution)/shard_map/ppermute | solution.py:20
  83.3 1.2 copy-start.2
  84.6 10.7 %collective-permute-start.11 = (f32[2,2,4,32,128]{4,3,2,1,0:T(8,128)S(1)}, f32[2,2,4,32,128]{4,3,2,1,0:T(8,128)S(1)}, u32[]{:S(2)}, u32[]{:S(2)}) collective-permute-start(f32[2,2,4,32,128]{4,3,2,1,0:T(8,128)S(1)} %multiply_select_fusion.1), channel_id=1, source_target_pairs={{4,0},{8,4},{12,8},{5,1},{9,5},{13,9},{6,2},{10,6},{14,10},{7,3},{... | collective-permute-start | bytes 786440 | tf_op jit(solution)/shard_map/ppermute | solution.py:12
  95.3 3.7 %collective-permute-start.12 = (f32[2,4,1,32,128]{4,3,2,1,0:T(8,128)S(1)}, f32[2,4,1,32,128]{4,3,2,1,0:T(8,128)S(1)}, u32[]{:S(2)}, u32[]{:S(2)}) collective-permute-start(f32[2,4,1,32,128]{4,3,2,1,0:T(8,128)S(1)} %get-tuple-element.61), channel_id=1, source_target_pairs={{0,1},{1,2},{2,3},{4,5},{5,6},{6,7},{8,9},{9,10},{10,11},{12,13},{... | collective-permute-start | bytes 393224 | tf_op jit(solution)/shard_map/ppermute | solution.py:20
  97.6 3.4 %collective-permute-start.13 = (f32[2,4,1,32,128]{4,3,2,1,0:T(8,128)S(1)}, f32[2,4,1,32,128]{4,3,2,1,0:T(8,128)S(1)}, u32[]{:S(2)}, u32[]{:S(2)}) collective-permute-start(f32[2,4,1,32,128]{4,3,2,1,0:T(8,128)S(1)} %get-tuple-element.62), channel_id=1, source_target_pairs={{1,0},{2,1},{3,2},{5,4},{6,5},{7,6},{9,8},{10,9},{11,10},{13,12},{... | collective-permute-start | bytes 393224 | tf_op jit(solution)/shard_map/ppermute | solution.py:23
  103.1 2.1 copy-start.4
  105.2 2.1 copy-start.3
  109.5 8.3 %collective-permute-start.14 = (f32[2,2,4,32,128]{4,3,2,1,0:T(8,128)S(1)}, f32[2,2,4,32,128]{4,3,2,1,0:T(8,128)S(1)}, u32[]{:S(2)}, u32[]{:S(2)}) collective-permute-start(f32[2,2,4,32,128]{4,3,2,1,0:T(8,128)S(1)} %bitcast.110), channel_id=1, source_target_pairs={{16,0},{17,1},{18,2},{19,3},{20,4},{21,5},{22,6},{23,7},{24,8},{25... | collective-permute-start | bytes 786440 | tf_op jit(solution)/shard_map/ppermute | solution.py:12
  (4 other events, 4.3 us)
Sparse Core Ops, SparseCore 0:
  131.3 97.6 all-reduce.5
where the time goes:
time: 239 us
  waiting for transfers between devices  135 us (56%)
  starting transfers between devices  40.5 us (17%)
  matrix products  28.3 us (12%)
  local copies, waits for them, and re-layouts  14.9 us (6%)
  between operations  14.2 us (6%)
  other arithmetic  6.02 us (3%)
    psum x1, waiting for transfers between devices, summed_grads(): return lax.psum(stacked, ('tm', 'space'))  97.8 us
    ppermute x7, waiting for transfers between devices, from_behind(): return lax.ppermute(block, axis, route)  28.6 us
    ppermute x7, starting transfers between devices, from_behind(): return lax.ppermute(block, axis, route)  24.3 us
    dot_general x12, matrix products, apply_conv(): jnp.dot(patches, weight_block, precision=highest, preferred_element_type=...  16.4 us
    dot_general x3, matrix products, weight_terms(): lax.dot_general(patches, flattened, (((0,), (0,)), ((), ())), precision=h...  11.8 us
    ppermute x4, starting transfers between devices, with_halo(): lax.ppermute(lax.slice_in_dim(block, block.shape[dim] - width, None, axis...  11.1 us
    ppermute x4, waiting for transfers between devices, with_halo(): lax.ppermute(lax.slice_in_dim(block, 0, width, axis=dim), axis, backward)  8.29 us
    unnamed x61, local copies, waits for them, and re-layouts  8.13 us
  transfers between devices with their start and end apart: 16, of which 11 were waited for; matrix products, arithmetic and copies ran while one was open for 3% of the time, Pallas kernels for 0%

commit v1 on v0

v1 whole, which is shorter than its diff:
```python
import functools

import jax
import jax.numpy as jnp
from jax import lax
from jax.experimental import pallas as pl
from jax.experimental.pallas import tpu as pltpu
from jax.sharding import PartitionSpec as P

f32 = jnp.float32
bf16 = jnp.bfloat16
AXES = ("segment", "tm", "space")
VMEM_LIMIT = 56 * 1024 * 1024


def split(x):
    high = x.astype(bf16)
    low = (x - high.astype(f32)).astype(bf16)
    return high, low


def dot(a, b):
    return jnp.dot(a, b, preferred_element_type=f32)


def rotate(x, amount, axis):
    size = x.shape[axis]
    amount = amount % size
    if amount == 0:
        return x
    return jnp.concatenate(
        [lax.slice_in_dim(x, size - amount, size, axis=axis), lax.slice_in_dim(x, 0, size - amount, axis=axis)],
        axis=axis,
    )


def column_triple(x):
    column = lax.broadcasted_iota(jnp.int32, x.shape, x.ndim - 2)
    before = jnp.where(column == 0, 0.0, rotate(x, 1, x.ndim - 2))
    after = jnp.where(column == x.shape[-2] - 1, 0.0, rotate(x, -1, x.ndim - 2))
    return [before, x, after]


def store_triple(high_ref, low_ref, index, x):
    channels = x.shape[-1]
    for i, part in enumerate(column_triple(x)):
        high, low = split(part)
        lanes = pl.ds(i * channels, channels)
        high_ref[index + (slice(None), lanes)] = high
        low_ref[index + (slice(None), lanes)] = low


def activations_kernel(
    dims, at_ref, block_ref, up_ref, down_ref, own_ref, mine_ref, other_ref,
    sent_ref, values_ref,
    xh, xl, lh, ll, ch, cl, weight, weight_t, video, hidden, grads,
):
    tm, own_frames, height, rows_all, columns, channels, factor = dims
    frames = tm * own_frames
    per = height // tm
    cells = frames * columns
    segment, z, p = at_ref[0], at_ref[1], at_ref[2]
    core = lax.rem(p, 2)
    half = own_ref.shape[0] // 2

    def put_weight(which, start, ref, rows, offset):
        step = 128
        for r in range(0, rows, step):
            n = min(step, rows - r)
            high, low = split(ref[pl.ds(offset + r, n), :])
            at = pl.ds(pl.multiple_of(start + r, 16), n)
            weight[which, at, pl.ds(0, channels)] = high
            weight[which, at, pl.ds(channels, channels)] = low

    put_weight(segment, 0, own_ref, own_ref.shape[0], 0)
    put_weight(1 - segment, core * half, mine_ref, half, 0)
    put_weight(1 - segment, (1 - core) * half, other_ref, half, 0)

    for ref in (xh, xl, lh, ll):
        ref[:, 0:2] = jnp.zeros((ref.shape[0], 2) + ref.shape[2:], bf16)
    for ref in (ch, cl):
        ref[:, frames:] = jnp.zeros((ref.shape[0], 2) + ref.shape[2:], bf16)
    values_ref[:, :, 0:2] = jnp.zeros((2, height + 2, 2, columns, 2 * channels), bf16)
    for k in range(tm):
        first = lax.rem(z - k + tm, tm) * own_frames
        for row in range(-3, height + 3):
            if row < 0:
                x = up_ref[k, :, 3 + row]
            elif row < height:
                x = block_ref[k, :, row]
            else:
                x = down_ref[k, :, row - height]
            store_triple(xh, xl, (row + 3, pl.ds(first + 2, own_frames)), x)
            if -1 <= row <= height:
                video[row + 1, pl.ds(first, own_frames)] = x
                high, low = split(x)
                at = pl.ds(first + 2, own_frames)
                values_ref[0, row + 1, at, :, pl.ds(0, channels)] = high
                values_ref[0, row + 1, at, :, pl.ds(channels, channels)] = low

    def convolved(high_ref, low_ref, row, count, which):
        high, low = [], []
        for a in range(3):
            for b in range(3):
                at = (pl.ds(row + b, count), pl.ds(a, frames))
                high.append(high_ref[at].reshape(count * cells, 3 * channels))
                low.append(low_ref[at].reshape(count * cells, 3 * channels))
        both = dot(jnp.concatenate(high, axis=1), weight[which])
        rest = dot(jnp.concatenate(low, axis=1), weight[which, :, pl.ds(0, channels)])
        return both[:, :channels] + both[:, channels:] + rest

    group = 2

    @pl.loop(0, (height + 4) // group)
    def _(i):
        row = i * group
        value = convolved(xh, xl, row, group, 0).reshape(group, frames, columns, channels)
        for j in range(group):
            place = p * height - 2 + row + j
            inside = jnp.logical_and(place >= 0, place < rows_all)
            one = value[j]
            hidden[row + j] = one
            latent = jnp.where(inside, one / (1.0 + jnp.exp(-one)), 0.0)
            store_triple(lh, ll, (row + j, pl.ds(2, frames)), latent)

    for row in range(height + 2):
        values_ref[1, row, pl.ds(2, frames), :, pl.ds(0, channels)] = lh[
            row + 1, pl.ds(2, frames), :, pl.ds(channels, channels)
        ]
        values_ref[1, row, pl.ds(2, frames), :, pl.ds(channels, channels)] = ll[
            row + 1, pl.ds(2, frames), :, pl.ds(channels, channels)
        ]

    for j in range(per + 2):
        row = z * per - 1 + j
        decoded = convolved(lh, ll, row + 1, 1, 1).reshape(frames, columns, channels)
        place = p * height + row
        inside = jnp.logical_and(place >= 0, place < rows_all)
        cotangent = jnp.where(inside, (decoded - video[row + 1]) * factor, 0.0)
        store_triple(ch, cl, (j, pl.ds(0, frames)), cotangent)
        if 1 <= j <= per:
            grads[1, :, pl.ds((j - 1) * cells, cells)] = cotangent.reshape(cells, channels).T

    for tap in range(9):
        for e in range(3):
            at = pl.ds((tap * 3 + 2 - e) * channels, channels)
            to = pl.ds((tap * 3 + e) * channels, channels)
            for part in range(2):
                lanes = pl.ds(part * channels, channels)
                weight_t[to, lanes] = weight[1, at, lanes].astype(f32).T.astype(bf16)

    for j in range(per):
        high, low = [], []
        for a in range(3):
            for b in range(3):
                at = (j + 2 - b, pl.ds(2 - a, frames))
                high.append(ch[at].reshape(cells, 3 * channels))
                low.append(cl[at].reshape(cells, 3 * channels))
        both = dot(jnp.concatenate(high, axis=1), weight_t[...])
        rest = dot(jnp.concatenate(low, axis=1), weight_t[:, pl.ds(0, channels)])
        grad_latent = both[:, :channels] + both[:, channels:] + rest
        value = hidden[z * per + j + 2].reshape(cells, channels)
        sigmoid = 1.0 / (1.0 + jnp.exp(-value))
        grad = grad_latent * (sigmoid * (1.0 + value * (1.0 - sigmoid)))
        grads[0, :, pl.ds(j * cells, cells)] = grad.T

    part = channels // tm
    for k in range(tm):
        target = lax.rem(z + k, tm)
        at = pl.ds(pl.multiple_of(target * part, part), part)
        for which in range(2):
            sent_ref[k, which] = grads[which, at, :]


def weights_kernel(dims, at_ref, *refs):
    tm, own_frames, height, rows_all, columns, channels, pairs = dims
    pieces, (values_ref, keep_ref, send_ref, field) = refs[:tm], refs[tm:]
    frames = tm * own_frames
    per = height // tm
    cells = frames * columns
    part = channels // tm
    share = part // 2
    width = share // pairs
    segment, z, p = at_ref[0], at_ref[1], at_ref[2]
    core = lax.rem(p, 2)
    y = lax.div(p, 2)

    for relative in range(2):
        which = segment if relative == 0 else 1 - segment
        for k in range(tm):
            first = lax.rem(z - k + tm, tm) * per
            ordered = []
            for side in range(2):
                its = core if side == 0 else 1 - core
                for step in range(pairs):
                    its_y = lax.rem(y + step, pairs)
                    start = its * share + its_y * width
                    ordered.append(pieces[k][which, pl.ds(start, width), :])
            x = jnp.concatenate(ordered, axis=0)
            for j in range(per):
                row = x[:, j * cells : (j + 1) * cells]
                column = lax.rem(lax.broadcasted_iota(jnp.int32, row.shape, 1), columns)
                after = jnp.where(column == columns - 1, 0.0, rotate(row, -1, 1))
                before = jnp.where(column == 0, 0.0, rotate(row, 1, 1))
                high, low = split(jnp.concatenate([after, row, before], axis=0))
                field[relative, first + j, pl.ds(0, 3 * part), :] = high
                field[relative, first + j, pl.ds(3 * part, 3 * part), :] = low

    for relative in range(2):
        which = segment if relative == 0 else 1 - segment
        left = jnp.concatenate([field[relative, row] for row in range(height)], axis=1)
        for a in range(3):
            for b in range(3):
                right = values_ref[which, pl.ds(b, height), pl.ds(a, frames)]
                product = dot(left, right.reshape(height * cells, 2 * channels))
                full = 3 * part
                total = product[:full, :channels] + product[:full, channels:] + product[full:, :channels]
                for e in range(3):
                    tap = (a * 3 + b) * 3 + e
                    for side, ref in enumerate((keep_ref, send_ref)):
                        for step in range(pairs):
                            start = e * part + side * share + step * width
                            ref[relative, step, tap] = total[start : start + width]


def assembled_kernel(dims, at_ref, kept_ref, came_ref, out_ref):
    tm, pairs, channels = dims
    segment, z, p = at_ref[0], at_ref[1], at_ref[2]
    core = lax.rem(p, 2)
    y = lax.div(p, 2)
    taps = kept_ref.shape[2]
    for tap in range(taps):
        parts = []
        for target in range(tm):
            k = lax.rem(z - target + tm, tm)
            for side in range(2):
                for its_y in range(pairs):
                    step = lax.rem(y - its_y + pairs, pairs)
                    kept = kept_ref[step, k, tap]
                    came = came_ref[step, k, tap]
                    parts.append(jnp.where(core == side, kept, came))
        out_ref[pl.ds(tap * channels, channels), :] = jnp.concatenate(parts, axis=0).T


def vmem(shape, dtype):
    return pltpu.VMEM(shape, dtype)


def call(kernel, shapes, scratch, count, flops):
    single = not isinstance(shapes, list)
    space = pl.BlockSpec(memory_space=pltpu.VMEM)
    return pl.pallas_call(
        kernel,
        out_shape=shapes,
        in_specs=[pl.BlockSpec(memory_space=pltpu.SMEM)] + [space] * count,
        out_specs=space if single else [space] * len(shapes),
        scratch_shapes=scratch,
        compiler_params=pltpu.CompilerParams(vmem_limit_bytes=VMEM_LIMIT),
        cost_estimate=pl.CostEstimate(flops=flops, bytes_accessed=8_000_000, transcendentals=0),
    )


def make_local(sizes):
    segments, tm, space = sizes["segment"], sizes["tm"], sizes["space"]
    pairs = space // 2

    def send(x, move):
        route = []
        for s in range(segments):
            for t in range(tm):
                for p in range(space):
                    target = move(s, t, p)
                    if target is not None:
                        s2, t2, p2 = target
                        route.append(((s * tm + t) * space + p, (s2 * tm + t2) * space + p2))
        return lax.ppermute(x, AXES, route)

    def later(k):
        return lambda s, t, p: (s, (t + k) % tm, p)

    def across(flip, step):
        return lambda s, t, p: (s ^ flip, t, ((p // 2 + step) % pairs) * 2 + p % 2)

    def swap_section(s, t, p):
        return (1 - s, t, p)

    def swap_core(s, t, p):
        return (s, t, p ^ 1)

    def row_down(s, t, p):
        return (s, t, p + 1) if p + 1 < space else None

    def row_up(s, t, p):
        return (s, t, p - 1) if p > 0 else None

    def local(video_clips, conv_weights):
        clips, own_frames, height, columns, channels = video_clips.shape
        frames = tm * own_frames
        rows_all = height * space
        per = height // tm
        cells = frames * columns
        factor = float(clips * frames * rows_all * columns) ** (-0.5)
        segment = lax.axis_index("segment")
        z = lax.axis_index("tm")
        p = lax.axis_index("space")
        at = jnp.stack([segment, z, p]).astype(jnp.int32)
        own = conv_weights[0]
        taps = own.shape[0] // channels
        half = own.shape[0] // 2

        mine = send(lax.dynamic_slice_in_dim(own, (p % 2) * half, half, 0), swap_section)
        clip = lax.dynamic_index_in_dim(video_clips, segment, 0, keepdims=False)
        block = jnp.stack([clip] + [send(clip, later(k)) for k in range(1, tm)])
        up = send(block[:, :, height - 3 :], row_down)
        down = send(block[:, :, :3], row_up)
        other = send(mine, swap_core)

        part = channels // tm
        full = 3 * channels
        sent, values = call(
            functools.partial(
                activations_kernel, (tm, own_frames, height, rows_all, columns, channels, factor)
            ),
            [
                jax.ShapeDtypeStruct((tm, 2, part, per * cells), f32),
                jax.ShapeDtypeStruct((2, height + 2, frames + 2, columns, 2 * channels), bf16),
            ],
            [vmem((height + 6, frames + 2, columns, full), bf16)] * 2
            + [vmem((height + 4, frames + 2, columns, full), bf16)] * 2
            + [vmem((per + 2, frames + 2, columns, full), bf16)] * 2
            + [
                vmem((2, own.shape[0], 2 * channels), bf16),
                vmem((own.shape[0], 2 * channels), bf16),
                vmem((height + 2, frames, columns, channels), f32),
                vmem((height + 4, frames, columns, channels), f32),
                vmem((2, channels, per * cells), f32),
            ],
            6,
            6 * own.shape[0] * channels * cells * (height + 4 + 2 * per + 2),
        )(at, block, up, down, own, mine, other)

        pieces = [sent[0]] + [send(sent[k], later(k)) for k in range(1, tm)]
        width = part // (2 * pairs)
        shape = jax.ShapeDtypeStruct((2, pairs, taps, width, channels), f32)
        keep, give = call(
            functools.partial(
                weights_kernel, (tm, own_frames, height, rows_all, columns, channels, pairs)
            ),
            [shape, shape],
            [vmem((2, height, 6 * part, cells), bf16)],
            tm + 1,
            16 * taps * part * height * cells * channels,
        )(at, *pieces, values)

        both = keep + send(give, swap_core)
        total = both[0, 0]
        for flip in range(2):
            for step in range(pairs):
                if flip or step:
                    total = total + send(both[flip, step], across(flip, step))

        gathered = jnp.stack([total] + [send(total, later(k)) for k in range(1, tm)])
        gathered = jnp.stack([gathered] + [send(gathered, across(0, k)) for k in range(1, pairs)])
        came = send(gathered, swap_core)
        out = call(
            functools.partial(assembled_kernel, (tm, pairs, channels)),
            jax.ShapeDtypeStruct(own.shape, f32),
            [],
            2,
            0,
        )(at, gathered, came)
        return out[None]

    return local


def solution(mesh):
    return jax.shard_map(
        make_local(dict(mesh.shape)),
        mesh=mesh,
        in_specs=(P(None, "tm", "space", None, None), P("segment", None, None)),
        out_specs=P("segment", None, None),
        check_vma=False,
    )
```

time: 239 us -> 113 us (0.47)
  waiting for transfers between devices: 135 us -> 47.3 us
  matrix products: 28.3 us -> 0 us
  Pallas kernels: 0 us -> 26.4 us
  between operations: 14.2 us -> 0.13 us
  local copies, waits for them, and re-layouts: 14.9 us -> 5.44 us
  starting transfers between devices: 40.5 us -> 31.9 us
  other arithmetic: 6.02 us -> 1.88 us
    psum x1 -> x0, waiting for transfers between devices: 97.8 us -> none  [summed_grads(): return lax.psum(stacked, ('tm', 'space'))]
    dot_general x15 -> x0, matrix products: 28.3 us -> none  [the longest x12 16.4 us: apply_conv(): jnp.dot(patches, weight_block, precision=highest, preferred_element_type=...]
    pallas_call x0 -> x3, Pallas kernels: none -> 26.4 us  [the longest x1 18.4 us: local(): call(functools.partial(activations_kernel, (tm, own_frames, height, rows_...]
    ppermute x15 -> x19, waiting for transfers between devices: 36.9 us -> 47.3 us  [send(): return lax.ppermute(x, AXES, route)]
    ppermute x15 -> x19, starting transfers between devices: 40.5 us -> 31.9 us  [send(): return lax.ppermute(x, AXES, route)]
    unnamed x61 -> x18, local copies, waits for them, and re-layouts: 8.13 us -> 2.48 us
    transpose x3 -> x0, local copies, waits for them, and re-layouts: 5.3 us -> none  [apply_conv(): weight_block = weight_block.reshape(9, channels, channels).transpose(0, 2...]
    concatenate x8 -> x0, other arithmetic: 2.45 us -> none  [with_halo(): block = jnp.concatenate([low, block, high], axis=dim)]
  transfers between devices with their start and end apart: 16 -> 19, of which waited for: 11 -> 13; matrix products, arithmetic and copies ran while one was open for 3% -> 1% of each run, Pallas kernels for 0% -> 0%
where the time goes in v1:
time: 113 us
  waiting for transfers between devices  47.3 us (42%)
  starting transfers between devices  31.9 us (28%)
  Pallas kernels  26.4 us (23%)
  local copies, waits for them, and re-layouts  5.44 us (5%)
  other arithmetic  1.88 us (2%)
    ppermute x19, waiting for transfers between devices, send(): return lax.ppermute(x, AXES, route)  47.3 us
    ppermute x19, starting transfers between devices, send(): return lax.ppermute(x, AXES, route)  31.9 us
    pallas_call x1, Pallas kernels, local(): call(functools.partial(activations_kernel, (tm, own_frames, height, rows_...  18.4 us
    pallas_call x1, Pallas kernels, local(): call(functools.partial(weights_kernel, (tm, own_frames, height, rows_all,...  4.75 us
    pallas_call x1, Pallas kernels, local(): call(functools.partial(assembled_kernel, (tm, pairs, channels)), jax.Shap...  3.2 us
    unnamed x18, local copies, waits for them, and re-layouts  2.48 us
  transfers between devices with their start and end apart: 19, of which 13 were waited for; matrix products, arithmetic and copies ran while one was open for 1% of the time, Pallas kernels for 0%

profile of v1, /device:TPU:0, one launch (start us, length us, event | category | flops | bytes accessed | tf_op | source)
XLA Modules:
  0.0 113.0 jit_solution(5087491627354569033)
XLA Ops:
  0.0 1.3 %dynamic-slice_bitcast_fusion = f32[1728,128]{1,0:T(8,128)S(1)} fusion(f32[1,3456,128]{2,1,0:T(8,128)} %param.3, s32[]{:T(128)S(6)} %select_n.16), kind=kLoop, calls=%fused_computation.1 | loop fusion | bytes 1769476 | tf_op jit(solution)/shard_map/dynamic_slice | solution.py:311
  1.3 3.0 %collective-permute-start.5 = (f32[1728,128]{1,0:T(8,128)S(1)}, f32[1728,128]{1,0:T(8,128)S(1)}, u32[]{:S(2)}, u32[]{:S(2)}) collective-permute-start(f32[1728,128]{1,0:T(8,128)S(1)} %dynamic-slice_bitcast_fusion), channel_id=1, source_target_pairs={{0,16},{1,17},{2,18},{3,19},{4,20},{5,21},{6,22},{7,23},{8,24},{9,... | collective-permute-start | bytes 2654216 | tf_op jit(solution)/shard_map/ppermute | solution.py:276
  4.3 3.7 %collective-permute-start.2 = (f32[2,4,32,128]{3,2,1,0:T(8,128)S(1)}, f32[2,4,32,128]{3,2,1,0:T(8,128)S(1)}, u32[]{:S(2)}, u32[]{:S(2)}) collective-permute-start(f32[2,4,32,128]{3,2,1,0:T(8,128)S(1)} %fusion.5), channel_id=1, source_target_pairs={{0,12},{1,13},{2,14},{3,15},{4,0},{5,1},{6,2},{7,3},{8,4},{9,5},{1... | collective-permute-start | bytes 393224 | tf_op jit(solution)/shard_map/ppermute | solution.py:276
  9.0 15.0 %collective-permute-done.5.mine_ref = f32[1728,128]{1,0:T(8,128)S(1)} collective-permute-done((f32[1728,128]{1,0:T(8,128)S(1)}, f32[1728,128]{1,0:T(8,128)S(1)}, u32[]{:S(2)}, u32[]{:S(2)}) %collective-permute-start.5) | collective-permute-done | bytes 884768 | tf_op jit(solution)/shard_map/ppermute | solution.py:276
  24.1 1.3 %collective-permute-start.4 = (f32[4,2,3,32,128]{4,3,2,1,0:T(8,128)S(1)}, f32[4,2,3,32,128]{4,3,2,1,0:T(8,128)}, u32[]{:S(2)}, u32[]{:S(2)}) collective-permute-start(f32[4,2,3,32,128]{4,3,2,1,0:T(8,128)S(1)} %get-tuple-element.13), channel_id=1, source_target_pairs={{1,0},{2,1},{3,2},{5,4},{6,5},{7,6},{9,8},{10,9},{11,10},{13,12},{... | collective-permute-start | bytes 1179656 | tf_op jit(solution)/shard_map/ppermute | solution.py:276
  25.4 3.8 %collective-permute-start.3 = (f32[4,2,3,32,128]{4,3,2,1,0:T(8,128)S(1)}, f32[4,2,3,32,128]{4,3,2,1,0:T(8,128)}, u32[]{:S(2)}, u32[]{:S(2)}) collective-permute-start(f32[4,2,3,32,128]{4,3,2,1,0:T(8,128)S(1)} %get-tuple-element.14), channel_id=1, source_target_pairs={{0,1},{1,2},{2,3},{4,5},{5,6},{6,7},{8,9},{9,10},{10,11},{12,13},{... | collective-permute-start | bytes 1179656 | tf_op jit(solution)/shard_map/ppermute | solution.py:276
  30.9 18.4 %shard_map.28 = (f32[4,2,32,256]{3,2,1,0:T(8,128)}, bf16[2,6,10,32,256]{4,3,2,1,0:T(8,128)(2,1)}) custom-call(s32[3]{0:T(128)} %pad_add_fusion.at_ref, f32[4,2,4,32,128]{4,3,2,1,0:T(8,128)} %copy-done.2, f32[4,2,3,32,128]{4,3,2,1,0:T(8,128)} %collective-permute-done.3.up_ref, f32[4,2,3,32,128]{4,3,2,1,0:T(8,128)} %collective-permute-done.4.down_ref, ...), custom_call_target="tpu_custom_call" | custom-call | flops 8153726976 | bytes 8000000 | tf_op jit(solution)/shard_map/pallas_call | solution.py:320
  49.3 1.6 %slice_bitcast_fusion.4 = (f32[2,32,256]{2,1,0:T(8,128)S(1)}, f32[2,32,256]{2,1,0:T(8,128)S(1)}, f32[2,32,256]{2,1,0:T(8,128)S(1)}, f32[2,32,256]{2,1,0:T(8,128)}) fusion(f32[4,2,32,256]{3,2,1,0:T(8,128)} %get-tuple-element.9), kind=kLoop, calls=%fused_computation.11 | loop fusion | bytes 524288 | tf_op jit(solution)/shard_map/squeeze | solution.py:342
  50.8 3.9 %collective-permute-start.9 = (f32[2,32,256]{2,1,0:T(8,128)S(1)}, f32[2,32,256]{2,1,0:T(8,128)S(1)}, u32[]{:S(2)}, u32[]{:S(2)}) collective-permute-start(f32[2,32,256]{2,1,0:T(8,128)S(1)} %get-tuple-element.20), channel_id=1, source_target_pairs={{0,12},{1,13},{2,14},{3,15},{4,0},{5,1},{6,2},{7,3},{8,4},{9,5},{1... | collective-permute-start | bytes 196616 | tf_op jit(solution)/shard_map/ppermute | solution.py:276
  56.6 3.5 %collective-permute-done.8.refs_2_ = f32[2,32,256]{2,1,0:T(8,128)S(1)} collective-permute-done((f32[2,32,256]{2,1,0:T(8,128)S(1)}, f32[2,32,256]{2,1,0:T(8,128)S(1)}, u32[]{:S(2)}, u32[]{:S(2)}) %collective-permute-start.8) | collective-permute-done | bytes 65568 | tf_op jit(solution)/shard_map/ppermute | solution.py:276
  61.5 4.8 %shard_map.29 = (f32[2,2,27,8,128]{4,3,2,1,0:T(8,128)}, f32[2,2,27,8,128]{4,3,2,1,0:T(8,128)}) custom-call(s32[3]{0:T(128)} %pad_add_fusion.at_ref, f32[2,32,256]{2,1,0:T(8,128)} %get-tuple-element.23.refs_0_, f32[2,32,256]{2,1,0:T(8,128)} %copy-done.8, f32[2,32,256]{2,1,0:T(8,128)} %copy-done.7, f32[2,32,256]{2,1,0:T(8,128)} %copy-done.6, ...), custom_call_target="tpu_custom_call" | custom-call | flops 1811939328 | bytes 8000000 | tf_op jit(solution)/shard_map/pallas_call | solution.py:345
  66.3 3.4 %collective-permute-start.10 = (f32[2,2,27,8,128]{4,3,2,1,0:T(8,128)}, f32[2,2,27,8,128]{4,3,2,1,0:T(8,128)S(1)}, u32[]{:S(2)}, u32[]{:S(2)}) collective-permute-start(f32[2,2,27,8,128]{4,3,2,1,0:T(8,128)} %get-tuple-element.12), channel_id=1, source_target_pairs={{0,1},{1,0},{2,3},{3,2},{4,5},{5,4},{6,7},{7,6},{8,9},{9,8},{10,11... | collective-permute-start | bytes 1327112 | tf_op jit(solution)/shard_map/ppermute | solution.py:276
  69.7 1.6 %collective-permute-done.10 = f32[2,2,27,8,128]{4,3,2,1,0:T(8,128)S(1)} collective-permute-done((f32[2,2,27,8,128]{4,3,2,1,0:T(8,128)}, f32[2,2,27,8,128]{4,3,2,1,0:T(8,128)S(1)}, u32[]{:S(2)}, u32[]{:S(2)}) %collective-permute-start.10) | collective-permute-done | bytes 442400 | tf_op jit(solution)/shard_map/ppermute | solution.py:276
  71.3 1.1 add.26
  72.4 4.3 %collective-permute-start.11 = (f32[27,8,128]{2,1,0:T(8,128)S(1)}, f32[27,8,128]{2,1,0:T(8,128)S(1)}, u32[]{:S(2)}, u32[]{:S(2)}) collective-permute-start(f32[27,8,128]{2,1,0:T(8,128)S(1)} %get-tuple-element.17), channel_id=1, source_target_pairs={{0,2},{1,3},{2,0},{3,1},{4,6},{5,7},{6,4},{7,5},{8,10},{9,11},{10,... | collective-permute-start | bytes 331784 | tf_op jit(solution)/shard_map/ppermute | solution.py:276
  78.3 3.5 %collective-permute-done.11 = f32[27,8,128]{2,1,0:T(8,128)S(1)} collective-permute-done((f32[27,8,128]{2,1,0:T(8,128)S(1)}, f32[27,8,128]{2,1,0:T(8,128)S(1)}, u32[]{:S(2)}, u32[]{:S(2)}) %collective-permute-start.11) | collective-permute-done | bytes 110624 | tf_op jit(solution)/shard_map/ppermute | solution.py:276
  81.8 1.8 %collective-permute-done.13 = f32[27,8,128]{2,1,0:T(8,128)S(1)} collective-permute-done((f32[27,8,128]{2,1,0:T(8,128)S(1)}, f32[27,8,128]{2,1,0:T(8,128)S(1)}, u32[]{:S(2)}, u32[]{:S(2)}) %collective-permute-start.13) | collective-permute-done | bytes 110624 | tf_op jit(solution)/shard_map/ppermute | solution.py:276
  85.1 1.9 %collective-permute-start.14 = (f32[27,8,128]{2,1,0:T(8,128)S(1)}, f32[27,8,128]{2,1,0:T(8,128)S(1)}, u32[]{:S(2)}, u32[]{:S(2)}) collective-permute-start(f32[27,8,128]{2,1,0:T(8,128)S(1)} %fusion.2), channel_id=1, source_target_pairs={{0,4},{1,5},{2,6},{3,7},{4,8},{5,9},{6,10},{7,11},{8,12},{9,13},{1... | collective-permute-start | bytes 331784 | tf_op jit(solution)/shard_map/ppermute | solution.py:276
  87.0 2.4 %collective-permute-done.16 = f32[27,8,128]{2,1,0:T(8,128)S(1)} collective-permute-done((f32[27,8,128]{2,1,0:T(8,128)S(1)}, f32[27,8,128]{2,1,0:T(8,128)S(1)}, u32[]{:S(2)}, u32[]{:S(2)}) %collective-permute-start.16) | collective-permute-done | bytes 110624 | tf_op jit(solution)/shard_map/ppermute | solution.py:276
  89.4 5.4 %collective-permute-done.15 = f32[27,8,128]{2,1,0:T(8,128)S(1)} collective-permute-done((f32[27,8,128]{2,1,0:T(8,128)S(1)}, f32[27,8,128]{2,1,0:T(8,128)S(1)}, u32[]{:S(2)}, u32[]{:S(2)}) %collective-permute-start.15) | collective-permute-done | bytes 110624 | tf_op jit(solution)/shard_map/ppermute | solution.py:276
  94.9 1.7 %collective-permute-start.17 = (f32[4,27,8,128]{3,2,1,0:T(8,128)S(1)}, f32[4,27,8,128]{3,2,1,0:T(8,128)S(1)}, u32[]{:S(2)}, u32[]{:S(2)}) collective-permute-start(f32[4,27,8,128]{3,2,1,0:T(8,128)S(1)} %get-tuple-element.16), channel_id=1, source_target_pairs={{0,2},{1,3},{2,0},{3,1},{4,6},{5,7},{6,4},{7,5},{8,10},{9,11},{10,... | collective-permute-start | bytes 1327112 | tf_op jit(solution)/shard_map/ppermute | solution.py:276
  96.6 9.7 %collective-permute-done.17 = f32[4,27,8,128]{3,2,1,0:T(8,128)S(1)} collective-permute-done((f32[4,27,8,128]{3,2,1,0:T(8,128)S(1)}, f32[4,27,8,128]{3,2,1,0:T(8,128)S(1)}, u32[]{:S(2)}, u32[]{:S(2)}) %collective-permute-start.17) | collective-permute-done | bytes 442400 | tf_op jit(solution)/shard_map/ppermute | solution.py:276
  106.5 2.4 %collective-permute-done.18.came_ref = f32[2,4,27,8,128]{4,3,2,1,0:T(8,128)S(1)} collective-permute-done((f32[2,4,27,8,128]{4,3,2,1,0:T(8,128)S(1)}, f32[2,4,27,8,128]{4,3,2,1,0:T(8,128)S(1)}, u32[]{:S(2)}, u32[]{:S(2)}) %collective-permute-start.18) | collective-permute-done | bytes 884768 | tf_op jit(solution)/shard_map/ppermute | solution.py:276
  109.8 3.2 %shard_map.30 = f32[3456,128]{1,0:T(8,128)} custom-call(s32[3]{0:T(128)} %pad_add_fusion.at_ref, f32[2,4,27,8,128]{4,3,2,1,0:T(8,128)} %copy-done.1, f32[2,4,27,8,128]{4,3,2,1,0:T(8,128)} %copy-done.3), custom_call_target="tpu_custom_call" | custom-call | bytes 8000000 | tf_op jit(solution)/shard_map/pallas_call | solution.py:365
  (47 shorter events, 10.3 us)
Async XLA Ops:
  0.0 4.3 %copy-start = (f32[2,2,4,32,128]{4,3,2,1,0:T(8,128)S(1)}, f32[2,2,4,32,128]{4,3,2,1,0:T(8,128)}, u32[]{:S(2)}) copy-start(f32[2,2,4,32,128]{4,3,2,1,0:T(8,128)} %param.2) | copy-start | bytes 786436
  1.3 22.7 %collective-permute-start.5 = (f32[1728,128]{1,0:T(8,128)S(1)}, f32[1728,128]{1,0:T(8,128)S(1)}, u32[]{:S(2)}, u32[]{:S(2)}) collective-permute-start(f32[1728,128]{1,0:T(8,128)S(1)} %dynamic-slice_bitcast_fusion), channel_id=1, source_target_pairs={{0,16},{1,17},{2,18},{3,19},{4,20},{5,21},{6,22},{7,23},{8,24},{9,... | collective-permute-start | bytes 2654216 | tf_op jit(solution)/shard_map/ppermute | solution.py:276
  4.3 19.7 %collective-permute-start.2 = (f32[2,4,32,128]{3,2,1,0:T(8,128)S(1)}, f32[2,4,32,128]{3,2,1,0:T(8,128)S(1)}, u32[]{:S(2)}, u32[]{:S(2)}) collective-permute-start(f32[2,4,32,128]{3,2,1,0:T(8,128)S(1)} %fusion.5), channel_id=1, source_target_pairs={{0,12},{1,13},{2,14},{3,15},{4,0},{5,1},{6,2},{7,3},{8,4},{9,5},{1... | collective-permute-start | bytes 393224 | tf_op jit(solution)/shard_map/ppermute | solution.py:276
  7.9 16.0 %collective-permute-start.1 = (f32[2,4,32,128]{3,2,1,0:T(8,128)S(1)}, f32[2,4,32,128]{3,2,1,0:T(8,128)S(1)}, u32[]{:S(2)}, u32[]{:S(2)}) collective-permute-start(f32[2,4,32,128]{3,2,1,0:T(8,128)S(1)} %fusion.5), channel_id=1, source_target_pairs={{0,8},{1,9},{2,10},{3,11},{4,12},{5,13},{6,14},{7,15},{8,0},{9,1},... | collective-permute-start | bytes 393224 | tf_op jit(solution)/shard_map/ppermute | solution.py:276
  8.0 16.0 %collective-permute-start = (f32[2,4,32,128]{3,2,1,0:T(8,128)S(1)}, f32[2,4,32,128]{3,2,1,0:T(8,128)S(1)}, u32[]{:S(2)}, u32[]{:S(2)}) collective-permute-start(f32[2,4,32,128]{3,2,1,0:T(8,128)S(1)} %fusion.5), channel_id=1, source_target_pairs={{0,4},{1,5},{2,6},{3,7},{4,8},{5,9},{6,10},{7,11},{8,12},{9,13},{1... | collective-permute-start | bytes 393224 | tf_op jit(solution)/shard_map/ppermute | solution.py:276
  23.9 6.0 %copy-start.4 = (f32[1728,128]{1,0:T(8,128)}, f32[1728,128]{1,0:T(8,128)S(1)}, u32[]{:S(2)}) copy-start(f32[1728,128]{1,0:T(8,128)S(1)} %collective-permute-done.5.mine_ref) | copy-start | bytes 2654212
  23.9 6.0 %collective-permute-start.6 = (f32[1728,128]{1,0:T(8,128)S(1)}, f32[1728,128]{1,0:T(8,128)S(1)}, u32[]{:S(2)}, u32[]{:S(2)}) collective-permute-start(f32[1728,128]{1,0:T(8,128)S(1)} %collective-permute-done.5.mine_ref), channel_id=1, source_target_pairs={{0,1},{1,0},{2,3},{3,2},{4,5},{5,4},{6,7},{7,6},{8,9},{9,8},{10,11... | collective-permute-start | bytes 2654216 | tf_op jit(solution)/shard_map/ppermute | solution.py:276
  24.0 5.9 %copy-start.2 = (f32[4,2,4,32,128]{4,3,2,1,0:T(8,128)}, f32[4,2,4,32,128]{4,3,2,1,0:T(8,128)S(1)}, u32[]{:S(2)}) copy-start(f32[4,2,4,32,128]{4,3,2,1,0:T(8,128)S(1)} %pad_maximum_fusion.1.block_ref) | copy-start | bytes 1572868
  24.1 5.7 %collective-permute-start.4 = (f32[4,2,3,32,128]{4,3,2,1,0:T(8,128)S(1)}, f32[4,2,3,32,128]{4,3,2,1,0:T(8,128)}, u32[]{:S(2)}, u32[]{:S(2)}) collective-permute-start(f32[4,2,3,32,128]{4,3,2,1,0:T(8,128)S(1)} %get-tuple-element.13), channel_id=1, source_target_pairs={{1,0},{2,1},{3,2},{5,4},{6,5},{7,6},{9,8},{10,9},{11,10},{13,12},{... | collective-permute-start | bytes 1179656 | tf_op jit(solution)/shard_map/ppermute | solution.py:276
  25.4 4.5 %collective-permute-start.3 = (f32[4,2,3,32,128]{4,3,2,1,0:T(8,128)S(1)}, f32[4,2,3,32,128]{4,3,2,1,0:T(8,128)}, u32[]{:S(2)}, u32[]{:S(2)}) collective-permute-start(f32[4,2,3,32,128]{4,3,2,1,0:T(8,128)S(1)} %get-tuple-element.14), channel_id=1, source_target_pairs={{0,1},{1,2},{2,3},{4,5},{5,6},{6,7},{8,9},{9,10},{10,11},{12,13},{... | collective-permute-start | bytes 1179656 | tf_op jit(solution)/shard_map/ppermute | solution.py:276
  50.8 5.8 %collective-permute-start.9 = (f32[2,32,256]{2,1,0:T(8,128)S(1)}, f32[2,32,256]{2,1,0:T(8,128)S(1)}, u32[]{:S(2)}, u32[]{:S(2)}) collective-permute-start(f32[2,32,256]{2,1,0:T(8,128)S(1)} %get-tuple-element.20), channel_id=1, source_target_pairs={{0,12},{1,13},{2,14},{3,15},{4,0},{5,1},{6,2},{7,3},{8,4},{9,5},{1... | collective-permute-start | bytes 196616 | tf_op jit(solution)/shard_map/ppermute | solution.py:276
  54.7 5.4 %collective-permute-start.8 = (f32[2,32,256]{2,1,0:T(8,128)S(1)}, f32[2,32,256]{2,1,0:T(8,128)S(1)}, u32[]{:S(2)}, u32[]{:S(2)}) collective-permute-start(f32[2,32,256]{2,1,0:T(8,128)S(1)} %get-tuple-element.21), channel_id=1, source_target_pairs={{0,8},{1,9},{2,10},{3,11},{4,12},{5,13},{6,14},{7,15},{8,0},{9,1},... | collective-permute-start | bytes 196616 | tf_op jit(solution)/shard_map/ppermute | solution.py:276
  54.7 6.2 %collective-permute-start.7 = (f32[2,32,256]{2,1,0:T(8,128)S(1)}, f32[2,32,256]{2,1,0:T(8,128)S(1)}, u32[]{:S(2)}, u32[]{:S(2)}) collective-permute-start(f32[2,32,256]{2,1,0:T(8,128)S(1)} %get-tuple-element.22), channel_id=1, source_target_pairs={{0,4},{1,5},{2,6},{3,7},{4,8},{5,9},{6,10},{7,11},{8,12},{9,13},{1... | collective-permute-start | bytes 196616 | tf_op jit(solution)/shard_map/ppermute | solution.py:276
  56.6 4.3 %copy-start.6 = (f32[2,32,256]{2,1,0:T(8,128)}, f32[2,32,256]{2,1,0:T(8,128)S(1)}, u32[]{:S(2)}) copy-start(f32[2,32,256]{2,1,0:T(8,128)S(1)} %collective-permute-done.9.refs_3_) | copy-start | bytes 196612
  66.3 5.0 %collective-permute-start.10 = (f32[2,2,27,8,128]{4,3,2,1,0:T(8,128)}, f32[2,2,27,8,128]{4,3,2,1,0:T(8,128)S(1)}, u32[]{:S(2)}, u32[]{:S(2)}) collective-permute-start(f32[2,2,27,8,128]{4,3,2,1,0:T(8,128)} %get-tuple-element.12), channel_id=1, source_target_pairs={{0,1},{1,0},{2,3},{3,2},{4,5},{5,4},{6,7},{7,6},{8,9},{9,8},{10,11... | collective-permute-start | bytes 1327112 | tf_op jit(solution)/shard_map/ppermute | solution.py:276
  72.4 9.4 %collective-permute-start.11 = (f32[27,8,128]{2,1,0:T(8,128)S(1)}, f32[27,8,128]{2,1,0:T(8,128)S(1)}, u32[]{:S(2)}, u32[]{:S(2)}) collective-permute-start(f32[27,8,128]{2,1,0:T(8,128)S(1)} %get-tuple-element.17), channel_id=1, source_target_pairs={{0,2},{1,3},{2,0},{3,1},{4,6},{5,7},{6,4},{7,5},{8,10},{9,11},{10,... | collective-permute-start | bytes 331784 | tf_op jit(solution)/shard_map/ppermute | solution.py:276
  76.8 6.8 %collective-permute-start.13 = (f32[27,8,128]{2,1,0:T(8,128)S(1)}, f32[27,8,128]{2,1,0:T(8,128)S(1)}, u32[]{:S(2)}, u32[]{:S(2)}) collective-permute-start(f32[27,8,128]{2,1,0:T(8,128)S(1)} %get-tuple-element.18), channel_id=1, source_target_pairs={{0,18},{1,19},{2,16},{3,17},{4,22},{5,23},{6,20},{7,21},{8,26},{9,... | collective-permute-start | bytes 331784 | tf_op jit(solution)/shard_map/ppermute | solution.py:276
  77.8 6.0 %collective-permute-start.12 = (f32[27,8,128]{2,1,0:T(8,128)S(1)}, f32[27,8,128]{2,1,0:T(8,128)S(1)}, u32[]{:S(2)}, u32[]{:S(2)}) collective-permute-start(f32[27,8,128]{2,1,0:T(8,128)S(1)} %get-tuple-element.19), channel_id=1, source_target_pairs={{0,16},{1,17},{2,18},{3,19},{4,20},{5,21},{6,22},{7,23},{8,24},{9,... | collective-permute-start | bytes 331784 | tf_op jit(solution)/shard_map/ppermute | solution.py:276
  83.8 5.6 %collective-permute-start.16 = (f32[27,8,128]{2,1,0:T(8,128)S(1)}, f32[27,8,128]{2,1,0:T(8,128)S(1)}, u32[]{:S(2)}, u32[]{:S(2)}) collective-permute-start(f32[27,8,128]{2,1,0:T(8,128)S(1)} %fusion.2), channel_id=1, source_target_pairs={{0,12},{1,13},{2,14},{3,15},{4,0},{5,1},{6,2},{7,3},{8,4},{9,5},{1... | collective-permute-start | bytes 331784 | tf_op jit(solution)/shard_map/ppermute | solution.py:276
  84.9 10.0 %collective-permute-start.15 = (f32[27,8,128]{2,1,0:T(8,128)S(1)}, f32[27,8,128]{2,1,0:T(8,128)S(1)}, u32[]{:S(2)}, u32[]{:S(2)}) collective-permute-start(f32[27,8,128]{2,1,0:T(8,128)S(1)} %fusion.2), channel_id=1, source_target_pairs={{0,8},{1,9},{2,10},{3,11},{4,12},{5,13},{6,14},{7,15},{8,0},{9,1},... | collective-permute-start | bytes 331784 | tf_op jit(solution)/shard_map/ppermute | solution.py:276
  85.1 9.8 %collective-permute-start.14 = (f32[27,8,128]{2,1,0:T(8,128)S(1)}, f32[27,8,128]{2,1,0:T(8,128)S(1)}, u32[]{:S(2)}, u32[]{:S(2)}) collective-permute-start(f32[27,8,128]{2,1,0:T(8,128)S(1)} %fusion.2), channel_id=1, source_target_pairs={{0,4},{1,5},{2,6},{3,7},{4,8},{5,9},{6,10},{7,11},{8,12},{9,13},{1... | collective-permute-start | bytes 331784 | tf_op jit(solution)/shard_map/ppermute | solution.py:276
  94.9 11.4 %collective-permute-start.17 = (f32[4,27,8,128]{3,2,1,0:T(8,128)S(1)}, f32[4,27,8,128]{3,2,1,0:T(8,128)S(1)}, u32[]{:S(2)}, u32[]{:S(2)}) collective-permute-start(f32[4,27,8,128]{3,2,1,0:T(8,128)S(1)} %get-tuple-element.16), channel_id=1, source_target_pairs={{0,2},{1,3},{2,0},{3,1},{4,6},{5,7},{6,4},{7,5},{8,10},{9,11},{10,... | collective-permute-start | bytes 1327112 | tf_op jit(solution)/shard_map/ppermute | solution.py:276
  106.4 2.5 %copy-start.1 = (f32[2,4,27,8,128]{4,3,2,1,0:T(8,128)}, f32[2,4,27,8,128]{4,3,2,1,0:T(8,128)S(1)}, u32[]{:S(2)}) copy-start(f32[2,4,27,8,128]{4,3,2,1,0:T(8,128)S(1)} %pad_maximum_fusion.kept_ref) | copy-start | bytes 2654212
  106.4 2.5 %collective-permute-start.18 = (f32[2,4,27,8,128]{4,3,2,1,0:T(8,128)S(1)}, f32[2,4,27,8,128]{4,3,2,1,0:T(8,128)S(1)}, u32[]{:S(2)}, u32[]{:S(2)}) collective-permute-start(f32[2,4,27,8,128]{4,3,2,1,0:T(8,128)S(1)} %pad_maximum_fusion.kept_ref), channel_id=1, source_target_pairs={{0,1},{1,0},{2,3},{3,2},{4,5},{5,4},{6,7},{7,6},{8,9},{9,8},{10,11... | collective-permute-start | bytes 2654216 | tf_op jit(solution)/shard_map/ppermute | solution.py:276
  (4 other events, 3.2 us)

commit v2 on v1

v2 whole, which is shorter than its diff:
```python
import functools

import jax
import jax.numpy as jnp
from jax import lax
from jax.experimental import pallas as pl
from jax.experimental.pallas import tpu as pltpu
from jax.sharding import PartitionSpec as P

f32 = jnp.float32
bf16 = jnp.bfloat16
AXES = ("segment", "tm", "space")
MIB = 1024 * 1024


def split(x):
    high = x.astype(bf16)
    low = (x - high.astype(f32)).astype(bf16)
    return high, low


def dot(a, b):
    return jnp.dot(a, b, preferred_element_type=f32)


def rotate(x, amount, axis):
    size = x.shape[axis]
    amount = amount % size
    if amount == 0:
        return x
    return jnp.concatenate(
        [lax.slice_in_dim(x, size - amount, size, axis=axis), lax.slice_in_dim(x, 0, size - amount, axis=axis)],
        axis=axis,
    )


def store_split(high_ref, low_ref, index, x):
    high, low = split(x)
    high_ref[index] = high
    low_ref[index] = low


def put_taps(to_ref, tap, x):
    channels = x.shape[-1]
    rows = pl.ds((tap // 3) * channels, channels)
    high, low = split(x)
    to_ref[rows, pl.ds((tap % 3) * channels, channels)] = high
    to_ref[rows, pl.ds((tap % 3 + 3) * channels, channels)] = low


def shifted_sum(y, columns, channels, flip):
    parts = [y[:, i * channels : (i + 1) * channels].reshape(-1, columns, channels) for i in range(3)]
    if flip:
        parts = parts[::-1]
    column = lax.broadcasted_iota(jnp.int32, parts[0].shape, 1)
    first = jnp.where(column == 0, 0.0, rotate(parts[0], 1, 1))
    last = jnp.where(column == columns - 1, 0.0, rotate(parts[2], -1, 1))
    return parts[1] + first + last


def convolved(high_ref, low_ref, places, count, dims, weight_ref, flip=False):
    frames, columns, channels = dims
    high, low = [], []
    for row, a in places:
        at = (pl.ds(row, count), pl.ds(a, frames))
        high.append(high_ref[at].reshape(count * frames * columns, channels))
        low.append(low_ref[at].reshape(count * frames * columns, channels))
    full = 3 * channels
    both = dot(jnp.concatenate(high, axis=1), weight_ref[...])
    rest = dot(jnp.concatenate(low, axis=1), weight_ref[:, pl.ds(0, full)])
    y = both[:, :full] + both[:, full:] + rest
    return shifted_sum(y, columns, channels, flip).reshape(count, frames, columns, channels)


def received_taps(core, refs, tap, channels):
    mine_ref, other_ref, mine_late_ref, other_late_ref = refs
    if tap < 18:
        at = pl.ds((tap % 9) * channels, channels)
        return jnp.where(core == tap // 9, mine_ref[at, :], other_ref[at, :])
    half = mine_late_ref.shape[0]
    start, parts = (tap - 18) * channels, []
    while start < (tap - 17) * channels:
        side = start // half
        stop = min((side + 1) * half, (tap - 17) * channels)
        at = pl.ds(start - side * half, stop - start)
        parts.append(jnp.where(core == side, mine_late_ref[at, :], other_late_ref[at, :]))
        start = stop
    return parts[0] if len(parts) == 1 else jnp.concatenate(parts, axis=0)


def field_rows(high_ref, low_ref, row, shape, weight_ref):
    places = [(row + b, a) for a in range(3) for b in range(3)]
    return convolved(high_ref, low_ref, places, 1, shape, weight_ref)[0]


def store_latent(high_ref, low_ref, row, place, rows_all, value):
    latent = value / (1.0 + jnp.exp(-value))
    inside = jnp.logical_and(place >= 0, place < rows_all)
    frames = value.shape[0]
    store_split(high_ref, low_ref, (row, pl.ds(2, frames)), jnp.where(inside, latent, 0.0))


def missing_row(z, i, height, per):
    below = jnp.maximum(z * per - 1, 0)
    row = jnp.where(i < below, 1 + i, z * per + per + 4 + i - below)
    return jnp.minimum(row, height + 3)


def latents_kernel(dims, xh, xl, encoder, lh, ll):
    tm, own_frames, height, rows_all, columns, channels, factor = dims
    frames = tm * own_frames
    per = height // tm
    z, p = lax.axis_index("tm"), lax.axis_index("space")
    for ref in (lh, ll):
        ref[:, 0:2] = jnp.zeros((ref.shape[0], 2) + ref.shape[2:], bf16)
    for i in range(lh.shape[0]):
        row = missing_row(z, i, height, per)
        value = field_rows(xh, xl, row, (frames, columns, channels), encoder)
        store_latent(lh, ll, i, p * height + row - 2, rows_all, value)


def pick_kernel(video_ref, weights_ref, early_ref, late_ref, clip_ref, sems):
    early, late = early_ref.shape[0], late_ref.shape[0]
    segment, core = lax.axis_index("segment"), lax.rem(lax.axis_index("space"), 2)
    copies = [
        pltpu.make_async_copy(weights_ref.at[0, pl.ds(core * early, early)], early_ref, sems.at[0]),
        pltpu.make_async_copy(weights_ref.at[0, pl.ds(2 * early + core * late, late)], late_ref, sems.at[1]),
        pltpu.make_async_copy(video_ref.at[segment], clip_ref, sems.at[2]),
    ]
    for copy in copies:
        copy.start()
    for copy in copies:
        copy.wait()


def activations_kernel(
    dims, block_ref, inner_ref, outer_ref, own_ref, *refs
):
    tm, own_frames, height, rows_all, columns, channels, factor = dims
    came_refs, sent_refs = refs[:4], refs[4 : 4 + tm]
    xh, xl, lh, ll, encoder, video, decoder, turned, ch, cl, hidden, grads = refs[4 + tm :]
    frames = tm * own_frames
    per = height // tm
    cells = frames * columns
    shape = (frames, columns, channels)
    segment, z, p = (lax.axis_index(name) for name in AXES)
    core = lax.rem(p, 2)

    for tap in range(27):
        own = own_ref[pl.ds(tap * channels, channels), :]
        came = received_taps(core, came_refs, tap, channels)
        put_taps(encoder, tap, jnp.where(segment == 0, own, came))
        block = jnp.where(segment == 0, came, own)
        put_taps(decoder, tap, block)
        put_taps(turned, tap, block.T)
    for ref in (xh, xl, lh, ll):
        ref[:, 0:2] = jnp.zeros((ref.shape[0], 2) + ref.shape[2:], bf16)
    for ref in (ch, cl):
        ref[:, frames:] = jnp.zeros((ref.shape[0], 2) + ref.shape[2:], bf16)

    for k in range(tm):
        first = k * own_frames
        for row in range(-3, height + 3):
            if row < 0:
                x = jnp.where(core == 0, outer_ref[k, :, 3 + row], inner_ref[k, :, 3 + row])
            elif row < height:
                x = block_ref[k, :, row]
            else:
                x = jnp.where(core == 0, inner_ref[k, :, row - height], outer_ref[k, :, row - height])
            store_split(xh, xl, (row + 3, pl.ds(first + 2, own_frames)), x)
            if -1 <= row <= height:
                video[row + 1, pl.ds(first, own_frames)] = x

    start = z * per
    for row in range(per + 4):
        value = field_rows(xh, xl, start + row, shape, encoder)
        if 2 <= row < per + 2:
            hidden[row - 2] = value
        store_latent(lh, ll, start + row, p * height + start + row - 2, rows_all, value)

    for j in range(per + 2):
        row = z * per - 1 + j
        decoded = field_rows(lh, ll, row + 1, shape, decoder)
        place = p * height + row
        inside = jnp.logical_and(place >= 0, place < rows_all)
        cotangent = jnp.where(inside, (decoded - video[row + 1]) * factor, 0.0)
        store_split(ch, cl, (j, pl.ds(0, frames)), cotangent)
        if 1 <= j <= per:
            grads[1, :, pl.ds((j - 1) * cells, cells)] = cotangent.reshape(cells, channels).T

    for j in range(per):
        places = [(j + 2 - b, 2 - a) for a in range(3) for b in range(3)]
        grad_latent = convolved(ch, cl, places, 1, shape, turned, flip=True)[0]
        value = hidden[j]
        sigmoid = 1.0 / (1.0 + jnp.exp(-value))
        grad = grad_latent * (sigmoid * (1.0 + value * (1.0 - sigmoid)))
        grads[0, :, pl.ds(j * cells, cells)] = grad.reshape(cells, channels).T

    part = channels // tm
    for k, ref in enumerate(sent_refs):
        target = lax.rem(z + k, tm)
        at = pl.ds(pl.multiple_of(target * part, part), part)
        for which in range(2):
            ref[which] = grads[which, at, :]


def weights_kernel(dims, *refs):
    tm, own_frames, height, rows_all, columns, channels, pairs = dims
    pieces = refs[:tm]
    xh, xl, own_high, own_low, more_high, more_low, keep_ref, send_ref, field, lh, ll = refs[tm:]
    frames = tm * own_frames
    per = height // tm
    cells = frames * columns
    part = channels // tm
    share = part // 2
    width = share // pairs
    full = 3 * part
    segment, z, p = (lax.axis_index(name) for name in AXES)
    core = lax.rem(p, 2)
    y = lax.div(p, 2)

    for own, more, to in ((own_high, more_high, lh), (own_low, more_low, ll)):
        for row in range(per + 4):
            to[z * per + row] = own[z * per + row]
        for i in range(more.shape[0]):
            to[missing_row(z, i, height, per)] = more[i]

    for which in range(2):
        for k in range(tm):
            first = lax.rem(z - k + tm, tm) * per
            ordered = []
            for side in range(2):
                its = core if side == 0 else 1 - core
                for step in range(pairs):
                    its_y = lax.rem(y + step, pairs)
                    start = its * share + its_y * width
                    ordered.append(pieces[k][which, pl.ds(start, width), :])
            x = jnp.concatenate(ordered, axis=0)
            for j in range(per):
                row = x[:, j * cells : (j + 1) * cells]
                column = lax.rem(lax.broadcasted_iota(jnp.int32, row.shape, 1), columns)
                after = jnp.where(column == columns - 1, 0.0, rotate(row, -1, 1))
                before = jnp.where(column == 0, 0.0, rotate(row, 1, 1))
                high, low = split(jnp.concatenate([after, row, before], axis=0))
                field[which, first + j, pl.ds(0, full), :] = high
                field[which, first + j, pl.ds(full, full), :] = low

    for which, (high_ref, low_ref, offset) in enumerate(((xh, xl, 2), (lh, ll, 1))):
        relative = segment if which == 0 else 1 - segment
        left = jnp.concatenate([field[which, row] for row in range(height)], axis=1)
        for a in range(3):
            for b in range(3):
                at = (pl.ds(offset + b, height), pl.ds(a, frames))
                right = jnp.concatenate(
                    [ref[at].reshape(height * cells, channels) for ref in (high_ref, low_ref)], axis=1
                )
                product = dot(left, right)
                total = product[:full, :channels] + product[:full, channels:] + product[full:, :channels]
                for e in range(3):
                    tap = (a * 3 + b) * 3 + e
                    for side, ref in enumerate((keep_ref, send_ref)):
                        for step in range(pairs):
                            start = e * part + side * share + step * width
                            ref[relative, step, tap] = total[start : start + width]


def assembled_kernel(dims, early_ref, late_ref, came_early_ref, came_late_ref, out_ref):
    tm, pairs, channels = dims
    z, p = lax.axis_index("tm"), lax.axis_index("space")
    core = lax.rem(p, 2)
    y = lax.div(p, 2)
    cut = early_ref.shape[2]
    for tap in range(cut + late_ref.shape[2]):
        parts = []
        for target in range(tm):
            k = lax.rem(z - target + tm, tm)
            for side in range(2):
                for its_y in range(pairs):
                    step = lax.rem(y - its_y + pairs, pairs)
                    if tap < cut:
                        kept, came = early_ref[step, k, tap], came_early_ref[step, k, tap]
                    else:
                        kept, came = late_ref[k, step, tap - cut], came_late_ref[k, step, tap - cut]
                    parts.append(jnp.where(core == side, kept, came))
        out_ref[pl.ds(tap * channels, channels), :] = jnp.concatenate(parts, axis=0).T


def vmem(shape, dtype):
    return pltpu.VMEM(shape, dtype)


def call(kernel, shapes, scratch, count, flops, limit, inputs=pltpu.VMEM):
    single = not isinstance(shapes, list)
    space = pl.BlockSpec(memory_space=pltpu.VMEM)
    return pl.pallas_call(
        kernel,
        out_shape=shapes,
        in_specs=[pl.BlockSpec(memory_space=inputs)] * count,
        out_specs=space if single else [space] * len(shapes),
        scratch_shapes=scratch,
        compiler_params=pltpu.CompilerParams(vmem_limit_bytes=limit * MIB),
        cost_estimate=pl.CostEstimate(flops=flops, bytes_accessed=4_000_000, transcendentals=0),
    )


def make_local(sizes):
    segments, tm, space = sizes["segment"], sizes["tm"], sizes["space"]
    pairs = space // 2

    def send(x, move):
        route = []
        for s in range(segments):
            for t in range(tm):
                for p in range(space):
                    target = move(s, t, p)
                    if target is not None:
                        s2, t2, p2 = target
                        route.append(((s * tm + t) * space + p, (s2 * tm + t2) * space + p2))
        return lax.ppermute(x, AXES, route)

    def later(k):
        return lambda s, t, p: (s, (t + k) % tm, p)

    def across(flip, step):
        return lambda s, t, p: (s ^ flip, t, ((p // 2 + step) % pairs) * 2 + p % 2)

    def swap_section(s, t, p):
        return (1 - s, t, p)

    def swap_core(s, t, p):
        return (s, t, p ^ 1)

    def swap_outer(s, t, p):
        target = p - 1 if p % 2 == 0 else p + 1
        return (s, t, target) if 0 <= target < space else None

    def local(video_clips, conv_weights):
        clips, own_frames, height, columns, channels = video_clips.shape
        frames = tm * own_frames
        rows_all = height * space
        per = height // tm
        cells = frames * columns
        factor = float(clips * frames * rows_all * columns) ** (-0.5)
        own = conv_weights[0]
        taps = own.shape[0] // channels
        third = own.shape[0] // 3
        core = lax.axis_index("space") % 2

        early, late, clip = call(
            pick_kernel,
            [
                jax.ShapeDtypeStruct((third, channels), f32),
                jax.ShapeDtypeStruct((third // 2, channels), f32),
                jax.ShapeDtypeStruct(video_clips.shape[1:], f32),
            ],
            [pltpu.SemaphoreType.DMA((3,))],
            2,
            0,
            60,
            pltpu.HBM,
        )(video_clips, conv_weights)
        mine = send(early, swap_section)
        mine_late = send(late, swap_section)
        block = lax.all_gather(clip, "tm")
        bottom, top = block[:, :, height - 3 :], block[:, :, :3]
        to_inner = jnp.where(core == 0, bottom, top)
        to_outer = jnp.where(core == 0, top, bottom)
        inner = send(to_inner, swap_core)
        outer = send(to_outer, swap_outer)
        ready, _, _ = lax.optimization_barrier((mine, to_inner, to_outer))
        other = send(ready, swap_core)
        other_late = send(mine_late, swap_core)

        part = channels // tm
        dims = (tm, own_frames, height, rows_all, columns, channels, factor)
        field = (frames + 2, columns, channels)
        rows = height + 4
        products = 8 * 128 * channels * cells * 9
        shape = jax.ShapeDtypeStruct
        *sent, xh, xl, lh, ll, encoder = call(
            functools.partial(activations_kernel, dims),
            [shape((2, part, per * cells), f32)] * tm
            + [shape((height + 6,) + field, bf16)] * 2
            + [shape((rows,) + field, bf16)] * 2
            + [shape((9 * channels, 6 * channels), bf16)],
            [
                vmem((height + 2, frames, columns, channels), f32),
                vmem((9 * channels, 6 * channels), bf16),
                vmem((9 * channels, 6 * channels), bf16),
                vmem((per + 2,) + field, bf16),
                vmem((per + 2,) + field, bf16),
                vmem((per, frames, columns, channels), f32),
                vmem((2, channels, per * cells), f32),
            ],
            8,
            3 * products * (3 * per + 6),
            32,
        )(block, inner, outer, own, mine, other, mine_late, other_late)

        extra = height - 1 - per
        more_high, more_low = call(
            functools.partial(latents_kernel, dims),
            [shape((extra,) + field, bf16)] * 2,
            [],
            3,
            3 * products * extra,
            12,
        )(xh, xl, encoder)
        pieces = [sent[0]] + [send(sent[k], later(k)) for k in range(1, tm)]
        width = part // (2 * pairs)
        grads = shape((2, pairs, taps, width, channels), f32)
        keep, give = call(
            functools.partial(
                weights_kernel, (tm, own_frames, height, rows_all, columns, channels, pairs)
            ),
            [grads, grads],
            [vmem((2, height, 6 * part, cells), bf16)] + [vmem((rows,) + field, bf16)] * 2,
            tm + 6,
            16 * taps * part * height * cells * channels,
            16,
        )(*pieces, xh, xl, lh, ll, more_high, more_low)

        both = keep + send(give, swap_core)
        total = both[0, 0]
        for flip in range(2):
            for step in range(pairs):
                if flip or step:
                    total = total + send(both[flip, step], across(flip, step))

        cut = taps // 2
        early, late = total[:cut], total[cut:]
        late_rows = [late] + [send(late, across(0, k)) for k in range(1, pairs)]
        early_all = [early] + [send(early, later(k)) for k in range(1, tm)]
        late_rows, early_all = lax.optimization_barrier((late_rows, early_all))
        late_rows, early_all = jnp.stack(late_rows), jnp.stack(early_all)
        early_all = jnp.stack([early_all] + [send(early_all, across(0, k)) for k in range(1, pairs)])
        late_all = jnp.stack([late_rows] + [send(late_rows, later(k)) for k in range(1, tm)])
        came = [send(x, swap_core) for x in (early_all, late_all)]
        out = call(
            functools.partial(assembled_kernel, (tm, pairs, channels)),
            jax.ShapeDtypeStruct(own.shape, f32),
            [],
            4,
            0,
            12,
        )(early_all, late_all, *came)
        return out[None]

    return local


def solution(mesh):
    return jax.shard_map(
        make_local(dict(mesh.shape)),
        mesh=mesh,
        in_specs=(P(None, "tm", "space", None, None), P("segment", None, None)),
        out_specs=P("segment", None, None),
        check_vma=False,
    )
```

time: 113 us -> 86.6 us (0.77)
  waiting for transfers between devices: 47.3 us -> 22.9 us
  blocking collectives: 0 us -> 16.1 us
  Pallas kernels: 26.4 us -> 16.8 us
  local copies, waits for them, and re-layouts: 5.44 us -> 0.04 us
  starting transfers between devices: 31.9 us -> 30.1 us
  other arithmetic: 1.88 us -> 0.3 us
    ppermute x19 -> x23, waiting for transfers between devices: 47.3 us -> 22.9 us  [send(): return lax.ppermute(x, AXES, route)]
    all_gather x0 -> x1, blocking collectives: none -> 16.1 us  [local(): block = lax.all_gather(clip, 'tm')]
    pallas_call x1 -> x3, Pallas kernels: 18.4 us -> 12.8 us  [the longest x1 8.69 us: local(): call(functools.partial(activations_kernel, dims), [shape((2, part, per *...]
    pallas_call x1, Pallas kernels: 4.75 us -> 2.18 us  [local(): call(functools.partial(weights_kernel, (tm, own_frames, height, rows_all,...]
    unnamed x18 -> x2, local copies, waits for them, and re-layouts: 2.48 us -> 0.01 us
    ppermute x19 -> x23, starting transfers between devices: 31.9 us -> 30.1 us  [send(): return lax.ppermute(x, AXES, route)]
    squeeze x2 -> x0, local copies, waits for them, and re-layouts: 1.57 us -> none  [the longest x1 1.57 us: local(): pieces = [sent[0]] + [send(sent[k], later(k)) for k in range(1, tm)]]
    pallas_call x1, Pallas kernels: 3.2 us -> 1.75 us  [local(): call(functools.partial(assembled_kernel, (tm, pairs, channels)), jax.Shap...]
  transfers between devices with their start and end apart: 19 -> 23, of which waited for: 13 -> 14; matrix products, arithmetic and copies ran while one was open for 1% -> 0% of each run, Pallas kernels for 0% -> 2%
where the time goes in v2:
time: 86.6 us; the launch traced here: 86.4 us
  starting transfers between devices  30.1 us (35%)
  waiting for transfers between devices  22.9 us (26%)
  Pallas kernels  16.8 us (19%)
  blocking collectives  16.1 us (19%)
    ppermute x23, starting transfers between devices, send(): return lax.ppermute(x, AXES, route)  30.1 us
    ppermute x23, waiting for transfers between devices, send(): return lax.ppermute(x, AXES, route)  22.9 us
    all_gather x1, blocking collectives, local(): block = lax.all_gather(clip, 'tm')  16.1 us
    pallas_call x1, Pallas kernels, local(): call(functools.partial(activations_kernel, dims), [shape((2, part, per *...  8.69 us
    pallas_call x1, Pallas kernels, local(): call(pick_kernel, [jax.ShapeDtypeStruct((third, channels), f32), jax.Shap...  2.27 us
    pallas_call x1, Pallas kernels, local(): call(functools.partial(weights_kernel, (tm, own_frames, height, rows_all,...  2.18 us
    pallas_call x1, Pallas kernels, local(): call(functools.partial(latents_kernel, dims), [shape((extra,) + field, bf...  1.88 us
    pallas_call x1, Pallas kernels, local(): call(functools.partial(assembled_kernel, (tm, pairs, channels)), jax.Shap...  1.75 us
  transfers between devices with their start and end apart: 23, of which 14 were waited for; matrix products, arithmetic and copies ran while one was open for 0% of the time, Pallas kernels for 2%

profile of v2, /device:TPU:0, one launch (start us, length us, event | category | flops | bytes accessed | tf_op | source)
XLA Modules:
  0.0 86.4 jit_solution(17398714459015053752)
XLA Ops:
  0.0 2.3 %shard_map.28 = (f32[1152,128]{1,0:T(8,128)}, f32[576,128]{1,0:T(8,128)}, f32[2,4,32,128]{3,2,1,0:T(8,128)}) custom-call(f32[2,2,4,32,128]{4,3,2,1,0:T(8,128)} %video_ref.1, f32[1,3456,128]{2,1,0:T(8,128)} %weights_ref.1), custom_call_target="tpu_custom_call" | custom-call | bytes 4000000 | tf_op jit(solution)/shard_map/pallas_call | solution.py:349
  2.3 3.0 %collective-permute-start.2 = (f32[1152,128]{1,0:T(8,128)}, f32[1152,128]{1,0:T(8,128)S(1)}, u32[]{:S(2)}, u32[]{:S(2)}) collective-permute-start(f32[1152,128]{1,0:T(8,128)} %get-tuple-element.29), channel_id=1, source_target_pairs={{0,16},{1,17},{2,18},{3,19},{4,20},{5,21},{6,22},{7,23},{8,24},{9,... | collective-permute-start | bytes 1769480 | tf_op jit(solution)/shard_map/ppermute | solution.py:319
  5.4 16.1 %all-gather = f32[8,4,32,128]{3,2,1,0:T(8,128)S(1)} all-gather(f32[2,4,32,128]{3,2,1,0:T(8,128)} %get-tuple-element.28), channel_id=2, replica_groups=mesh['segment'=2,'tm'=4,'space'=4] {'tm'}, dimensions={0}, use_global_device_ids=true | all-gather | bytes 655360 | tf_op jit(solution)/shard_map/all_gather | solution.py:364
  22.4 2.9 %collective-permute-start = (f32[4,2,3,32,128]{4,3,2,1,0:T(8,128)S(1)}, f32[4,2,3,32,128]{4,3,2,1,0:T(8,128)S(1)}, u32[]{:S(2)}, u32[]{:S(2)}) collective-permute-start(f32[4,2,3,32,128]{4,3,2,1,0:T(8,128)S(1)} %get-tuple-element.52), channel_id=1, source_target_pairs={{0,1},{1,0},{2,3},{3,2},{4,5},{5,4},{6,7},{7,6},{8,9},{9,8},{10,11... | collective-permute-start | bytes 1179656 | tf_op jit(solution)/shard_map/ppermute | solution.py:319
  25.4 1.3 %collective-permute-done.inner_ref = f32[4,2,3,32,128]{4,3,2,1,0:T(8,128)S(1)} collective-permute-done((f32[4,2,3,32,128]{4,3,2,1,0:T(8,128)S(1)}, f32[4,2,3,32,128]{4,3,2,1,0:T(8,128)S(1)}, u32[]{:S(2)}, u32[]{:S(2)}) %collective-permute-start) | collective-permute-done | bytes 393248 | tf_op jit(solution)/shard_map/ppermute | solution.py:319
  27.1 8.7 %shard_map.29 = (f32[2,32,256]{2,1,0:T(8,128)S(1)}, f32[2,32,256]{2,1,0:T(8,128)S(1)}, f32[2,32,256]{2,1,0:T(8,128)S(1)}, f32[2,32,256]{2,1,0:T(8,128)S(1)}, bf1...) custom-call(f32[4,2,4,32,128]{4,3,2,1,0:T(8,128)S(1)} %bitcast.32, ...), custom_call_target="tpu_custom_call" | custom-call | flops 8153726976 | bytes 4000000 | tf_op jit(solution)/shard_map/pallas_call | solution.py:380
  35.8 2.2 %collective-permute-start.6 = (f32[2,32,256]{2,1,0:T(8,128)S(1)}, f32[2,32,256]{2,1,0:T(8,128)S(1)}, u32[]{:S(2)}, u32[]{:S(2)}) collective-permute-start(f32[2,32,256]{2,1,0:T(8,128)S(1)} %get-tuple-element.33), channel_id=1, source_target_pairs={{0,4},{1,5},{2,6},{3,7},{4,8},{5,9},{6,10},{7,11},{8,12},{9,13},{1... | collective-permute-start | bytes 196616 | tf_op jit(solution)/shard_map/ppermute | solution.py:319
  38.0 2.6 %collective-permute-start.7 = (f32[2,32,256]{2,1,0:T(8,128)S(1)}, f32[2,32,256]{2,1,0:T(8,128)S(1)}, u32[]{:S(2)}, u32[]{:S(2)}) collective-permute-start(f32[2,32,256]{2,1,0:T(8,128)S(1)} %get-tuple-element.34), channel_id=1, source_target_pairs={{0,8},{1,9},{2,10},{3,11},{4,12},{5,13},{6,14},{7,15},{8,0},{9,1},... | collective-permute-start | bytes 196616 | tf_op jit(solution)/shard_map/ppermute | solution.py:319
  41.3 1.9 %shard_map.30 = (bf16[2,10,32,128]{3,2,1,0:T(8,128)(2,1)S(1)}, bf16[2,10,32,128]{3,2,1,0:T(8,128)(2,1)S(1)}) custom-call(bf16[10,10,32,128]{3,2,1,0:T(8,128)(2,1)S(1)} %get-tuple-element.36.xh.refs_4_, bf16[10,10,32,128]{3,2,1,0:T(8,128)(2,1)S(1)} %get-tuple-element.37.xl.refs_5_, bf16[1152,768]{1,0:T(8,128)(2,1)S(1)} %get-tuple-element.40.encoder), custom_call_target="tpu_custom_call" | custom-call | flops 1811939328 | bytes 4000000 | tf_op jit(solution)/shard_map/pallas_call | solution.py:401
  44.8 2.2 %shard_map.31 = (f32[2,2,27,8,128]{4,3,2,1,0:T(8,128)S(1)}, f32[2,2,27,8,128]{4,3,2,1,0:T(8,128)S(1)}) custom-call(f32[2,32,256]{2,1,0:T(8,128)S(1)} %get-tuple-element.32.refs_0_, f32[2,32,256]{2,1,0:T(8,128)S(1)} %collective-permute-done.6.refs_1_, f32[2,32,256]{2,1,0:T(8,128)S(1)} %collective-permute-done.7.refs_2_, ...), custom_call_target="tpu_custom_call" | custom-call | flops 1811939328 | bytes 4000000 | tf_op jit(solution)/shard_map/pallas_call | solution.py:412
  47.0 2.9 %collective-permute-start.9 = (f32[2,2,27,8,128]{4,3,2,1,0:T(8,128)S(1)}, f32[2,2,27,8,128]{4,3,2,1,0:T(8,128)S(1)}, u32[]{:S(2)}, u32[]{:S(2)}) collective-permute-start(f32[2,2,27,8,128]{4,3,2,1,0:T(8,128)S(1)} %get-tuple-element.44), channel_id=1, source_target_pairs={{0,1},{1,0},{2,3},{3,2},{4,5},{5,4},{6,7},{7,6},{8,9},{9,8},{10,11... | collective-permute-start | bytes 1327112 | tf_op jit(solution)/shard_map/ppermute | solution.py:319
  49.9 1.4 %collective-permute-done.9 = f32[2,2,27,8,128]{4,3,2,1,0:T(8,128)S(1)} collective-permute-done((f32[2,2,27,8,128]{4,3,2,1,0:T(8,128)S(1)}, f32[2,2,27,8,128]{4,3,2,1,0:T(8,128)S(1)}, u32[]{:S(2)}, u32[]{:S(2)}) %collective-permute-start.9) | collective-permute-done | bytes 442400 | tf_op jit(solution)/shard_map/ppermute | solution.py:319
  51.4 2.8 %collective-permute-start.10 = (f32[27,8,128]{2,1,0:T(8,128)S(1)}, f32[27,8,128]{2,1,0:T(8,128)S(1)}, u32[]{:S(2)}, u32[]{:S(2)}) collective-permute-start(f32[27,8,128]{2,1,0:T(8,128)S(1)} %get-tuple-element.53), channel_id=1, source_target_pairs={{0,2},{1,3},{2,0},{3,1},{4,6},{5,7},{6,4},{7,5},{8,10},{9,11},{10,... | collective-permute-start | bytes 331784 | tf_op jit(solution)/shard_map/ppermute | solution.py:319
  55.8 3.5 %collective-permute-done.10 = f32[27,8,128]{2,1,0:T(8,128)S(1)} collective-permute-done((f32[27,8,128]{2,1,0:T(8,128)S(1)}, f32[27,8,128]{2,1,0:T(8,128)S(1)}, u32[]{:S(2)}, u32[]{:S(2)}) %collective-permute-start.10) | collective-permute-done | bytes 110624 | tf_op jit(solution)/shard_map/ppermute | solution.py:319
  59.3 1.8 %collective-permute-done.12 = f32[27,8,128]{2,1,0:T(8,128)S(1)} collective-permute-done((f32[27,8,128]{2,1,0:T(8,128)S(1)}, f32[27,8,128]{2,1,0:T(8,128)S(1)}, u32[]{:S(2)}, u32[]{:S(2)}) %collective-permute-start.12) | collective-permute-done | bytes 110624 | tf_op jit(solution)/shard_map/ppermute | solution.py:319
  61.3 1.7 %collective-permute-start.13 = (f32[14,8,128]{2,1,0:T(8,128)S(1)}, f32[14,8,128]{2,1,0:T(8,128)S(1)}, u32[]{:S(2)}, u32[]{:S(2)}) collective-permute-start(f32[14,8,128]{2,1,0:T(8,128)S(1)} %slice.38), channel_id=1, source_target_pairs={{0,2},{1,3},{2,0},{3,1},{4,6},{5,7},{6,4},{7,5},{8,10},{9,11},{10,... | collective-permute-start | bytes 172040 | tf_op jit(solution)/shard_map/ppermute | solution.py:319
  63.0 2.5 %collective-permute-start.16 = (f32[13,8,128]{2,1,0:T(8,128)S(1)}, f32[13,8,128]{2,1,0:T(8,128)S(1)}, u32[]{:S(2)}, u32[]{:S(2)}) collective-permute-start(f32[13,8,128]{2,1,0:T(8,128)S(1)} %slice.39), channel_id=1, source_target_pairs={{0,12},{1,13},{2,14},{3,15},{4,0},{5,1},{6,2},{7,3},{8,4},{9,5},{1... | collective-permute-start | bytes 159752 | tf_op jit(solution)/shard_map/ppermute | solution.py:319
  67.3 3.2 %collective-permute-done.15 = f32[13,8,128]{2,1,0:T(8,128)S(1)} collective-permute-done((f32[13,8,128]{2,1,0:T(8,128)S(1)}, f32[13,8,128]{2,1,0:T(8,128)S(1)}, u32[]{:S(2)}, u32[]{:S(2)}) %collective-permute-start.15) | collective-permute-done | bytes 53280 | tf_op jit(solution)/shard_map/ppermute | solution.py:319
  71.5 1.5 %collective-permute-start.19 = (f32[2,14,8,128]{3,2,1,0:T(8,128)S(1)}, f32[2,14,8,128]{3,2,1,0:T(8,128)S(1)}, u32[]{:S(2)}, u32[]{:S(2)}) collective-permute-start(f32[2,14,8,128]{3,2,1,0:T(8,128)S(1)} %get-tuple-element.59), channel_id=1, source_target_pairs={{0,8},{1,9},{2,10},{3,11},{4,12},{5,13},{6,14},{7,15},{8,0},{9,1},... | collective-permute-start | bytes 344072 | tf_op jit(solution)/shard_map/ppermute | solution.py:319
  73.0 3.8 %collective-permute-start.20 = (f32[2,14,8,128]{3,2,1,0:T(8,128)S(1)}, f32[2,14,8,128]{3,2,1,0:T(8,128)S(1)}, u32[]{:S(2)}, u32[]{:S(2)}) collective-permute-start(f32[2,14,8,128]{3,2,1,0:T(8,128)S(1)} %get-tuple-element.59), channel_id=1, source_target_pairs={{0,12},{1,13},{2,14},{3,15},{4,0},{5,1},{6,2},{7,3},{8,4},{9,5},{1... | collective-permute-start | bytes 344072 | tf_op jit(solution)/shard_map/ppermute | solution.py:319
  77.0 4.0 %collective-permute-done.19 = f32[2,14,8,128]{3,2,1,0:T(8,128)S(1)} collective-permute-done((f32[2,14,8,128]{3,2,1,0:T(8,128)S(1)}, f32[2,14,8,128]{3,2,1,0:T(8,128)S(1)}, u32[]{:S(2)}, u32[]{:S(2)}) %collective-permute-start.19) | collective-permute-done | bytes 114720 | tf_op jit(solution)/shard_map/ppermute | solution.py:319
  81.1 1.7 %collective-permute-done.17 = f32[4,13,8,128]{3,2,1,0:T(8,128)S(1)} collective-permute-done((f32[4,13,8,128]{3,2,1,0:T(8,128)S(1)}, f32[4,13,8,128]{3,2,1,0:T(8,128)S(1)}, u32[]{:S(2)}, u32[]{:S(2)}) %collective-permute-start.17) | collective-permute-done | bytes 213024 | tf_op jit(solution)/shard_map/ppermute | solution.py:319
  82.9 1.7 %collective-permute-done.21.came_early_ref = f32[2,4,13,8,128]{4,3,2,1,0:T(8,128)S(1)} collective-permute-done((f32[2,4,13,8,128]{4,3,2,1,0:T(8,128)S(1)}, f32[2,4,13,8,128]{4,3,2,1,0:T(8,128)S(1)}, u32[]{:S(2)}, u32[]{:S(2)}) %collective-permute-start.21) | collective-permute-done | bytes 426016 | tf_op jit(solution)/shard_map/ppermute | solution.py:319
  84.6 1.8 %shard_map.32 = f32[3456,128]{1,0:T(8,128)} custom-call(f32[2,4,13,8,128]{4,3,2,1,0:T(8,128)S(1)} %pad_maximum_fusion.1.early_ref, f32[4,2,14,8,128]{4,3,2,1,0:T(8,128)S(1)} %pad_maximum_fusion.late_ref, f32[2,4,13,8,128]{4,3,2,1,0:T(8,128)S(1)} %collective-permute-done.21.came_early_ref, f32[4,2,14,8,128]{4,3,2,1,0:T(8,128)S(1)} %collective-permute-done.22.came_late_ref), custom_call_target="tpu_custom_call" | custom-call | bytes 4000000 | tf_op jit(solution)/shard_map/pallas_call | solution.py:439
  (40 shorter events, 8.8 us)
Async XLA Ops:
  0.0 27.1 %copy-start = (f32[1,3456,128]{2,1,0:T(8,128)S(1)}, f32[1,3456,128]{2,1,0:T(8,128)}, u32[]{:S(2)}) copy-start(f32[1,3456,128]{2,1,0:T(8,128)} %weights_ref.1) | copy-start | bytes 5308420
  2.3 19.3 %collective-permute-start.2 = (f32[1152,128]{1,0:T(8,128)}, f32[1152,128]{1,0:T(8,128)S(1)}, u32[]{:S(2)}, u32[]{:S(2)}) collective-permute-start(f32[1152,128]{1,0:T(8,128)} %get-tuple-element.29), channel_id=1, source_target_pairs={{0,16},{1,17},{2,18},{3,19},{4,20},{5,21},{6,22},{7,23},{8,24},{9,... | collective-permute-start | bytes 1769480 | tf_op jit(solution)/shard_map/ppermute | solution.py:319
  5.3 20.0 %collective-permute-start.4 = (f32[576,128]{1,0:T(8,128)}, f32[576,128]{1,0:T(8,128)S(1)}, u32[]{:S(2)}, u32[]{:S(2)}) collective-permute-start(f32[576,128]{1,0:T(8,128)} %get-tuple-element.31), channel_id=1, source_target_pairs={{0,16},{1,17},{2,18},{3,19},{4,20},{5,21},{6,22},{7,23},{8,24},{9,... | collective-permute-start | bytes 884744 | tf_op jit(solution)/shard_map/ppermute | solution.py:319
  21.6 5.5 %collective-permute-start.3 = (f32[1152,128]{1,0:T(8,128)S(1)}, f32[1152,128]{1,0:T(8,128)S(1)}, u32[]{:S(2)}, u32[]{:S(2)}) collective-permute-start(f32[1152,128]{1,0:T(8,128)S(1)} %collective-permute-done.2.refs_0_), channel_id=1, source_target_pairs={{0,1},{1,0},{2,3},{3,2},{4,5},{5,4},{6,7},{7,6},{8,9},{9,8},{10,11... | collective-permute-start | bytes 1769480 | tf_op jit(solution)/shard_map/ppermute | solution.py:319
  21.7 3.7 %collective-permute-start.1 = (f32[4,2,3,32,128]{4,3,2,1,0:T(8,128)S(1)}, f32[4,2,3,32,128]{4,3,2,1,0:T(8,128)S(1)}, u32[]{:S(2)}, u32[]{:S(2)}) collective-permute-start(f32[4,2,3,32,128]{4,3,2,1,0:T(8,128)S(1)} %get-tuple-element.51), channel_id=1, source_target_pairs={{1,2},{2,1},{5,6},{6,5},{9,10},{10,9},{13,14},{14,13},{17,18},{18,... | collective-permute-start | bytes 1179656 | tf_op jit(solution)/shard_map/ppermute | solution.py:319
  22.4 4.3 %collective-permute-start = (f32[4,2,3,32,128]{4,3,2,1,0:T(8,128)S(1)}, f32[4,2,3,32,128]{4,3,2,1,0:T(8,128)S(1)}, u32[]{:S(2)}, u32[]{:S(2)}) collective-permute-start(f32[4,2,3,32,128]{4,3,2,1,0:T(8,128)S(1)} %get-tuple-element.52), channel_id=1, source_target_pairs={{0,1},{1,0},{2,3},{3,2},{4,5},{5,4},{6,7},{7,6},{8,9},{9,8},{10,11... | collective-permute-start | bytes 1179656 | tf_op jit(solution)/shard_map/ppermute | solution.py:319
  25.3 1.8 %collective-permute-start.5 = (f32[576,128]{1,0:T(8,128)S(1)}, f32[576,128]{1,0:T(8,128)S(1)}, u32[]{:S(2)}, u32[]{:S(2)}) collective-permute-start(f32[576,128]{1,0:T(8,128)S(1)} %collective-permute-done.4.refs_2_), channel_id=1, source_target_pairs={{0,1},{1,0},{2,3},{3,2},{4,5},{5,4},{6,7},{7,6},{8,9},{9,8},{10,11... | collective-permute-start | bytes 884744 | tf_op jit(solution)/shard_map/ppermute | solution.py:319
  35.8 7.4 %collective-permute-start.6 = (f32[2,32,256]{2,1,0:T(8,128)S(1)}, f32[2,32,256]{2,1,0:T(8,128)S(1)}, u32[]{:S(2)}, u32[]{:S(2)}) collective-permute-start(f32[2,32,256]{2,1,0:T(8,128)S(1)} %get-tuple-element.33), channel_id=1, source_target_pairs={{0,4},{1,5},{2,6},{3,7},{4,8},{5,9},{6,10},{7,11},{8,12},{9,13},{1... | collective-permute-start | bytes 196616 | tf_op jit(solution)/shard_map/ppermute | solution.py:319
  38.0 5.9 %collective-permute-start.7 = (f32[2,32,256]{2,1,0:T(8,128)S(1)}, f32[2,32,256]{2,1,0:T(8,128)S(1)}, u32[]{:S(2)}, u32[]{:S(2)}) collective-permute-start(f32[2,32,256]{2,1,0:T(8,128)S(1)} %get-tuple-element.34), channel_id=1, source_target_pairs={{0,8},{1,9},{2,10},{3,11},{4,12},{5,13},{6,14},{7,15},{8,0},{9,1},... | collective-permute-start | bytes 196616 | tf_op jit(solution)/shard_map/ppermute | solution.py:319
  40.5 4.3 %collective-permute-start.8 = (f32[2,32,256]{2,1,0:T(8,128)S(1)}, f32[2,32,256]{2,1,0:T(8,128)S(1)}, u32[]{:S(2)}, u32[]{:S(2)}) collective-permute-start(f32[2,32,256]{2,1,0:T(8,128)S(1)} %get-tuple-element.35), channel_id=1, source_target_pairs={{0,12},{1,13},{2,14},{3,15},{4,0},{5,1},{6,2},{7,3},{8,4},{9,5},{1... | collective-permute-start | bytes 196616 | tf_op jit(solution)/shard_map/ppermute | solution.py:319
  47.0 4.3 %collective-permute-start.9 = (f32[2,2,27,8,128]{4,3,2,1,0:T(8,128)S(1)}, f32[2,2,27,8,128]{4,3,2,1,0:T(8,128)S(1)}, u32[]{:S(2)}, u32[]{:S(2)}) collective-permute-start(f32[2,2,27,8,128]{4,3,2,1,0:T(8,128)S(1)} %get-tuple-element.44), channel_id=1, source_target_pairs={{0,1},{1,0},{2,3},{3,2},{4,5},{5,4},{6,7},{7,6},{8,9},{9,8},{10,11... | collective-permute-start | bytes 1327112 | tf_op jit(solution)/shard_map/ppermute | solution.py:319
  51.4 7.9 %collective-permute-start.10 = (f32[27,8,128]{2,1,0:T(8,128)S(1)}, f32[27,8,128]{2,1,0:T(8,128)S(1)}, u32[]{:S(2)}, u32[]{:S(2)}) collective-permute-start(f32[27,8,128]{2,1,0:T(8,128)S(1)} %get-tuple-element.53), channel_id=1, source_target_pairs={{0,2},{1,3},{2,0},{3,1},{4,6},{5,7},{6,4},{7,5},{8,10},{9,11},{10,... | collective-permute-start | bytes 331784 | tf_op jit(solution)/shard_map/ppermute | solution.py:319
  54.3 6.8 %collective-permute-start.12 = (f32[27,8,128]{2,1,0:T(8,128)S(1)}, f32[27,8,128]{2,1,0:T(8,128)S(1)}, u32[]{:S(2)}, u32[]{:S(2)}) collective-permute-start(f32[27,8,128]{2,1,0:T(8,128)S(1)} %get-tuple-element.54), channel_id=1, source_target_pairs={{0,18},{1,19},{2,16},{3,17},{4,22},{5,23},{6,20},{7,21},{8,26},{9,... | collective-permute-start | bytes 331784 | tf_op jit(solution)/shard_map/ppermute | solution.py:319
  55.3 6.0 %collective-permute-start.11 = (f32[27,8,128]{2,1,0:T(8,128)S(1)}, f32[27,8,128]{2,1,0:T(8,128)S(1)}, u32[]{:S(2)}, u32[]{:S(2)}) collective-permute-start(f32[27,8,128]{2,1,0:T(8,128)S(1)} %get-tuple-element.55), channel_id=1, source_target_pairs={{0,16},{1,17},{2,18},{3,19},{4,20},{5,21},{6,22},{7,23},{8,24},{9,... | collective-permute-start | bytes 331784 | tf_op jit(solution)/shard_map/ppermute | solution.py:319
  61.3 10.1 %collective-permute-start.13 = (f32[14,8,128]{2,1,0:T(8,128)S(1)}, f32[14,8,128]{2,1,0:T(8,128)S(1)}, u32[]{:S(2)}, u32[]{:S(2)}) collective-permute-start(f32[14,8,128]{2,1,0:T(8,128)S(1)} %slice.38), channel_id=1, source_target_pairs={{0,2},{1,3},{2,0},{3,1},{4,6},{5,7},{6,4},{7,5},{8,10},{9,11},{10,... | collective-permute-start | bytes 172040 | tf_op jit(solution)/shard_map/ppermute | solution.py:319
  63.0 4.3 %collective-permute-start.16 = (f32[13,8,128]{2,1,0:T(8,128)S(1)}, f32[13,8,128]{2,1,0:T(8,128)S(1)}, u32[]{:S(2)}, u32[]{:S(2)}) collective-permute-start(f32[13,8,128]{2,1,0:T(8,128)S(1)} %slice.39), channel_id=1, source_target_pairs={{0,12},{1,13},{2,14},{3,15},{4,0},{5,1},{6,2},{7,3},{8,4},{9,5},{1... | collective-permute-start | bytes 159752 | tf_op jit(solution)/shard_map/ppermute | solution.py:319
  65.5 5.0 %collective-permute-start.15 = (f32[13,8,128]{2,1,0:T(8,128)S(1)}, f32[13,8,128]{2,1,0:T(8,128)S(1)}, u32[]{:S(2)}, u32[]{:S(2)}) collective-permute-start(f32[13,8,128]{2,1,0:T(8,128)S(1)} %slice.39), channel_id=1, source_target_pairs={{0,8},{1,9},{2,10},{3,11},{4,12},{5,13},{6,14},{7,15},{8,0},{9,1},... | collective-permute-start | bytes 159752 | tf_op jit(solution)/shard_map/ppermute | solution.py:319
  65.5 5.9 %collective-permute-start.14 = (f32[13,8,128]{2,1,0:T(8,128)S(1)}, f32[13,8,128]{2,1,0:T(8,128)S(1)}, u32[]{:S(2)}, u32[]{:S(2)}) collective-permute-start(f32[13,8,128]{2,1,0:T(8,128)S(1)} %slice.39), channel_id=1, source_target_pairs={{0,4},{1,5},{2,6},{3,7},{4,8},{5,9},{6,10},{7,11},{8,12},{9,13},{1... | collective-permute-start | bytes 159752 | tf_op jit(solution)/shard_map/ppermute | solution.py:319
  71.5 9.5 %collective-permute-start.19 = (f32[2,14,8,128]{3,2,1,0:T(8,128)S(1)}, f32[2,14,8,128]{3,2,1,0:T(8,128)S(1)}, u32[]{:S(2)}, u32[]{:S(2)}) collective-permute-start(f32[2,14,8,128]{3,2,1,0:T(8,128)S(1)} %get-tuple-element.59), channel_id=1, source_target_pairs={{0,8},{1,9},{2,10},{3,11},{4,12},{5,13},{6,14},{7,15},{8,0},{9,1},... | collective-permute-start | bytes 344072 | tf_op jit(solution)/shard_map/ppermute | solution.py:319
  73.0 8.0 %collective-permute-start.18 = (f32[2,14,8,128]{3,2,1,0:T(8,128)S(1)}, f32[2,14,8,128]{3,2,1,0:T(8,128)S(1)}, u32[]{:S(2)}, u32[]{:S(2)}) collective-permute-start(f32[2,14,8,128]{3,2,1,0:T(8,128)S(1)} %get-tuple-element.59), channel_id=1, source_target_pairs={{0,4},{1,5},{2,6},{3,7},{4,8},{5,9},{6,10},{7,11},{8,12},{9,13},{1... | collective-permute-start | bytes 344072 | tf_op jit(solution)/shard_map/ppermute | solution.py:319
  73.0 8.0 %collective-permute-start.20 = (f32[2,14,8,128]{3,2,1,0:T(8,128)S(1)}, f32[2,14,8,128]{3,2,1,0:T(8,128)S(1)}, u32[]{:S(2)}, u32[]{:S(2)}) collective-permute-start(f32[2,14,8,128]{3,2,1,0:T(8,128)S(1)} %get-tuple-element.59), channel_id=1, source_target_pairs={{0,12},{1,13},{2,14},{3,15},{4,0},{5,1},{6,2},{7,3},{8,4},{9,5},{1... | collective-permute-start | bytes 344072 | tf_op jit(solution)/shard_map/ppermute | solution.py:319
  76.9 5.9 %collective-permute-start.17 = (f32[4,13,8,128]{3,2,1,0:T(8,128)S(1)}, f32[4,13,8,128]{3,2,1,0:T(8,128)S(1)}, u32[]{:S(2)}, u32[]{:S(2)}) collective-permute-start(f32[4,13,8,128]{3,2,1,0:T(8,128)S(1)} %get-tuple-element.57), channel_id=1, source_target_pairs={{0,2},{1,3},{2,0},{3,1},{4,6},{5,7},{6,4},{7,5},{8,10},{9,11},{10,... | collective-permute-start | bytes 638984 | tf_op jit(solution)/shard_map/ppermute | solution.py:319
  81.0 1.9 %collective-permute-start.22 = (f32[4,2,14,8,128]{4,3,2,1,0:T(8,128)S(1)}, f32[4,2,14,8,128]{4,3,2,1,0:T(8,128)S(1)}, u32[]{:S(2)}, u32[]{:S(2)}) collective-permute-start(f32[4,2,14,8,128]{4,3,2,1,0:T(8,128)S(1)} %pad_maximum_fusion.late_ref), channel_id=1, source_target_pairs={{0,1},{1,0},{2,3},{3,2},{4,5},{5,4},{6,7},{7,6},{8,9},{9,8},{10,11... | collective-permute-start | bytes 1376264 | tf_op jit(solution)/shard_map/ppermute | solution.py:319
  82.8 1.8 %collective-permute-start.21 = (f32[2,4,13,8,128]{4,3,2,1,0:T(8,128)S(1)}, f32[2,4,13,8,128]{4,3,2,1,0:T(8,128)S(1)}, u32[]{:S(2)}, u32[]{:S(2)}) collective-permute-start(f32[2,4,13,8,128]{4,3,2,1,0:T(8,128)S(1)} %pad_maximum_fusion.1.early_ref), channel_id=1, source_target_pairs={{0,1},{1,0},{2,3},{3,2},{4,5},{5,4},{6,7},{7,6},{8,9},{9,8},{10,11... | collective-permute-start | bytes 1277960 | tf_op jit(solution)/shard_map/ppermute | solution.py:319

commit v3 on v2

--- a/solution.py
+++ b/solution.py
@@ -43,9 +43,15 @@
 def put_taps(to_ref, tap, x):
     channels = x.shape[-1]
     rows = pl.ds((tap // 3) * channels, channels)
+    lanes = pl.ds((tap % 3) * channels, channels)
+    low_lanes = pl.ds((tap % 3 + 3) * channels, channels)
     high, low = split(x)
-    to_ref[rows, pl.ds((tap % 3) * channels, channels)] = high
-    to_ref[rows, pl.ds((tap % 3 + 3) * channels, channels)] = low
+    to_ref[rows, lanes] = high
+    to_ref[rows, low_lanes] = low
+    if tap >= 24:
+        rows = pl.ds(9 * channels, channels)
+        to_ref[rows, lanes] = high
+        to_ref[rows, low_lanes] = jnp.zeros_like(low)
 
 
 def shifted_sum(y, columns, channels, flip):
@@ -66,8 +72,8 @@
         high.append(high_ref[at].reshape(count * frames * columns, channels))
         low.append(low_ref[at].reshape(count * frames * columns, channels))
     full = 3 * channels
-    both = dot(jnp.concatenate(high, axis=1), weight_ref[...])
-    rest = dot(jnp.concatenate(low, axis=1), weight_ref[:, pl.ds(0, full)])
+    both = dot(jnp.concatenate(high + low[8:], axis=1), weight_ref[...])
+    rest = dot(jnp.concatenate(low[:8], axis=1), weight_ref[pl.ds(0, 8 * channels), pl.ds(0, full)])
     y = both[:, :full] + both[:, full:] + rest
     return shifted_sum(y, columns, channels, flip).reshape(count, frames, columns, channels)
 
@@ -382,11 +388,11 @@
             [shape((2, part, per * cells), f32)] * tm
             + [shape((height + 6,) + field, bf16)] * 2
             + [shape((rows,) + field, bf16)] * 2
-            + [shape((9 * channels, 6 * channels), bf16)],
+            + [shape((10 * channels, 6 * channels), bf16)],
             [
                 vmem((height + 2, frames, columns, channels), f32),
-                vmem((9 * channels, 6 * channels), bf16),
-                vmem((9 * channels, 6 * channels), bf16),
+                vmem((10 * channels, 6 * channels), bf16),
+                vmem((10 * channels, 6 * channels), bf16),
                 vmem((per + 2,) + field, bf16),
                 vmem((per + 2,) + field, bf16),
                 vmem((per, frames, columns, channels), f32),
@@ -427,7 +433,7 @@
                 if flip or step:
                     total = total + send(both[flip, step], across(flip, step))
 
-        cut = taps // 2
+        cut = 2 * taps // 3
         early, late = total[:cut], total[cut:]
         late_rows = [late] + [send(late, across(0, k)) for k in range(1, pairs)]
         early_all = [early] + [send(early, later(k)) for k in range(1, tm)]
@@ -435,6 +441,7 @@
         late_rows, early_all = jnp.stack(late_rows), jnp.stack(early_all)
         early_all = jnp.stack([early_all] + [send(early_all, across(0, k)) for k in range(1, pairs)])
         late_all = jnp.stack([late_rows] + [send(late_rows, later(k)) for k in range(1, tm)])
+        early_all, late_all = lax.optimization_barrier((early_all, late_all))
         came = [send(x, swap_core) for x in (early_all, late_all)]
         out = call(
             functools.partial(assembled_kernel, (tm, pairs, channels)),

time: 86.6 us -> 84.3 us (0.973)
  waiting for transfers between devices: 22.9 us -> 19.4 us
  starting transfers between devices: 30.1 us -> 31.9 us
    ppermute x23, waiting for transfers between devices: 22.9 us -> 19.4 us  [send(): return lax.ppermute(x, AXES, route)]
    ppermute x23, starting transfers between devices: 30.1 us -> 31.9 us  [send(): return lax.ppermute(x, AXES, route)]
  transfers between devices with their start and end apart: 23 -> 23, of which waited for: 14 -> 13; matrix products, arithmetic and copies ran while one was open for 0% -> 0% of each run, Pallas kernels for 2% -> 2%
where the time goes in v3:
time: 84.3 us; the launch traced here: 84.2 us
  starting transfers between devices  31.9 us (38%)
  waiting for transfers between devices  19.4 us (23%)
  Pallas kernels  16.3 us (19%)
  blocking collectives  16.1 us (19%)
    ppermute x23, starting transfers between devices, send(): return lax.ppermute(x, AXES, route)  31.9 us
    ppermute x23, waiting for transfers between devices, send(): return lax.ppermute(x, AXES, route)  19.4 us
    all_gather x1, blocking collectives, local(): block = lax.all_gather(clip, 'tm')  16.1 us
    pallas_call x1, Pallas kernels, local(): call(functools.partial(activations_kernel, dims), [shape((2, part, per *...  8.34 us
    pallas_call x1, Pallas kernels, local(): call(pick_kernel, [jax.ShapeDtypeStruct((third, channels), f32), jax.Shap...  2.27 us
    pallas_call x1, Pallas kernels, local(): call(functools.partial(weights_kernel, (tm, own_frames, height, rows_all,...  2.19 us
    pallas_call x1, Pallas kernels, local(): call(functools.partial(latents_kernel, dims), [shape((extra,) + field, bf...  1.76 us
    pallas_call x1, Pallas kernels, local(): call(functools.partial(assembled_kernel, (tm, pairs, channels)), jax.Shap...  1.75 us
  transfers between devices with their start and end apart: 23, of which 13 were waited for; matrix products, arithmetic and copies ran while one was open for 0% of the time, Pallas kernels for 2%

profile of v3, /device:TPU:0, one launch (start us, length us, event | category | flops | bytes accessed | tf_op | source)
XLA Modules:
  0.0 84.2 jit_solution(12212491744267664130)
XLA Ops:
  0.0 2.3 %shard_map.28 = (f32[1152,128]{1,0:T(8,128)}, f32[576,128]{1,0:T(8,128)}, f32[2,4,32,128]{3,2,1,0:T(8,128)}) custom-call(f32[2,2,4,32,128]{4,3,2,1,0:T(8,128)} %video_ref.1, f32[1,3456,128]{2,1,0:T(8,128)} %weights_ref.1), custom_call_target="tpu_custom_call" | custom-call | bytes 4000000 | tf_op jit(solution)/shard_map/pallas_call | solution.py:355
  2.3 3.0 %collective-permute-start.2 = (f32[1152,128]{1,0:T(8,128)}, f32[1152,128]{1,0:T(8,128)S(1)}, u32[]{:S(2)}, u32[]{:S(2)}) collective-permute-start(f32[1152,128]{1,0:T(8,128)} %get-tuple-element.31), channel_id=1, source_target_pairs={{0,16},{1,17},{2,18},{3,19},{4,20},{5,21},{6,22},{7,23},{8,24},{9,... | collective-permute-start | bytes 1769480 | tf_op jit(solution)/shard_map/ppermute | solution.py:325
  5.4 16.1 %all-gather = f32[8,4,32,128]{3,2,1,0:T(8,128)S(1)} all-gather(f32[2,4,32,128]{3,2,1,0:T(8,128)} %get-tuple-element.30), channel_id=2, replica_groups=mesh['segment'=2,'tm'=4,'space'=4] {'tm'}, dimensions={0}, use_global_device_ids=true | all-gather | bytes 655360 | tf_op jit(solution)/shard_map/all_gather | solution.py:370
  22.4 2.9 %collective-permute-start = (f32[4,2,3,32,128]{4,3,2,1,0:T(8,128)S(1)}, f32[4,2,3,32,128]{4,3,2,1,0:T(8,128)S(1)}, u32[]{:S(2)}, u32[]{:S(2)}) collective-permute-start(f32[4,2,3,32,128]{4,3,2,1,0:T(8,128)S(1)} %get-tuple-element.56), channel_id=1, source_target_pairs={{0,1},{1,0},{2,3},{3,2},{4,5},{5,4},{6,7},{7,6},{8,9},{9,8},{10,11... | collective-permute-start | bytes 1179656 | tf_op jit(solution)/shard_map/ppermute | solution.py:325
  27.1 8.3 %shard_map.29 = (f32[2,32,256]{2,1,0:T(8,128)S(1)}, f32[2,32,256]{2,1,0:T(8,128)S(1)}, f32[2,32,256]{2,1,0:T(8,128)S(1)}, f32[2,32,256]{2,1,0:T(8,128)S(1)}, bf1...) custom-call(f32[4,2,4,32,128]{4,3,2,1,0:T(8,128)S(1)} %bitcast.32, ...), custom_call_target="tpu_custom_call" | custom-call | flops 8153726976 | bytes 4000000 | tf_op jit(solution)/shard_map/pallas_call | solution.py:386
  35.4 2.2 %collective-permute-start.6 = (f32[2,32,256]{2,1,0:T(8,128)S(1)}, f32[2,32,256]{2,1,0:T(8,128)S(1)}, u32[]{:S(2)}, u32[]{:S(2)}) collective-permute-start(f32[2,32,256]{2,1,0:T(8,128)S(1)} %get-tuple-element.35), channel_id=1, source_target_pairs={{0,4},{1,5},{2,6},{3,7},{4,8},{5,9},{6,10},{7,11},{8,12},{9,13},{1... | collective-permute-start | bytes 196616 | tf_op jit(solution)/shard_map/ppermute | solution.py:325
  37.6 2.5 %collective-permute-start.7 = (f32[2,32,256]{2,1,0:T(8,128)S(1)}, f32[2,32,256]{2,1,0:T(8,128)S(1)}, u32[]{:S(2)}, u32[]{:S(2)}) collective-permute-start(f32[2,32,256]{2,1,0:T(8,128)S(1)} %get-tuple-element.36), channel_id=1, source_target_pairs={{0,8},{1,9},{2,10},{3,11},{4,12},{5,13},{6,14},{7,15},{8,0},{9,1},... | collective-permute-start | bytes 196616 | tf_op jit(solution)/shard_map/ppermute | solution.py:325
  40.9 1.8 %shard_map.30 = (bf16[2,10,32,128]{3,2,1,0:T(8,128)(2,1)S(1)}, bf16[2,10,32,128]{3,2,1,0:T(8,128)(2,1)S(1)}) custom-call(bf16[10,10,32,128]{3,2,1,0:T(8,128)(2,1)S(1)} %get-tuple-element.38.xh.refs_4_, bf16[10,10,32,128]{3,2,1,0:T(8,128)(2,1)S(1)} %get-tuple-element.39.xl.refs_5_, bf16[1280,768]{1,0:T(8,128)(2,1)S(1)} %get-tuple-element.42.encoder), custom_call_target="tpu_custom_call" | custom-call | flops 1811939328 | bytes 4000000 | tf_op jit(solution)/shard_map/pallas_call | solution.py:407
  44.4 2.2 %shard_map.31 = (f32[2,2,27,8,128]{4,3,2,1,0:T(8,128)S(1)}, f32[2,2,27,8,128]{4,3,2,1,0:T(8,128)S(1)}) custom-call(f32[2,32,256]{2,1,0:T(8,128)S(1)} %get-tuple-element.34.refs_0_, f32[2,32,256]{2,1,0:T(8,128)S(1)} %collective-permute-done.6.refs_1_, f32[2,32,256]{2,1,0:T(8,128)S(1)} %collective-permute-done.7.refs_2_, ...), custom_call_target="tpu_custom_call" | custom-call | flops 1811939328 | bytes 4000000 | tf_op jit(solution)/shard_map/pallas_call | solution.py:418
  46.6 2.9 %collective-permute-start.9 = (f32[2,2,27,8,128]{4,3,2,1,0:T(8,128)S(1)}, f32[2,2,27,8,128]{4,3,2,1,0:T(8,128)S(1)}, u32[]{:S(2)}, u32[]{:S(2)}) collective-permute-start(f32[2,2,27,8,128]{4,3,2,1,0:T(8,128)S(1)} %get-tuple-element.46), channel_id=1, source_target_pairs={{0,1},{1,0},{2,3},{3,2},{4,5},{5,4},{6,7},{7,6},{8,9},{9,8},{10,11... | collective-permute-start | bytes 1327112 | tf_op jit(solution)/shard_map/ppermute | solution.py:325
  49.6 1.4 %collective-permute-done.9 = f32[2,2,27,8,128]{4,3,2,1,0:T(8,128)S(1)} collective-permute-done((f32[2,2,27,8,128]{4,3,2,1,0:T(8,128)S(1)}, f32[2,2,27,8,128]{4,3,2,1,0:T(8,128)S(1)}, u32[]{:S(2)}, u32[]{:S(2)}) %collective-permute-start.9) | collective-permute-done | bytes 442400 | tf_op jit(solution)/shard_map/ppermute | solution.py:325
  51.1 2.8 %collective-permute-start.10 = (f32[27,8,128]{2,1,0:T(8,128)S(1)}, f32[27,8,128]{2,1,0:T(8,128)S(1)}, u32[]{:S(2)}, u32[]{:S(2)}) collective-permute-start(f32[27,8,128]{2,1,0:T(8,128)S(1)} %get-tuple-element.57), channel_id=1, source_target_pairs={{0,2},{1,3},{2,0},{3,1},{4,6},{5,7},{6,4},{7,5},{8,10},{9,11},{10,... | collective-permute-start | bytes 331784 | tf_op jit(solution)/shard_map/ppermute | solution.py:325
  55.4 3.5 %collective-permute-done.10 = f32[27,8,128]{2,1,0:T(8,128)S(1)} collective-permute-done((f32[27,8,128]{2,1,0:T(8,128)S(1)}, f32[27,8,128]{2,1,0:T(8,128)S(1)}, u32[]{:S(2)}, u32[]{:S(2)}) %collective-permute-start.10) | collective-permute-done | bytes 110624 | tf_op jit(solution)/shard_map/ppermute | solution.py:325
  58.9 1.8 %collective-permute-done.12 = f32[27,8,128]{2,1,0:T(8,128)S(1)} collective-permute-done((f32[27,8,128]{2,1,0:T(8,128)S(1)}, f32[27,8,128]{2,1,0:T(8,128)S(1)}, u32[]{:S(2)}, u32[]{:S(2)}) %collective-permute-start.12) | collective-permute-done | bytes 110624 | tf_op jit(solution)/shard_map/ppermute | solution.py:325
  61.0 2.6 %collective-permute-start.16 = (f32[18,8,128]{2,1,0:T(8,128)S(1)}, f32[18,8,128]{2,1,0:T(8,128)S(1)}, u32[]{:S(2)}, u32[]{:S(2)}) collective-permute-start(f32[18,8,128]{2,1,0:T(8,128)S(1)} %slice.39), channel_id=1, source_target_pairs={{0,12},{1,13},{2,14},{3,15},{4,0},{5,1},{6,2},{7,3},{8,4},{9,5},{1... | collective-permute-start | bytes 221192 | tf_op jit(solution)/shard_map/ppermute | solution.py:325
  64.2 1.6 %collective-permute-start.13 = (f32[9,8,128]{2,1,0:T(8,128)S(1)}, f32[9,8,128]{2,1,0:T(8,128)S(1)}, u32[]{:S(2)}, u32[]{:S(2)}) collective-permute-start(f32[9,8,128]{2,1,0:T(8,128)S(1)} %slice.38), channel_id=1, source_target_pairs={{0,2},{1,3},{2,0},{3,1},{4,6},{5,7},{6,4},{7,5},{8,10},{9,11},{10,... | collective-permute-start | bytes 110600 | tf_op jit(solution)/shard_map/ppermute | solution.py:325
  65.8 2.3 %collective-permute-done.13 = f32[9,8,128]{2,1,0:T(8,128)S(1)} collective-permute-done((f32[9,8,128]{2,1,0:T(8,128)S(1)}, f32[9,8,128]{2,1,0:T(8,128)S(1)}, u32[]{:S(2)}, u32[]{:S(2)}) %collective-permute-start.13) | collective-permute-done | bytes 36896 | tf_op jit(solution)/shard_map/ppermute | solution.py:325
  68.2 2.1 %collective-permute-done.15 = f32[18,8,128]{2,1,0:T(8,128)S(1)} collective-permute-done((f32[18,8,128]{2,1,0:T(8,128)S(1)}, f32[18,8,128]{2,1,0:T(8,128)S(1)}, u32[]{:S(2)}, u32[]{:S(2)}) %collective-permute-start.15) | collective-permute-done | bytes 73760 | tf_op jit(solution)/shard_map/ppermute | solution.py:325
  71.6 1.8 %collective-permute-start.19 = (f32[2,9,8,128]{3,2,1,0:T(8,128)S(1)}, f32[2,9,8,128]{3,2,1,0:T(8,128)S(1)}, u32[]{:S(2)}, u32[]{:S(2)}) collective-permute-start(f32[2,9,8,128]{3,2,1,0:T(8,128)S(1)} %get-tuple-element.63), channel_id=1, source_target_pairs={{0,8},{1,9},{2,10},{3,11},{4,12},{5,13},{6,14},{7,15},{8,0},{9,1},... | collective-permute-start | bytes 221192 | tf_op jit(solution)/shard_map/ppermute | solution.py:325
  74.0 3.2 %collective-permute-start.20 = (f32[2,9,8,128]{3,2,1,0:T(8,128)S(1)}, f32[2,9,8,128]{3,2,1,0:T(8,128)S(1)}, u32[]{:S(2)}, u32[]{:S(2)}) collective-permute-start(f32[2,9,8,128]{3,2,1,0:T(8,128)S(1)} %get-tuple-element.63), channel_id=1, source_target_pairs={{0,12},{1,13},{2,14},{3,15},{4,0},{5,1},{6,2},{7,3},{8,4},{9,5},{1... | collective-permute-start | bytes 221192 | tf_op jit(solution)/shard_map/ppermute | solution.py:325
  77.2 1.4 %collective-permute-done.19 = f32[2,9,8,128]{3,2,1,0:T(8,128)S(1)} collective-permute-done((f32[2,9,8,128]{3,2,1,0:T(8,128)S(1)}, f32[2,9,8,128]{3,2,1,0:T(8,128)S(1)}, u32[]{:S(2)}, u32[]{:S(2)}) %collective-permute-start.19) | collective-permute-done | bytes 73760 | tf_op jit(solution)/shard_map/ppermute | solution.py:325
  78.6 1.3 %collective-permute-done.18 = f32[2,9,8,128]{3,2,1,0:T(8,128)S(1)} collective-permute-done((f32[2,9,8,128]{3,2,1,0:T(8,128)S(1)}, f32[2,9,8,128]{3,2,1,0:T(8,128)S(1)}, u32[]{:S(2)}, u32[]{:S(2)}) %collective-permute-start.18) | collective-permute-done | bytes 73760 | tf_op jit(solution)/shard_map/ppermute | solution.py:325
  80.5 1.9 %collective-permute-done.22.came_late_ref = f32[4,2,9,8,128]{4,3,2,1,0:T(8,128)S(1)} collective-permute-done((f32[4,2,9,8,128]{4,3,2,1,0:T(8,128)S(1)}, f32[4,2,9,8,128]{4,3,2,1,0:T(8,128)S(1)}, u32[]{:S(2)}, u32[]{:S(2)}) %collective-permute-start.22) | collective-permute-done | bytes 294944 | tf_op jit(solution)/shard_map/ppermute | solution.py:325
  82.4 1.8 %shard_map.32 = f32[3456,128]{1,0:T(8,128)} custom-call(f32[2,4,18,8,128]{4,3,2,1,0:T(8,128)S(1)} %pad_maximum_fusion.early_ref, f32[4,2,9,8,128]{4,3,2,1,0:T(8,128)S(1)} %pad_maximum_fusion.2.late_ref, f32[2,4,18,8,128]{4,3,2,1,0:T(8,128)S(1)} %collective-permute-done.21.came_early_ref, f32[4,2,9,8,128]{4,3,2,1,0:T(8,128)S(1)} %collective-permute-done.22.came_late_ref), custom_call_target="tpu_custom_call" | custom-call | bytes 4000000 | tf_op jit(solution)/shard_map/pallas_call | solution.py:446
  (40 shorter events, 10.3 us)
Async XLA Ops:
  0.0 27.1 %copy-start = (f32[1,3456,128]{2,1,0:T(8,128)S(1)}, f32[1,3456,128]{2,1,0:T(8,128)}, u32[]{:S(2)}) copy-start(f32[1,3456,128]{2,1,0:T(8,128)} %weights_ref.1) | copy-start | bytes 5308420
  2.3 19.3 %collective-permute-start.2 = (f32[1152,128]{1,0:T(8,128)}, f32[1152,128]{1,0:T(8,128)S(1)}, u32[]{:S(2)}, u32[]{:S(2)}) collective-permute-start(f32[1152,128]{1,0:T(8,128)} %get-tuple-element.31), channel_id=1, source_target_pairs={{0,16},{1,17},{2,18},{3,19},{4,20},{5,21},{6,22},{7,23},{8,24},{9,... | collective-permute-start | bytes 1769480 | tf_op jit(solution)/shard_map/ppermute | solution.py:325
  5.3 20.0 %collective-permute-start.4 = (f32[576,128]{1,0:T(8,128)}, f32[576,128]{1,0:T(8,128)S(1)}, u32[]{:S(2)}, u32[]{:S(2)}) collective-permute-start(f32[576,128]{1,0:T(8,128)} %get-tuple-element.33), channel_id=1, source_target_pairs={{0,16},{1,17},{2,18},{3,19},{4,20},{5,21},{6,22},{7,23},{8,24},{9,... | collective-permute-start | bytes 884744 | tf_op jit(solution)/shard_map/ppermute | solution.py:325
  21.6 5.5 %collective-permute-start.3 = (f32[1152,128]{1,0:T(8,128)S(1)}, f32[1152,128]{1,0:T(8,128)S(1)}, u32[]{:S(2)}, u32[]{:S(2)}) collective-permute-start(f32[1152,128]{1,0:T(8,128)S(1)} %collective-permute-done.2.refs_0_), channel_id=1, source_target_pairs={{0,1},{1,0},{2,3},{3,2},{4,5},{5,4},{6,7},{7,6},{8,9},{9,8},{10,11... | collective-permute-start | bytes 1769480 | tf_op jit(solution)/shard_map/ppermute | solution.py:325
  21.7 3.7 %collective-permute-start.1 = (f32[4,2,3,32,128]{4,3,2,1,0:T(8,128)S(1)}, f32[4,2,3,32,128]{4,3,2,1,0:T(8,128)S(1)}, u32[]{:S(2)}, u32[]{:S(2)}) collective-permute-start(f32[4,2,3,32,128]{4,3,2,1,0:T(8,128)S(1)} %get-tuple-element.55), channel_id=1, source_target_pairs={{1,2},{2,1},{5,6},{6,5},{9,10},{10,9},{13,14},{14,13},{17,18},{18,... | collective-permute-start | bytes 1179656 | tf_op jit(solution)/shard_map/ppermute | solution.py:325
  22.4 4.3 %collective-permute-start = (f32[4,2,3,32,128]{4,3,2,1,0:T(8,128)S(1)}, f32[4,2,3,32,128]{4,3,2,1,0:T(8,128)S(1)}, u32[]{:S(2)}, u32[]{:S(2)}) collective-permute-start(f32[4,2,3,32,128]{4,3,2,1,0:T(8,128)S(1)} %get-tuple-element.56), channel_id=1, source_target_pairs={{0,1},{1,0},{2,3},{3,2},{4,5},{5,4},{6,7},{7,6},{8,9},{9,8},{10,11... | collective-permute-start | bytes 1179656 | tf_op jit(solution)/shard_map/ppermute | solution.py:325
  25.3 1.8 %collective-permute-start.5 = (f32[576,128]{1,0:T(8,128)S(1)}, f32[576,128]{1,0:T(8,128)S(1)}, u32[]{:S(2)}, u32[]{:S(2)}) collective-permute-start(f32[576,128]{1,0:T(8,128)S(1)} %collective-permute-done.4.refs_2_), channel_id=1, source_target_pairs={{0,1},{1,0},{2,3},{3,2},{4,5},{5,4},{6,7},{7,6},{8,9},{9,8},{10,11... | collective-permute-start | bytes 884744 | tf_op jit(solution)/shard_map/ppermute | solution.py:325
  35.4 7.3 %collective-permute-start.6 = (f32[2,32,256]{2,1,0:T(8,128)S(1)}, f32[2,32,256]{2,1,0:T(8,128)S(1)}, u32[]{:S(2)}, u32[]{:S(2)}) collective-permute-start(f32[2,32,256]{2,1,0:T(8,128)S(1)} %get-tuple-element.35), channel_id=1, source_target_pairs={{0,4},{1,5},{2,6},{3,7},{4,8},{5,9},{6,10},{7,11},{8,12},{9,13},{1... | collective-permute-start | bytes 196616 | tf_op jit(solution)/shard_map/ppermute | solution.py:325
  37.6 5.9 %collective-permute-start.7 = (f32[2,32,256]{2,1,0:T(8,128)S(1)}, f32[2,32,256]{2,1,0:T(8,128)S(1)}, u32[]{:S(2)}, u32[]{:S(2)}) collective-permute-start(f32[2,32,256]{2,1,0:T(8,128)S(1)} %get-tuple-element.36), channel_id=1, source_target_pairs={{0,8},{1,9},{2,10},{3,11},{4,12},{5,13},{6,14},{7,15},{8,0},{9,1},... | collective-permute-start | bytes 196616 | tf_op jit(solution)/shard_map/ppermute | solution.py:325
  40.2 4.3 %collective-permute-start.8 = (f32[2,32,256]{2,1,0:T(8,128)S(1)}, f32[2,32,256]{2,1,0:T(8,128)S(1)}, u32[]{:S(2)}, u32[]{:S(2)}) collective-permute-start(f32[2,32,256]{2,1,0:T(8,128)S(1)} %get-tuple-element.37), channel_id=1, source_target_pairs={{0,12},{1,13},{2,14},{3,15},{4,0},{5,1},{6,2},{7,3},{8,4},{9,5},{1... | collective-permute-start | bytes 196616 | tf_op jit(solution)/shard_map/ppermute | solution.py:325
  46.6 4.4 %collective-permute-start.9 = (f32[2,2,27,8,128]{4,3,2,1,0:T(8,128)S(1)}, f32[2,2,27,8,128]{4,3,2,1,0:T(8,128)S(1)}, u32[]{:S(2)}, u32[]{:S(2)}) collective-permute-start(f32[2,2,27,8,128]{4,3,2,1,0:T(8,128)S(1)} %get-tuple-element.46), channel_id=1, source_target_pairs={{0,1},{1,0},{2,3},{3,2},{4,5},{5,4},{6,7},{7,6},{8,9},{9,8},{10,11... | collective-permute-start | bytes 1327112 | tf_op jit(solution)/shard_map/ppermute | solution.py:325
  51.1 7.8 %collective-permute-start.10 = (f32[27,8,128]{2,1,0:T(8,128)S(1)}, f32[27,8,128]{2,1,0:T(8,128)S(1)}, u32[]{:S(2)}, u32[]{:S(2)}) collective-permute-start(f32[27,8,128]{2,1,0:T(8,128)S(1)} %get-tuple-element.57), channel_id=1, source_target_pairs={{0,2},{1,3},{2,0},{3,1},{4,6},{5,7},{6,4},{7,5},{8,10},{9,11},{10,... | collective-permute-start | bytes 331784 | tf_op jit(solution)/shard_map/ppermute | solution.py:325
  53.9 6.8 %collective-permute-start.12 = (f32[27,8,128]{2,1,0:T(8,128)S(1)}, f32[27,8,128]{2,1,0:T(8,128)S(1)}, u32[]{:S(2)}, u32[]{:S(2)}) collective-permute-start(f32[27,8,128]{2,1,0:T(8,128)S(1)} %get-tuple-element.58), channel_id=1, source_target_pairs={{0,18},{1,19},{2,16},{3,17},{4,22},{5,23},{6,20},{7,21},{8,26},{9,... | collective-permute-start | bytes 331784 | tf_op jit(solution)/shard_map/ppermute | solution.py:325
  54.9 6.0 %collective-permute-start.11 = (f32[27,8,128]{2,1,0:T(8,128)S(1)}, f32[27,8,128]{2,1,0:T(8,128)S(1)}, u32[]{:S(2)}, u32[]{:S(2)}) collective-permute-start(f32[27,8,128]{2,1,0:T(8,128)S(1)} %get-tuple-element.59), channel_id=1, source_target_pairs={{0,16},{1,17},{2,18},{3,19},{4,20},{5,21},{6,22},{7,23},{8,24},{9,... | collective-permute-start | bytes 331784 | tf_op jit(solution)/shard_map/ppermute | solution.py:325
  61.0 7.2 %collective-permute-start.16 = (f32[18,8,128]{2,1,0:T(8,128)S(1)}, f32[18,8,128]{2,1,0:T(8,128)S(1)}, u32[]{:S(2)}, u32[]{:S(2)}) collective-permute-start(f32[18,8,128]{2,1,0:T(8,128)S(1)} %slice.39), channel_id=1, source_target_pairs={{0,12},{1,13},{2,14},{3,15},{4,0},{5,1},{6,2},{7,3},{8,4},{9,5},{1... | collective-permute-start | bytes 221192 | tf_op jit(solution)/shard_map/ppermute | solution.py:325
  63.5 6.7 %collective-permute-start.15 = (f32[18,8,128]{2,1,0:T(8,128)S(1)}, f32[18,8,128]{2,1,0:T(8,128)S(1)}, u32[]{:S(2)}, u32[]{:S(2)}) collective-permute-start(f32[18,8,128]{2,1,0:T(8,128)S(1)} %slice.39), channel_id=1, source_target_pairs={{0,8},{1,9},{2,10},{3,11},{4,12},{5,13},{6,14},{7,15},{8,0},{9,1},... | collective-permute-start | bytes 221192 | tf_op jit(solution)/shard_map/ppermute | solution.py:325
  63.5 6.7 %collective-permute-start.14 = (f32[18,8,128]{2,1,0:T(8,128)S(1)}, f32[18,8,128]{2,1,0:T(8,128)S(1)}, u32[]{:S(2)}, u32[]{:S(2)}) collective-permute-start(f32[18,8,128]{2,1,0:T(8,128)S(1)} %slice.39), channel_id=1, source_target_pairs={{0,4},{1,5},{2,6},{3,7},{4,8},{5,9},{6,10},{7,11},{8,12},{9,13},{1... | collective-permute-start | bytes 221192 | tf_op jit(solution)/shard_map/ppermute | solution.py:325
  64.2 4.0 %collective-permute-start.13 = (f32[9,8,128]{2,1,0:T(8,128)S(1)}, f32[9,8,128]{2,1,0:T(8,128)S(1)}, u32[]{:S(2)}, u32[]{:S(2)}) collective-permute-start(f32[9,8,128]{2,1,0:T(8,128)S(1)} %slice.38), channel_id=1, source_target_pairs={{0,2},{1,3},{2,0},{3,1},{4,6},{5,7},{6,4},{7,5},{8,10},{9,11},{10,... | collective-permute-start | bytes 110600 | tf_op jit(solution)/shard_map/ppermute | solution.py:325
  70.3 9.6 %collective-permute-start.17 = (f32[4,18,8,128]{3,2,1,0:T(8,128)S(1)}, f32[4,18,8,128]{3,2,1,0:T(8,128)S(1)}, u32[]{:S(2)}, u32[]{:S(2)}) collective-permute-start(f32[4,18,8,128]{3,2,1,0:T(8,128)S(1)} %get-tuple-element.61), channel_id=1, source_target_pairs={{0,2},{1,3},{2,0},{3,1},{4,6},{5,7},{6,4},{7,5},{8,10},{9,11},{10,... | collective-permute-start | bytes 884744 | tf_op jit(solution)/shard_map/ppermute | solution.py:325
  71.6 7.0 %collective-permute-start.19 = (f32[2,9,8,128]{3,2,1,0:T(8,128)S(1)}, f32[2,9,8,128]{3,2,1,0:T(8,128)S(1)}, u32[]{:S(2)}, u32[]{:S(2)}) collective-permute-start(f32[2,9,8,128]{3,2,1,0:T(8,128)S(1)} %get-tuple-element.63), channel_id=1, source_target_pairs={{0,8},{1,9},{2,10},{3,11},{4,12},{5,13},{6,14},{7,15},{8,0},{9,1},... | collective-permute-start | bytes 221192 | tf_op jit(solution)/shard_map/ppermute | solution.py:325
  73.4 6.5 %collective-permute-start.18 = (f32[2,9,8,128]{3,2,1,0:T(8,128)S(1)}, f32[2,9,8,128]{3,2,1,0:T(8,128)S(1)}, u32[]{:S(2)}, u32[]{:S(2)}) collective-permute-start(f32[2,9,8,128]{3,2,1,0:T(8,128)S(1)} %get-tuple-element.63), channel_id=1, source_target_pairs={{0,4},{1,5},{2,6},{3,7},{4,8},{5,9},{6,10},{7,11},{8,12},{9,13},{1... | collective-permute-start | bytes 221192 | tf_op jit(solution)/shard_map/ppermute | solution.py:325
  74.0 5.8 %collective-permute-start.20 = (f32[2,9,8,128]{3,2,1,0:T(8,128)S(1)}, f32[2,9,8,128]{3,2,1,0:T(8,128)S(1)}, u32[]{:S(2)}, u32[]{:S(2)}) collective-permute-start(f32[2,9,8,128]{3,2,1,0:T(8,128)S(1)} %get-tuple-element.63), channel_id=1, source_target_pairs={{0,12},{1,13},{2,14},{3,15},{4,0},{5,1},{6,2},{7,3},{8,4},{9,5},{1... | collective-permute-start | bytes 221192 | tf_op jit(solution)/shard_map/ppermute | solution.py:325
  79.9 2.5 %collective-permute-start.21 = (f32[2,4,18,8,128]{4,3,2,1,0:T(8,128)S(1)}, f32[2,4,18,8,128]{4,3,2,1,0:T(8,128)S(1)}, u32[]{:S(2)}, u32[]{:S(2)}) collective-permute-start(f32[2,4,18,8,128]{4,3,2,1,0:T(8,128)S(1)} %pad_maximum_fusion.early_ref), channel_id=1, source_target_pairs={{0,1},{1,0},{2,3},{3,2},{4,5},{5,4},{6,7},{7,6},{8,9},{9,8},{10,11... | collective-permute-start | bytes 1769480 | tf_op jit(solution)/shard_map/ppermute | solution.py:325
  80.0 2.4 %collective-permute-start.22 = (f32[4,2,9,8,128]{4,3,2,1,0:T(8,128)S(1)}, f32[4,2,9,8,128]{4,3,2,1,0:T(8,128)S(1)}, u32[]{:S(2)}, u32[]{:S(2)}) collective-permute-start(f32[4,2,9,8,128]{4,3,2,1,0:T(8,128)S(1)} %pad_maximum_fusion.2.late_ref), channel_id=1, source_target_pairs={{0,1},{1,0},{2,3},{3,2},{4,5},{5,4},{6,7},{7,6},{8,9},{9,8},{10,11... | collective-permute-start | bytes 884744 | tf_op jit(solution)/shard_map/ppermute | solution.py:325

commit v4 on v3

--- a/solution.py
+++ b/solution.py
@@ -139,16 +139,15 @@
         copy.wait()
 
 
-def activations_kernel(
-    dims, block_ref, inner_ref, outer_ref, own_ref, *refs
-):
+def first_rows(z, height, per):
+    return jnp.clip(z * per, 1, height - 3)
+
+
+def first_kernel(dims, block_ref, own_ref, *refs):
     tm, own_frames, height, rows_all, columns, channels, factor = dims
-    came_refs, sent_refs = refs[:4], refs[4 : 4 + tm]
-    xh, xl, lh, ll, encoder, video, decoder, turned, ch, cl, hidden, grads = refs[4 + tm :]
+    came_refs, (encoder, decoder, turned, begun_high, begun_low, begun, xh, xl) = refs[:4], refs[4:]
     frames = tm * own_frames
     per = height // tm
-    cells = frames * columns
-    shape = (frames, columns, channels)
     segment, z, p = (lax.axis_index(name) for name in AXES)
     core = lax.rem(p, 2)
 
@@ -159,6 +158,32 @@
         block = jnp.where(segment == 0, came, own)
         put_taps(decoder, tap, block)
         put_taps(turned, tap, block.T)
+    for ref in (xh, xl, begun_high, begun_low):
+        ref[:, 0:2] = jnp.zeros((ref.shape[0], 2) + ref.shape[2:], bf16)
+    for k in range(tm):
+        for row in range(height):
+            at = (row, pl.ds(k * own_frames + 2, own_frames))
+            store_split(xh, xl, at, block_ref[k, :, row])
+    row = first_rows(z, height, per)
+    for i in range(2):
+        value = field_rows(xh, xl, row + i - 1, (frames, columns, channels), encoder)
+        begun[i] = value
+        store_latent(begun_high, begun_low, i, p * height + row + i, rows_all, value)
+
+
+def activations_kernel(
+    dims, block_ref, inner_ref, outer_ref, encoder, decoder, turned, begun_high, begun_low, begun, *refs
+):
+    tm, own_frames, height, rows_all, columns, channels, factor = dims
+    sent_refs = refs[:tm]
+    xh, xl, lh, ll, video, ch, cl, hidden, grads = refs[tm:]
+    frames = tm * own_frames
+    per = height // tm
+    cells = frames * columns
+    shape = (frames, columns, channels)
+    segment, z, p = (lax.axis_index(name) for name in AXES)
+    core = lax.rem(p, 2)
+
     for ref in (xh, xl, lh, ll):
         ref[:, 0:2] = jnp.zeros((ref.shape[0], 2) + ref.shape[2:], bf16)
     for ref in (ch, cl):
@@ -178,10 +203,16 @@
                 video[row + 1, pl.ds(first, own_frames)] = x
 
     start = z * per
-    for row in range(per + 4):
+    row_begun = first_rows(z, height, per)
+    skip = row_begun + 2 - start
+    for i in range(2):
+        lh[row_begun + 2 + i] = begun_high[i]
+        ll[row_begun + 2 + i] = begun_low[i]
+        hidden[skip + i] = begun[i]
+    for i in range(per + 2):
+        row = i + jnp.where(i >= skip, 2, 0)
         value = field_rows(xh, xl, start + row, shape, encoder)
-        if 2 <= row < per + 2:
-            hidden[row - 2] = value
+        hidden[row] = value
         store_latent(lh, ll, start + row, p * height + start + row - 2, rows_all, value)
 
     for j in range(per + 2):
@@ -197,7 +228,7 @@
     for j in range(per):
         places = [(j + 2 - b, 2 - a) for a in range(3) for b in range(3)]
         grad_latent = convolved(ch, cl, places, 1, shape, turned, flip=True)[0]
-        value = hidden[j]
+        value = hidden[j + 2]
         sigmoid = 1.0 / (1.0 + jnp.exp(-value))
         grad = grad_latent * (sigmoid * (1.0 + value * (1.0 - sigmoid)))
         grads[0, :, pl.ds(j * cells, cells)] = grad.reshape(cells, channels).T
@@ -383,25 +414,32 @@
         rows = height + 4
         products = 8 * 128 * channels * cells * 9
         shape = jax.ShapeDtypeStruct
-        *sent, xh, xl, lh, ll, encoder = call(
+        taken = shape((10 * channels, 6 * channels), bf16)
+        encoder, decoder, turned, *begun = call(
+            functools.partial(first_kernel, dims),
+            [taken] * 3 + [shape((2,) + field, bf16)] * 2 + [shape((2, frames, columns, channels), f32)],
+            [vmem((height,) + field, bf16)] * 2,
+            6,
+            0,
+            24,
+        )(block, own, mine, other, mine_late, other_late)
+
+        *sent, xh, xl, lh, ll = call(
             functools.partial(activations_kernel, dims),
             [shape((2, part, per * cells), f32)] * tm
             + [shape((height + 6,) + field, bf16)] * 2
-            + [shape((rows,) + field, bf16)] * 2
-            + [shape((10 * channels, 6 * channels), bf16)],
+            + [shape((rows,) + field, bf16)] * 2,
             [
                 vmem((height + 2, frames, columns, channels), f32),
-                vmem((10 * channels, 6 * channels), bf16),
-                vmem((10 * channels, 6 * channels), bf16),
                 vmem((per + 2,) + field, bf16),
                 vmem((per + 2,) + field, bf16),
-                vmem((per, frames, columns, channels), f32),
+                vmem((per + 4, frames, columns, channels), f32),
                 vmem((2, channels, per * cells), f32),
             ],
-            8,
-            3 * products * (3 * per + 6),
-            32,
-        )(block, inner, outer, own, mine, other, mine_late, other_late)
+            9,
+            3 * products * (3 * per + 4),
+            28,
+        )(block, inner, outer, encoder, decoder, turned, *begun)
 
         extra = height - 1 - per
         more_high, more_low = call(

time: 84.3 us -> 82.4 us (0.977)
  starting transfers between devices: 31.9 us -> 27.8 us
  waiting for transfers between devices: 19.4 us -> 21.2 us
    ppermute x23, starting transfers between devices: 31.9 us -> 27.8 us  [send(): return lax.ppermute(x, AXES, route)]
    pallas_call x0 -> x1, Pallas kernels: none -> 2.29 us  [local(): call(functools.partial(first_kernel, dims), [taken] * 3 + [shape((2,) + f...]
    pallas_call x1, Pallas kernels: 8.34 us -> 6.35 us  [local(): call(functools.partial(activations_kernel, dims), [shape((2, part, per *...]
    ppermute x23, waiting for transfers between devices: 19.4 us -> 21.2 us  [send(): return lax.ppermute(x, AXES, route)]
  transfers between devices with their start and end apart: 23 -> 23, of which waited for: 13 -> 12; matrix products, arithmetic and copies ran while one was open for 0% -> 0% of each run, Pallas kernels for 2% -> 5%
where the time goes in v4:
time: 82.4 us; the launch traced here: 82.2 us
  starting transfers between devices  27.8 us (34%)
  waiting for transfers between devices  21.2 us (26%)
  Pallas kernels  16.6 us (20%)
  blocking collectives  16.1 us (20%)
    ppermute x23, starting transfers between devices, send(): return lax.ppermute(x, AXES, route)  27.8 us
    ppermute x23, waiting for transfers between devices, send(): return lax.ppermute(x, AXES, route)  21.2 us
    all_gather x1, blocking collectives, local(): block = lax.all_gather(clip, 'tm')  16.1 us
    pallas_call x1, Pallas kernels, local(): call(functools.partial(activations_kernel, dims), [shape((2, part, per *...  6.35 us
    pallas_call x1, Pallas kernels, local(): call(functools.partial(first_kernel, dims), [taken] * 3 + [shape((2,) + f...  2.29 us
    pallas_call x1, Pallas kernels, local(): call(pick_kernel, [jax.ShapeDtypeStruct((third, channels), f32), jax.Shap...  2.26 us
    pallas_call x1, Pallas kernels, local(): call(functools.partial(weights_kernel, (tm, own_frames, height, rows_all,...  2.18 us
    pallas_call x1, Pallas kernels, local(): call(functools.partial(latents_kernel, dims), [shape((extra,) + field, bf...  1.76 us
  transfers between devices with their start and end apart: 23, of which 12 were waited for; matrix products, arithmetic and copies ran while one was open for 0% of the time, Pallas kernels for 5%

profile of v4, /device:TPU:0, one launch (start us, length us, event | category | flops | bytes accessed | tf_op | source)
XLA Modules:
  0.0 82.2 jit_solution(16387782119948242485)
XLA Ops:
  0.0 2.3 %shard_map.28 = (f32[1152,128]{1,0:T(8,128)}, f32[576,128]{1,0:T(8,128)}, f32[2,4,32,128]{3,2,1,0:T(8,128)}) custom-call(f32[2,2,4,32,128]{4,3,2,1,0:T(8,128)} %video_ref.1, f32[1,3456,128]{2,1,0:T(8,128)} %weights_ref.1), custom_call_target="tpu_custom_call" | custom-call | bytes 4000000 | tf_op jit(solution)/shard_map/pallas_call | solution.py:386
  2.3 3.0 %collective-permute-start.2 = (f32[1152,128]{1,0:T(8,128)}, f32[1152,128]{1,0:T(8,128)S(1)}, u32[]{:S(2)}, u32[]{:S(2)}) collective-permute-start(f32[1152,128]{1,0:T(8,128)} %get-tuple-element.36), channel_id=1, source_target_pairs={{0,16},{1,17},{2,18},{3,19},{4,20},{5,21},{6,22},{7,23},{8,24},{9,... | collective-permute-start | bytes 1769480 | tf_op jit(solution)/shard_map/ppermute | solution.py:356
  5.4 16.1 %all-gather = f32[8,4,32,128]{3,2,1,0:T(8,128)S(1)} all-gather(f32[2,4,32,128]{3,2,1,0:T(8,128)} %get-tuple-element.35), channel_id=2, replica_groups=mesh['segment'=2,'tm'=4,'space'=4] {'tm'}, dimensions={0}, use_global_device_ids=true | all-gather | bytes 655360 | tf_op jit(solution)/shard_map/all_gather | solution.py:401
  22.4 2.9 %collective-permute-start = (f32[4,2,3,32,128]{4,3,2,1,0:T(8,128)S(1)}, f32[4,2,3,32,128]{4,3,2,1,0:T(8,128)S(1)}, u32[]{:S(2)}, u32[]{:S(2)}) collective-permute-start(f32[4,2,3,32,128]{4,3,2,1,0:T(8,128)S(1)} %get-tuple-element.66), channel_id=1, source_target_pairs={{0,1},{1,0},{2,3},{3,2},{4,5},{5,4},{6,7},{7,6},{8,9},{9,8},{10,11... | collective-permute-start | bytes 1179656 | tf_op jit(solution)/shard_map/ppermute | solution.py:356
  25.4 1.7 %collective-permute-done.5.refs_3_ = f32[576,128]{1,0:T(8,128)S(1)} collective-permute-done((f32[576,128]{1,0:T(8,128)S(1)}, f32[576,128]{1,0:T(8,128)S(1)}, u32[]{:S(2)}, u32[]{:S(2)}) %collective-permute-start.5) | collective-permute-done | bytes 294944 | tf_op jit(solution)/shard_map/ppermute | solution.py:356
  27.1 2.3 %shard_map.29 = (bf16[1280,768]{1,0:T(8,128)(2,1)S(1)}, bf16[1280,768]{1,0:T(8,128)(2,1)S(1)}, bf16[1280,768]{1,0:T(8,128)(2,1)S(1)}, bf16[2,10,32,128]{3,2,1,0:...) custom-call(f32[4,2,4,32,128]{4,3,2,1,0:T(8,128)S(1)} %bitcast.33, ...), custom_call_target="tpu_custom_call" | custom-call | bytes 4000000 | tf_op jit(solution)/shard_map/pallas_call | solution.py:418
  29.4 6.3 %shard_map.30 = (f32[2,32,256]{2,1,0:T(8,128)S(1)}, f32[2,32,256]{2,1,0:T(8,128)S(1)}, f32[2,32,256]{2,1,0:T(8,128)S(1)}, f32[2,32,256]{2,1,0:T(8,128)S(1)}, bf1...) custom-call(f32[4,2,4,32,128]{4,3,2,1,0:T(8,128)S(1)} %bitcast.34, ...), custom_call_target="tpu_custom_call" | custom-call | flops 6341787648 | bytes 4000000 | tf_op jit(solution)/shard_map/pallas_call | solution.py:427
  35.7 2.2 %collective-permute-start.6 = (f32[2,32,256]{2,1,0:T(8,128)S(1)}, f32[2,32,256]{2,1,0:T(8,128)S(1)}, u32[]{:S(2)}, u32[]{:S(2)}) collective-permute-start(f32[2,32,256]{2,1,0:T(8,128)S(1)} %get-tuple-element.46), channel_id=1, source_target_pairs={{0,4},{1,5},{2,6},{3,7},{4,8},{5,9},{6,10},{7,11},{8,12},{9,13},{1... | collective-permute-start | bytes 196616 | tf_op jit(solution)/shard_map/ppermute | solution.py:356
  37.9 2.5 %collective-permute-start.7 = (f32[2,32,256]{2,1,0:T(8,128)S(1)}, f32[2,32,256]{2,1,0:T(8,128)S(1)}, u32[]{:S(2)}, u32[]{:S(2)}) collective-permute-start(f32[2,32,256]{2,1,0:T(8,128)S(1)} %get-tuple-element.47), channel_id=1, source_target_pairs={{0,8},{1,9},{2,10},{3,11},{4,12},{5,13},{6,14},{7,15},{8,0},{9,1},... | collective-permute-start | bytes 196616 | tf_op jit(solution)/shard_map/ppermute | solution.py:356
  41.2 1.8 %shard_map.31 = (bf16[2,10,32,128]{3,2,1,0:T(8,128)(2,1)S(1)}, bf16[2,10,32,128]{3,2,1,0:T(8,128)(2,1)S(1)}) custom-call(bf16[10,10,32,128]{3,2,1,0:T(8,128)(2,1)S(1)} %get-tuple-element.49.xh.refs_4_, bf16[10,10,32,128]{3,2,1,0:T(8,128)(2,1)S(1)} %get-tuple-element.50.xl.refs_5_, bf16[1280,768]{1,0:T(8,128)(2,1)S(1)} %get-tuple-element.39.encoder), custom_call_target="tpu_custom_call" | custom-call | flops 1811939328 | bytes 4000000 | tf_op jit(solution)/shard_map/pallas_call | solution.py:445
  43.0 2.7 %collective-permute-done.7.refs_2_ = f32[2,32,256]{2,1,0:T(8,128)S(1)} collective-permute-done((f32[2,32,256]{2,1,0:T(8,128)S(1)}, f32[2,32,256]{2,1,0:T(8,128)S(1)}, u32[]{:S(2)}, u32[]{:S(2)}) %collective-permute-start.7) | collective-permute-done | bytes 65568 | tf_op jit(solution)/shard_map/ppermute | solution.py:356
  46.2 2.2 %shard_map.32 = (f32[2,2,27,8,128]{4,3,2,1,0:T(8,128)S(1)}, f32[2,2,27,8,128]{4,3,2,1,0:T(8,128)S(1)}) custom-call(f32[2,32,256]{2,1,0:T(8,128)S(1)} %get-tuple-element.45.refs_0_, f32[2,32,256]{2,1,0:T(8,128)S(1)} %collective-permute-done.6.refs_1_, f32[2,32,256]{2,1,0:T(8,128)S(1)} %collective-permute-done.7.refs_2_, ...), custom_call_target="tpu_custom_call" | custom-call | flops 1811939328 | bytes 4000000 | tf_op jit(solution)/shard_map/pallas_call | solution.py:456
  48.6 1.6 %collective-permute-done.9 = f32[2,2,27,8,128]{4,3,2,1,0:T(8,128)S(1)} collective-permute-done((f32[2,2,27,8,128]{4,3,2,1,0:T(8,128)S(1)}, f32[2,2,27,8,128]{4,3,2,1,0:T(8,128)S(1)}, u32[]{:S(2)}, u32[]{:S(2)}) %collective-permute-start.9) | collective-permute-done | bytes 442400 | tf_op jit(solution)/shard_map/ppermute | solution.py:356
  50.3 1.5 %collective-permute-start.10 = (f32[27,8,128]{2,1,0:T(8,128)S(1)}, f32[27,8,128]{2,1,0:T(8,128)S(1)}, u32[]{:S(2)}, u32[]{:S(2)}) collective-permute-start(f32[27,8,128]{2,1,0:T(8,128)S(1)} %get-tuple-element.67), channel_id=1, source_target_pairs={{0,2},{1,3},{2,0},{3,1},{4,6},{5,7},{6,4},{7,5},{8,10},{9,11},{10,... | collective-permute-start | bytes 331784 | tf_op jit(solution)/shard_map/ppermute | solution.py:356
  53.9 3.2 %collective-permute-done.10 = f32[27,8,128]{2,1,0:T(8,128)S(1)} collective-permute-done((f32[27,8,128]{2,1,0:T(8,128)S(1)}, f32[27,8,128]{2,1,0:T(8,128)S(1)}, u32[]{:S(2)}, u32[]{:S(2)}) %collective-permute-start.10) | collective-permute-done | bytes 110624 | tf_op jit(solution)/shard_map/ppermute | solution.py:356
  57.1 1.6 %collective-permute-done.12 = f32[27,8,128]{2,1,0:T(8,128)S(1)} collective-permute-done((f32[27,8,128]{2,1,0:T(8,128)S(1)}, f32[27,8,128]{2,1,0:T(8,128)S(1)}, u32[]{:S(2)}, u32[]{:S(2)}) %collective-permute-start.12) | collective-permute-done | bytes 110624 | tf_op jit(solution)/shard_map/ppermute | solution.py:356
  59.2 2.4 %collective-permute-start.16 = (f32[18,8,128]{2,1,0:T(8,128)S(1)}, f32[18,8,128]{2,1,0:T(8,128)S(1)}, u32[]{:S(2)}, u32[]{:S(2)}) collective-permute-start(f32[18,8,128]{2,1,0:T(8,128)S(1)} %slice.39), channel_id=1, source_target_pairs={{0,12},{1,13},{2,14},{3,15},{4,0},{5,1},{6,2},{7,3},{8,4},{9,5},{1... | collective-permute-start | bytes 221192 | tf_op jit(solution)/shard_map/ppermute | solution.py:356
  62.2 1.6 %collective-permute-start.13 = (f32[9,8,128]{2,1,0:T(8,128)S(1)}, f32[9,8,128]{2,1,0:T(8,128)S(1)}, u32[]{:S(2)}, u32[]{:S(2)}) collective-permute-start(f32[9,8,128]{2,1,0:T(8,128)S(1)} %slice.38), channel_id=1, source_target_pairs={{0,2},{1,3},{2,0},{3,1},{4,6},{5,7},{6,4},{7,5},{8,10},{9,11},{10,... | collective-permute-start | bytes 110600 | tf_op jit(solution)/shard_map/ppermute | solution.py:356
  63.8 2.4 %collective-permute-done.13 = f32[9,8,128]{2,1,0:T(8,128)S(1)} collective-permute-done((f32[9,8,128]{2,1,0:T(8,128)S(1)}, f32[9,8,128]{2,1,0:T(8,128)S(1)}, u32[]{:S(2)}, u32[]{:S(2)}) %collective-permute-start.13) | collective-permute-done | bytes 36896 | tf_op jit(solution)/shard_map/ppermute | solution.py:356
  66.2 2.6 %collective-permute-done.15 = f32[18,8,128]{2,1,0:T(8,128)S(1)} collective-permute-done((f32[18,8,128]{2,1,0:T(8,128)S(1)}, f32[18,8,128]{2,1,0:T(8,128)S(1)}, u32[]{:S(2)}, u32[]{:S(2)}) %collective-permute-start.15) | collective-permute-done | bytes 73760 | tf_op jit(solution)/shard_map/ppermute | solution.py:356
  69.7 1.7 %collective-permute-start.19 = (f32[2,9,8,128]{3,2,1,0:T(8,128)S(1)}, f32[2,9,8,128]{3,2,1,0:T(8,128)S(1)}, u32[]{:S(2)}, u32[]{:S(2)}) collective-permute-start(f32[2,9,8,128]{3,2,1,0:T(8,128)S(1)} %get-tuple-element.73), channel_id=1, source_target_pairs={{0,8},{1,9},{2,10},{3,11},{4,12},{5,13},{6,14},{7,15},{8,0},{9,1},... | collective-permute-start | bytes 221192 | tf_op jit(solution)/shard_map/ppermute | solution.py:356
  72.1 3.2 %collective-permute-start.20 = (f32[2,9,8,128]{3,2,1,0:T(8,128)S(1)}, f32[2,9,8,128]{3,2,1,0:T(8,128)S(1)}, u32[]{:S(2)}, u32[]{:S(2)}) collective-permute-start(f32[2,9,8,128]{3,2,1,0:T(8,128)S(1)} %get-tuple-element.73), channel_id=1, source_target_pairs={{0,12},{1,13},{2,14},{3,15},{4,0},{5,1},{6,2},{7,3},{8,4},{9,5},{1... | collective-permute-start | bytes 221192 | tf_op jit(solution)/shard_map/ppermute | solution.py:356
  78.6 1.9 %collective-permute-done.22.came_late_ref = f32[4,2,9,8,128]{4,3,2,1,0:T(8,128)S(1)} collective-permute-done((f32[4,2,9,8,128]{4,3,2,1,0:T(8,128)S(1)}, f32[4,2,9,8,128]{4,3,2,1,0:T(8,128)S(1)}, u32[]{:S(2)}, u32[]{:S(2)}) %collective-permute-start.22) | collective-permute-done | bytes 294944 | tf_op jit(solution)/shard_map/ppermute | solution.py:356
  80.5 1.8 %shard_map.33 = f32[3456,128]{1,0:T(8,128)} custom-call(f32[2,4,18,8,128]{4,3,2,1,0:T(8,128)S(1)} %pad_maximum_fusion.early_ref, f32[4,2,9,8,128]{4,3,2,1,0:T(8,128)S(1)} %pad_maximum_fusion.2.late_ref, f32[2,4,18,8,128]{4,3,2,1,0:T(8,128)S(1)} %collective-permute-done.21.came_early_ref, f32[4,2,9,8,128]{4,3,2,1,0:T(8,128)S(1)} %collective-permute-done.22.came_late_ref), custom_call_target="tpu_custom_call" | custom-call | bytes 4000000 | tf_op jit(solution)/shard_map/pallas_call | solution.py:484
  (41 shorter events, 10.6 us)
Async XLA Ops:
  0.0 27.1 %copy-start = (f32[1,3456,128]{2,1,0:T(8,128)S(1)}, f32[1,3456,128]{2,1,0:T(8,128)}, u32[]{:S(2)}) copy-start(f32[1,3456,128]{2,1,0:T(8,128)} %weights_ref.1) | copy-start | bytes 5308420
  2.3 19.3 %collective-permute-start.2 = (f32[1152,128]{1,0:T(8,128)}, f32[1152,128]{1,0:T(8,128)S(1)}, u32[]{:S(2)}, u32[]{:S(2)}) collective-permute-start(f32[1152,128]{1,0:T(8,128)} %get-tuple-element.36), channel_id=1, source_target_pairs={{0,16},{1,17},{2,18},{3,19},{4,20},{5,21},{6,22},{7,23},{8,24},{9,... | collective-permute-start | bytes 1769480 | tf_op jit(solution)/shard_map/ppermute | solution.py:356
  5.3 20.0 %collective-permute-start.4 = (f32[576,128]{1,0:T(8,128)}, f32[576,128]{1,0:T(8,128)S(1)}, u32[]{:S(2)}, u32[]{:S(2)}) collective-permute-start(f32[576,128]{1,0:T(8,128)} %get-tuple-element.38), channel_id=1, source_target_pairs={{0,16},{1,17},{2,18},{3,19},{4,20},{5,21},{6,22},{7,23},{8,24},{9,... | collective-permute-start | bytes 884744 | tf_op jit(solution)/shard_map/ppermute | solution.py:356
  21.6 5.5 %collective-permute-start.3 = (f32[1152,128]{1,0:T(8,128)S(1)}, f32[1152,128]{1,0:T(8,128)S(1)}, u32[]{:S(2)}, u32[]{:S(2)}) collective-permute-start(f32[1152,128]{1,0:T(8,128)S(1)} %collective-permute-done.2.refs_0_), channel_id=1, source_target_pairs={{0,1},{1,0},{2,3},{3,2},{4,5},{5,4},{6,7},{7,6},{8,9},{9,8},{10,11... | collective-permute-start | bytes 1769480 | tf_op jit(solution)/shard_map/ppermute | solution.py:356
  21.7 7.7 %collective-permute-start.1 = (f32[4,2,3,32,128]{4,3,2,1,0:T(8,128)S(1)}, f32[4,2,3,32,128]{4,3,2,1,0:T(8,128)S(1)}, u32[]{:S(2)}, u32[]{:S(2)}) collective-permute-start(f32[4,2,3,32,128]{4,3,2,1,0:T(8,128)S(1)} %get-tuple-element.65), channel_id=1, source_target_pairs={{1,2},{2,1},{5,6},{6,5},{9,10},{10,9},{13,14},{14,13},{17,18},{18,... | collective-permute-start | bytes 1179656 | tf_op jit(solution)/shard_map/ppermute | solution.py:356
  22.4 7.0 %collective-permute-start = (f32[4,2,3,32,128]{4,3,2,1,0:T(8,128)S(1)}, f32[4,2,3,32,128]{4,3,2,1,0:T(8,128)S(1)}, u32[]{:S(2)}, u32[]{:S(2)}) collective-permute-start(f32[4,2,3,32,128]{4,3,2,1,0:T(8,128)S(1)} %get-tuple-element.66), channel_id=1, source_target_pairs={{0,1},{1,0},{2,3},{3,2},{4,5},{5,4},{6,7},{7,6},{8,9},{9,8},{10,11... | collective-permute-start | bytes 1179656 | tf_op jit(solution)/shard_map/ppermute | solution.py:356
  25.3 1.8 %collective-permute-start.5 = (f32[576,128]{1,0:T(8,128)S(1)}, f32[576,128]{1,0:T(8,128)S(1)}, u32[]{:S(2)}, u32[]{:S(2)}) collective-permute-start(f32[576,128]{1,0:T(8,128)S(1)} %collective-permute-done.4.refs_2_), channel_id=1, source_target_pairs={{0,1},{1,0},{2,3},{3,2},{4,5},{5,4},{6,7},{7,6},{8,9},{9,8},{10,11... | collective-permute-start | bytes 884744 | tf_op jit(solution)/shard_map/ppermute | solution.py:356
  35.7 7.3 %collective-permute-start.6 = (f32[2,32,256]{2,1,0:T(8,128)S(1)}, f32[2,32,256]{2,1,0:T(8,128)S(1)}, u32[]{:S(2)}, u32[]{:S(2)}) collective-permute-start(f32[2,32,256]{2,1,0:T(8,128)S(1)} %get-tuple-element.46), channel_id=1, source_target_pairs={{0,4},{1,5},{2,6},{3,7},{4,8},{5,9},{6,10},{7,11},{8,12},{9,13},{1... | collective-permute-start | bytes 196616 | tf_op jit(solution)/shard_map/ppermute | solution.py:356
  37.9 7.7 %collective-permute-start.7 = (f32[2,32,256]{2,1,0:T(8,128)S(1)}, f32[2,32,256]{2,1,0:T(8,128)S(1)}, u32[]{:S(2)}, u32[]{:S(2)}) collective-permute-start(f32[2,32,256]{2,1,0:T(8,128)S(1)} %get-tuple-element.47), channel_id=1, source_target_pairs={{0,8},{1,9},{2,10},{3,11},{4,12},{5,13},{6,14},{7,15},{8,0},{9,1},... | collective-permute-start | bytes 196616 | tf_op jit(solution)/shard_map/ppermute | solution.py:356
  40.5 5.7 %collective-permute-start.8 = (f32[2,32,256]{2,1,0:T(8,128)S(1)}, f32[2,32,256]{2,1,0:T(8,128)S(1)}, u32[]{:S(2)}, u32[]{:S(2)}) collective-permute-start(f32[2,32,256]{2,1,0:T(8,128)S(1)} %get-tuple-element.48), channel_id=1, source_target_pairs={{0,12},{1,13},{2,14},{3,15},{4,0},{5,1},{6,2},{7,3},{8,4},{9,5},{1... | collective-permute-start | bytes 196616 | tf_op jit(solution)/shard_map/ppermute | solution.py:356
  48.4 1.9 %collective-permute-start.9 = (f32[2,2,27,8,128]{4,3,2,1,0:T(8,128)S(1)}, f32[2,2,27,8,128]{4,3,2,1,0:T(8,128)S(1)}, u32[]{:S(2)}, u32[]{:S(2)}) collective-permute-start(f32[2,2,27,8,128]{4,3,2,1,0:T(8,128)S(1)} %get-tuple-element.56), channel_id=1, source_target_pairs={{0,1},{1,0},{2,3},{3,2},{4,5},{5,4},{6,7},{7,6},{8,9},{9,8},{10,11... | collective-permute-start | bytes 1327112 | tf_op jit(solution)/shard_map/ppermute | solution.py:356
  50.3 6.7 %collective-permute-start.10 = (f32[27,8,128]{2,1,0:T(8,128)S(1)}, f32[27,8,128]{2,1,0:T(8,128)S(1)}, u32[]{:S(2)}, u32[]{:S(2)}) collective-permute-start(f32[27,8,128]{2,1,0:T(8,128)S(1)} %get-tuple-element.67), channel_id=1, source_target_pairs={{0,2},{1,3},{2,0},{3,1},{4,6},{5,7},{6,4},{7,5},{8,10},{9,11},{10,... | collective-permute-start | bytes 331784 | tf_op jit(solution)/shard_map/ppermute | solution.py:356
  51.9 6.8 %collective-permute-start.12 = (f32[27,8,128]{2,1,0:T(8,128)S(1)}, f32[27,8,128]{2,1,0:T(8,128)S(1)}, u32[]{:S(2)}, u32[]{:S(2)}) collective-permute-start(f32[27,8,128]{2,1,0:T(8,128)S(1)} %get-tuple-element.68), channel_id=1, source_target_pairs={{0,18},{1,19},{2,16},{3,17},{4,22},{5,23},{6,20},{7,21},{8,26},{9,... | collective-permute-start | bytes 331784 | tf_op jit(solution)/shard_map/ppermute | solution.py:356
  53.4 5.8 %collective-permute-start.11 = (f32[27,8,128]{2,1,0:T(8,128)S(1)}, f32[27,8,128]{2,1,0:T(8,128)S(1)}, u32[]{:S(2)}, u32[]{:S(2)}) collective-permute-start(f32[27,8,128]{2,1,0:T(8,128)S(1)} %get-tuple-element.69), channel_id=1, source_target_pairs={{0,16},{1,17},{2,18},{3,19},{4,20},{5,21},{6,22},{7,23},{8,24},{9,... | collective-permute-start | bytes 331784 | tf_op jit(solution)/shard_map/ppermute | solution.py:356
  59.2 7.0 %collective-permute-start.16 = (f32[18,8,128]{2,1,0:T(8,128)S(1)}, f32[18,8,128]{2,1,0:T(8,128)S(1)}, u32[]{:S(2)}, u32[]{:S(2)}) collective-permute-start(f32[18,8,128]{2,1,0:T(8,128)S(1)} %slice.39), channel_id=1, source_target_pairs={{0,12},{1,13},{2,14},{3,15},{4,0},{5,1},{6,2},{7,3},{8,4},{9,5},{1... | collective-permute-start | bytes 221192 | tf_op jit(solution)/shard_map/ppermute | solution.py:356
  61.6 7.2 %collective-permute-start.15 = (f32[18,8,128]{2,1,0:T(8,128)S(1)}, f32[18,8,128]{2,1,0:T(8,128)S(1)}, u32[]{:S(2)}, u32[]{:S(2)}) collective-permute-start(f32[18,8,128]{2,1,0:T(8,128)S(1)} %slice.39), channel_id=1, source_target_pairs={{0,8},{1,9},{2,10},{3,11},{4,12},{5,13},{6,14},{7,15},{8,0},{9,1},... | collective-permute-start | bytes 221192 | tf_op jit(solution)/shard_map/ppermute | solution.py:356
  62.0 6.7 %collective-permute-start.14 = (f32[18,8,128]{2,1,0:T(8,128)S(1)}, f32[18,8,128]{2,1,0:T(8,128)S(1)}, u32[]{:S(2)}, u32[]{:S(2)}) collective-permute-start(f32[18,8,128]{2,1,0:T(8,128)S(1)} %slice.39), channel_id=1, source_target_pairs={{0,4},{1,5},{2,6},{3,7},{4,8},{5,9},{6,10},{7,11},{8,12},{9,13},{1... | collective-permute-start | bytes 221192 | tf_op jit(solution)/shard_map/ppermute | solution.py:356
  62.2 4.0 %collective-permute-start.13 = (f32[9,8,128]{2,1,0:T(8,128)S(1)}, f32[9,8,128]{2,1,0:T(8,128)S(1)}, u32[]{:S(2)}, u32[]{:S(2)}) collective-permute-start(f32[9,8,128]{2,1,0:T(8,128)S(1)} %slice.38), channel_id=1, source_target_pairs={{0,2},{1,3},{2,0},{3,1},{4,6},{5,7},{6,4},{7,5},{8,10},{9,11},{10,... | collective-permute-start | bytes 110600 | tf_op jit(solution)/shard_map/ppermute | solution.py:356
  68.8 9.2 %collective-permute-start.17 = (f32[4,18,8,128]{3,2,1,0:T(8,128)S(1)}, f32[4,18,8,128]{3,2,1,0:T(8,128)S(1)}, u32[]{:S(2)}, u32[]{:S(2)}) collective-permute-start(f32[4,18,8,128]{3,2,1,0:T(8,128)S(1)} %get-tuple-element.71), channel_id=1, source_target_pairs={{0,2},{1,3},{2,0},{3,1},{4,6},{5,7},{6,4},{7,5},{8,10},{9,11},{10,... | collective-permute-start | bytes 884744 | tf_op jit(solution)/shard_map/ppermute | solution.py:356
  69.7 7.0 %collective-permute-start.19 = (f32[2,9,8,128]{3,2,1,0:T(8,128)S(1)}, f32[2,9,8,128]{3,2,1,0:T(8,128)S(1)}, u32[]{:S(2)}, u32[]{:S(2)}) collective-permute-start(f32[2,9,8,128]{3,2,1,0:T(8,128)S(1)} %get-tuple-element.73), channel_id=1, source_target_pairs={{0,8},{1,9},{2,10},{3,11},{4,12},{5,13},{6,14},{7,15},{8,0},{9,1},... | collective-permute-start | bytes 221192 | tf_op jit(solution)/shard_map/ppermute | solution.py:356
  71.4 6.5 %collective-permute-start.18 = (f32[2,9,8,128]{3,2,1,0:T(8,128)S(1)}, f32[2,9,8,128]{3,2,1,0:T(8,128)S(1)}, u32[]{:S(2)}, u32[]{:S(2)}) collective-permute-start(f32[2,9,8,128]{3,2,1,0:T(8,128)S(1)} %get-tuple-element.73), channel_id=1, source_target_pairs={{0,4},{1,5},{2,6},{3,7},{4,8},{5,9},{6,10},{7,11},{8,12},{9,13},{1... | collective-permute-start | bytes 221192 | tf_op jit(solution)/shard_map/ppermute | solution.py:356
  72.1 5.9 %collective-permute-start.20 = (f32[2,9,8,128]{3,2,1,0:T(8,128)S(1)}, f32[2,9,8,128]{3,2,1,0:T(8,128)S(1)}, u32[]{:S(2)}, u32[]{:S(2)}) collective-permute-start(f32[2,9,8,128]{3,2,1,0:T(8,128)S(1)} %get-tuple-element.73), channel_id=1, source_target_pairs={{0,12},{1,13},{2,14},{3,15},{4,0},{5,1},{6,2},{7,3},{8,4},{9,5},{1... | collective-permute-start | bytes 221192 | tf_op jit(solution)/shard_map/ppermute | solution.py:356
  78.0 2.5 %collective-permute-start.21 = (f32[2,4,18,8,128]{4,3,2,1,0:T(8,128)S(1)}, f32[2,4,18,8,128]{4,3,2,1,0:T(8,128)S(1)}, u32[]{:S(2)}, u32[]{:S(2)}) collective-permute-start(f32[2,4,18,8,128]{4,3,2,1,0:T(8,128)S(1)} %pad_maximum_fusion.early_ref), channel_id=1, source_target_pairs={{0,1},{1,0},{2,3},{3,2},{4,5},{5,4},{6,7},{7,6},{8,9},{9,8},{10,11... | collective-permute-start | bytes 1769480 | tf_op jit(solution)/shard_map/ppermute | solution.py:356
  78.1 2.4 %collective-permute-start.22 = (f32[4,2,9,8,128]{4,3,2,1,0:T(8,128)S(1)}, f32[4,2,9,8,128]{4,3,2,1,0:T(8,128)S(1)}, u32[]{:S(2)}, u32[]{:S(2)}) collective-permute-start(f32[4,2,9,8,128]{4,3,2,1,0:T(8,128)S(1)} %pad_maximum_fusion.2.late_ref), channel_id=1, source_target_pairs={{0,1},{1,0},{2,3},{3,2},{4,5},{5,4},{6,7},{7,6},{8,9},{9,8},{10,11... | collective-permute-start | bytes 884744 | tf_op jit(solution)/shard_map/ppermute | solution.py:356

commit v5 on v4

--- a/solution.py
+++ b/solution.py
@@ -475,7 +475,6 @@
         early, late = total[:cut], total[cut:]
         late_rows = [late] + [send(late, across(0, k)) for k in range(1, pairs)]
         early_all = [early] + [send(early, later(k)) for k in range(1, tm)]
-        late_rows, early_all = lax.optimization_barrier((late_rows, early_all))
         late_rows, early_all = jnp.stack(late_rows), jnp.stack(early_all)
         early_all = jnp.stack([early_all] + [send(early_all, across(0, k)) for k in range(1, pairs)])
         late_all = jnp.stack([late_rows] + [send(late_rows, later(k)) for k in range(1, tm)])

time: 82.4 us -> 81.7 us (level)
  waiting for transfers between devices: 21.2 us -> 19.6 us
  starting transfers between devices: 27.8 us -> 28.7 us
    ppermute x23, waiting for transfers between devices: 21.2 us -> 19.6 us  [send(): return lax.ppermute(x, AXES, route)]
    ppermute x23, starting transfers between devices: 27.8 us -> 28.7 us  [send(): return lax.ppermute(x, AXES, route)]
where the time goes in v5:
time: 81.7 us; the launch traced here: 81.6 us
  starting transfers between devices  28.7 us (35%)
  waiting for transfers between devices  19.6 us (24%)
  Pallas kernels  16.6 us (20%)
  blocking collectives  16.1 us (20%)
    ppermute x23, starting transfers between devices, send(): return lax.ppermute(x, AXES, route)  28.7 us
    ppermute x23, waiting for transfers between devices, send(): return lax.ppermute(x, AXES, route)  19.6 us
    all_gather x1, blocking collectives, local(): block = lax.all_gather(clip, 'tm')  16.1 us
    pallas_call x1, Pallas kernels, local(): call(functools.partial(activations_kernel, dims), [shape((2, part, per *...  6.35 us
    pallas_call x1, Pallas kernels, local(): call(functools.partial(first_kernel, dims), [taken] * 3 + [shape((2,) + f...  2.29 us
    pallas_call x1, Pallas kernels, local(): call(pick_kernel, [jax.ShapeDtypeStruct((third, channels), f32), jax.Shap...  2.27 us
    pallas_call x1, Pallas kernels, local(): call(functools.partial(weights_kernel, (tm, own_frames, height, rows_all,...  2.19 us
    pallas_call x1, Pallas kernels, local(): call(functools.partial(latents_kernel, dims), [shape((extra,) + field, bf...  1.76 us
  transfers between devices with their start and end apart: 23, of which 12 were waited for; matrix products, arithmetic and copies ran while one was open for 0% of the time, Pallas kernels for 5%

profile of v5, /device:TPU:0, one launch (start us, length us, event | category | flops | bytes accessed | tf_op | source)
XLA Modules:
  0.0 81.6 jit_solution(18260680835115253727)
XLA Ops:
  0.0 2.3 %shard_map.28 = (f32[1152,128]{1,0:T(8,128)}, f32[576,128]{1,0:T(8,128)}, f32[2,4,32,128]{3,2,1,0:T(8,128)}) custom-call(f32[2,2,4,32,128]{4,3,2,1,0:T(8,128)} %video_ref.1, f32[1,3456,128]{2,1,0:T(8,128)} %weights_ref.1), custom_call_target="tpu_custom_call" | custom-call | bytes 4000000 | tf_op jit(solution)/shard_map/pallas_call | solution.py:386
  2.3 3.0 %collective-permute-start.2 = (f32[1152,128]{1,0:T(8,128)}, f32[1152,128]{1,0:T(8,128)S(1)}, u32[]{:S(2)}, u32[]{:S(2)}) collective-permute-start(f32[1152,128]{1,0:T(8,128)} %get-tuple-element.30), channel_id=1, source_target_pairs={{0,16},{1,17},{2,18},{3,19},{4,20},{5,21},{6,22},{7,23},{8,24},{9,... | collective-permute-start | bytes 1769480 | tf_op jit(solution)/shard_map/ppermute | solution.py:356
  5.4 16.1 %all-gather = f32[8,4,32,128]{3,2,1,0:T(8,128)S(1)} all-gather(f32[2,4,32,128]{3,2,1,0:T(8,128)} %get-tuple-element.29), channel_id=2, replica_groups=mesh['segment'=2,'tm'=4,'space'=4] {'tm'}, dimensions={0}, use_global_device_ids=true | all-gather | bytes 655360 | tf_op jit(solution)/shard_map/all_gather | solution.py:401
  22.4 2.9 %collective-permute-start = (f32[4,2,3,32,128]{4,3,2,1,0:T(8,128)S(1)}, f32[4,2,3,32,128]{4,3,2,1,0:T(8,128)S(1)}, u32[]{:S(2)}, u32[]{:S(2)}) collective-permute-start(f32[4,2,3,32,128]{4,3,2,1,0:T(8,128)S(1)} %get-tuple-element.54), channel_id=1, source_target_pairs={{0,1},{1,0},{2,3},{3,2},{4,5},{5,4},{6,7},{7,6},{8,9},{9,8},{10,11... | collective-permute-start | bytes 1179656 | tf_op jit(solution)/shard_map/ppermute | solution.py:356
  25.4 1.7 %collective-permute-done.5.refs_3_ = f32[576,128]{1,0:T(8,128)S(1)} collective-permute-done((f32[576,128]{1,0:T(8,128)S(1)}, f32[576,128]{1,0:T(8,128)S(1)}, u32[]{:S(2)}, u32[]{:S(2)}) %collective-permute-start.5) | collective-permute-done | bytes 294944 | tf_op jit(solution)/shard_map/ppermute | solution.py:356
  27.1 2.3 %shard_map.29 = (bf16[1280,768]{1,0:T(8,128)(2,1)S(1)}, bf16[1280,768]{1,0:T(8,128)(2,1)S(1)}, bf16[1280,768]{1,0:T(8,128)(2,1)S(1)}, bf16[2,10,32,128]{3,2,1,0:...) custom-call(f32[4,2,4,32,128]{4,3,2,1,0:T(8,128)S(1)} %bitcast.35, ...), custom_call_target="tpu_custom_call" | custom-call | bytes 4000000 | tf_op jit(solution)/shard_map/pallas_call | solution.py:418
  29.4 6.4 %shard_map.30 = (f32[2,32,256]{2,1,0:T(8,128)S(1)}, f32[2,32,256]{2,1,0:T(8,128)S(1)}, f32[2,32,256]{2,1,0:T(8,128)S(1)}, f32[2,32,256]{2,1,0:T(8,128)S(1)}, bf1...) custom-call(f32[4,2,4,32,128]{4,3,2,1,0:T(8,128)S(1)} %bitcast.36, ...), custom_call_target="tpu_custom_call" | custom-call | flops 6341787648 | bytes 4000000 | tf_op jit(solution)/shard_map/pallas_call | solution.py:427
  35.7 2.2 %collective-permute-start.6 = (f32[2,32,256]{2,1,0:T(8,128)S(1)}, f32[2,32,256]{2,1,0:T(8,128)S(1)}, u32[]{:S(2)}, u32[]{:S(2)}) collective-permute-start(f32[2,32,256]{2,1,0:T(8,128)S(1)} %get-tuple-element.40), channel_id=1, source_target_pairs={{0,4},{1,5},{2,6},{3,7},{4,8},{5,9},{6,10},{7,11},{8,12},{9,13},{1... | collective-permute-start | bytes 196616 | tf_op jit(solution)/shard_map/ppermute | solution.py:356
  37.9 2.5 %collective-permute-start.7 = (f32[2,32,256]{2,1,0:T(8,128)S(1)}, f32[2,32,256]{2,1,0:T(8,128)S(1)}, u32[]{:S(2)}, u32[]{:S(2)}) collective-permute-start(f32[2,32,256]{2,1,0:T(8,128)S(1)} %get-tuple-element.41), channel_id=1, source_target_pairs={{0,8},{1,9},{2,10},{3,11},{4,12},{5,13},{6,14},{7,15},{8,0},{9,1},... | collective-permute-start | bytes 196616 | tf_op jit(solution)/shard_map/ppermute | solution.py:356
  41.2 1.8 %shard_map.31 = (bf16[2,10,32,128]{3,2,1,0:T(8,128)(2,1)S(1)}, bf16[2,10,32,128]{3,2,1,0:T(8,128)(2,1)S(1)}) custom-call(bf16[10,10,32,128]{3,2,1,0:T(8,128)(2,1)S(1)} %get-tuple-element.43.xh.refs_4_, bf16[10,10,32,128]{3,2,1,0:T(8,128)(2,1)S(1)} %get-tuple-element.44.xl.refs_5_, bf16[1280,768]{1,0:T(8,128)(2,1)S(1)} %get-tuple-element.33.encoder), custom_call_target="tpu_custom_call" | custom-call | flops 1811939328 | bytes 4000000 | tf_op jit(solution)/shard_map/pallas_call | solution.py:445
  43.0 2.7 %collective-permute-done.7.refs_2_ = f32[2,32,256]{2,1,0:T(8,128)S(1)} collective-permute-done((f32[2,32,256]{2,1,0:T(8,128)S(1)}, f32[2,32,256]{2,1,0:T(8,128)S(1)}, u32[]{:S(2)}, u32[]{:S(2)}) %collective-permute-start.7) | collective-permute-done | bytes 65568 | tf_op jit(solution)/shard_map/ppermute | solution.py:356
  46.2 2.2 %shard_map.32 = (f32[2,2,27,8,128]{4,3,2,1,0:T(8,128)S(1)}, f32[2,2,27,8,128]{4,3,2,1,0:T(8,128)S(1)}) custom-call(f32[2,32,256]{2,1,0:T(8,128)S(1)} %get-tuple-element.39.refs_0_, f32[2,32,256]{2,1,0:T(8,128)S(1)} %collective-permute-done.6.refs_1_, f32[2,32,256]{2,1,0:T(8,128)S(1)} %collective-permute-done.7.refs_2_, ...), custom_call_target="tpu_custom_call" | custom-call | flops 1811939328 | bytes 4000000 | tf_op jit(solution)/shard_map/pallas_call | solution.py:456
  48.6 1.6 %collective-permute-done.9 = f32[2,2,27,8,128]{4,3,2,1,0:T(8,128)S(1)} collective-permute-done((f32[2,2,27,8,128]{4,3,2,1,0:T(8,128)S(1)}, f32[2,2,27,8,128]{4,3,2,1,0:T(8,128)S(1)}, u32[]{:S(2)}, u32[]{:S(2)}) %collective-permute-start.9) | collective-permute-done | bytes 442400 | tf_op jit(solution)/shard_map/ppermute | solution.py:356
  50.3 1.5 %collective-permute-start.10 = (f32[27,8,128]{2,1,0:T(8,128)S(1)}, f32[27,8,128]{2,1,0:T(8,128)S(1)}, u32[]{:S(2)}, u32[]{:S(2)}) collective-permute-start(f32[27,8,128]{2,1,0:T(8,128)S(1)} %get-tuple-element.55), channel_id=1, source_target_pairs={{0,2},{1,3},{2,0},{3,1},{4,6},{5,7},{6,4},{7,5},{8,10},{9,11},{10,... | collective-permute-start | bytes 331784 | tf_op jit(solution)/shard_map/ppermute | solution.py:356
  53.9 3.2 %collective-permute-done.10 = f32[27,8,128]{2,1,0:T(8,128)S(1)} collective-permute-done((f32[27,8,128]{2,1,0:T(8,128)S(1)}, f32[27,8,128]{2,1,0:T(8,128)S(1)}, u32[]{:S(2)}, u32[]{:S(2)}) %collective-permute-start.10) | collective-permute-done | bytes 110624 | tf_op jit(solution)/shard_map/ppermute | solution.py:356
  57.1 1.6 %collective-permute-done.12 = f32[27,8,128]{2,1,0:T(8,128)S(1)} collective-permute-done((f32[27,8,128]{2,1,0:T(8,128)S(1)}, f32[27,8,128]{2,1,0:T(8,128)S(1)}, u32[]{:S(2)}, u32[]{:S(2)}) %collective-permute-start.12) | collective-permute-done | bytes 110624 | tf_op jit(solution)/shard_map/ppermute | solution.py:356
  59.9 2.2 %collective-permute-start.13 = (f32[18,8,128]{2,1,0:T(8,128)S(1)}, f32[18,8,128]{2,1,0:T(8,128)S(1)}, u32[]{:S(2)}, u32[]{:S(2)}) collective-permute-start(f32[18,8,128]{2,1,0:T(8,128)S(1)} %get-tuple-element.63), channel_id=1, source_target_pairs={{0,4},{1,5},{2,6},{3,7},{4,8},{5,9},{6,10},{7,11},{8,12},{9,13},{1... | collective-permute-start | bytes 221192 | tf_op jit(solution)/shard_map/ppermute | solution.py:356
  62.2 1.6 %collective-permute-start.15 = (f32[18,8,128]{2,1,0:T(8,128)S(1)}, f32[18,8,128]{2,1,0:T(8,128)S(1)}, u32[]{:S(2)}, u32[]{:S(2)}) collective-permute-start(f32[18,8,128]{2,1,0:T(8,128)S(1)} %get-tuple-element.63), channel_id=1, source_target_pairs={{0,12},{1,13},{2,14},{3,15},{4,0},{5,1},{6,2},{7,3},{8,4},{9,5},{1... | collective-permute-start | bytes 221192 | tf_op jit(solution)/shard_map/ppermute | solution.py:356
  63.8 1.6 %collective-permute-start.17 = (f32[9,8,128]{2,1,0:T(8,128)S(1)}, f32[9,8,128]{2,1,0:T(8,128)S(1)}, u32[]{:S(2)}, u32[]{:S(2)}) collective-permute-start(f32[9,8,128]{2,1,0:T(8,128)S(1)} %get-tuple-element.61), channel_id=1, source_target_pairs={{0,2},{1,3},{2,0},{3,1},{4,6},{5,7},{6,4},{7,5},{8,10},{9,11},{10,... | collective-permute-start | bytes 110600 | tf_op jit(solution)/shard_map/ppermute | solution.py:356
  65.4 2.0 %collective-permute-done.14 = f32[18,8,128]{2,1,0:T(8,128)S(1)} collective-permute-done((f32[18,8,128]{2,1,0:T(8,128)S(1)}, f32[18,8,128]{2,1,0:T(8,128)S(1)}, u32[]{:S(2)}, u32[]{:S(2)}) %collective-permute-start.14) | collective-permute-done | bytes 73760 | tf_op jit(solution)/shard_map/ppermute | solution.py:356
  69.8 2.5 %collective-permute-start.18 = (f32[2,9,8,128]{3,2,1,0:T(8,128)S(1)}, f32[2,9,8,128]{3,2,1,0:T(8,128)S(1)}, u32[]{:S(2)}, u32[]{:S(2)}) collective-permute-start(f32[2,9,8,128]{3,2,1,0:T(8,128)S(1)} %get-tuple-element.65), channel_id=1, source_target_pairs={{0,4},{1,5},{2,6},{3,7},{4,8},{5,9},{6,10},{7,11},{8,12},{9,13},{1... | collective-permute-start | bytes 221192 | tf_op jit(solution)/shard_map/ppermute | solution.py:356
  73.6 3.0 %collective-permute-done.19 = f32[2,9,8,128]{3,2,1,0:T(8,128)S(1)} collective-permute-done((f32[2,9,8,128]{3,2,1,0:T(8,128)S(1)}, f32[2,9,8,128]{3,2,1,0:T(8,128)S(1)}, u32[]{:S(2)}, u32[]{:S(2)}) %collective-permute-start.19) | collective-permute-done | bytes 73760 | tf_op jit(solution)/shard_map/ppermute | solution.py:356
  77.9 1.9 %collective-permute-done.22.came_late_ref = f32[4,2,9,8,128]{4,3,2,1,0:T(8,128)S(1)} collective-permute-done((f32[4,2,9,8,128]{4,3,2,1,0:T(8,128)S(1)}, f32[4,2,9,8,128]{4,3,2,1,0:T(8,128)S(1)}, u32[]{:S(2)}, u32[]{:S(2)}) %collective-permute-start.22) | collective-permute-done | bytes 294944 | tf_op jit(solution)/shard_map/ppermute | solution.py:356
  79.8 1.8 %shard_map.33 = f32[3456,128]{1,0:T(8,128)} custom-call(f32[2,4,18,8,128]{4,3,2,1,0:T(8,128)S(1)} %pad_maximum_fusion.early_ref, f32[4,2,9,8,128]{4,3,2,1,0:T(8,128)S(1)} %pad_maximum_fusion.2.late_ref, f32[2,4,18,8,128]{4,3,2,1,0:T(8,128)S(1)} %collective-permute-done.21.came_early_ref, f32[4,2,9,8,128]{4,3,2,1,0:T(8,128)S(1)} %collective-permute-done.22.came_late_ref), custom_call_target="tpu_custom_call" | custom-call | bytes 4000000 | tf_op jit(solution)/shard_map/pallas_call | solution.py:483
  (41 shorter events, 10.8 us)
Async XLA Ops:
  0.0 27.1 %copy-start = (f32[1,3456,128]{2,1,0:T(8,128)S(1)}, f32[1,3456,128]{2,1,0:T(8,128)}, u32[]{:S(2)}) copy-start(f32[1,3456,128]{2,1,0:T(8,128)} %weights_ref.1) | copy-start | bytes 5308420
  2.3 19.3 %collective-permute-start.2 = (f32[1152,128]{1,0:T(8,128)}, f32[1152,128]{1,0:T(8,128)S(1)}, u32[]{:S(2)}, u32[]{:S(2)}) collective-permute-start(f32[1152,128]{1,0:T(8,128)} %get-tuple-element.30), channel_id=1, source_target_pairs={{0,16},{1,17},{2,18},{3,19},{4,20},{5,21},{6,22},{7,23},{8,24},{9,... | collective-permute-start | bytes 1769480 | tf_op jit(solution)/shard_map/ppermute | solution.py:356
  5.3 20.0 %collective-permute-start.4 = (f32[576,128]{1,0:T(8,128)}, f32[576,128]{1,0:T(8,128)S(1)}, u32[]{:S(2)}, u32[]{:S(2)}) collective-permute-start(f32[576,128]{1,0:T(8,128)} %get-tuple-element.32), channel_id=1, source_target_pairs={{0,16},{1,17},{2,18},{3,19},{4,20},{5,21},{6,22},{7,23},{8,24},{9,... | collective-permute-start | bytes 884744 | tf_op jit(solution)/shard_map/ppermute | solution.py:356
  21.6 5.5 %collective-permute-start.3 = (f32[1152,128]{1,0:T(8,128)S(1)}, f32[1152,128]{1,0:T(8,128)S(1)}, u32[]{:S(2)}, u32[]{:S(2)}) collective-permute-start(f32[1152,128]{1,0:T(8,128)S(1)} %collective-permute-done.2.refs_0_), channel_id=1, source_target_pairs={{0,1},{1,0},{2,3},{3,2},{4,5},{5,4},{6,7},{7,6},{8,9},{9,8},{10,11... | collective-permute-start | bytes 1769480 | tf_op jit(solution)/shard_map/ppermute | solution.py:356
  21.7 7.7 %collective-permute-start.1 = (f32[4,2,3,32,128]{4,3,2,1,0:T(8,128)S(1)}, f32[4,2,3,32,128]{4,3,2,1,0:T(8,128)S(1)}, u32[]{:S(2)}, u32[]{:S(2)}) collective-permute-start(f32[4,2,3,32,128]{4,3,2,1,0:T(8,128)S(1)} %get-tuple-element.53), channel_id=1, source_target_pairs={{1,2},{2,1},{5,6},{6,5},{9,10},{10,9},{13,14},{14,13},{17,18},{18,... | collective-permute-start | bytes 1179656 | tf_op jit(solution)/shard_map/ppermute | solution.py:356
  22.4 7.0 %collective-permute-start = (f32[4,2,3,32,128]{4,3,2,1,0:T(8,128)S(1)}, f32[4,2,3,32,128]{4,3,2,1,0:T(8,128)S(1)}, u32[]{:S(2)}, u32[]{:S(2)}) collective-permute-start(f32[4,2,3,32,128]{4,3,2,1,0:T(8,128)S(1)} %get-tuple-element.54), channel_id=1, source_target_pairs={{0,1},{1,0},{2,3},{3,2},{4,5},{5,4},{6,7},{7,6},{8,9},{9,8},{10,11... | collective-permute-start | bytes 1179656 | tf_op jit(solution)/shard_map/ppermute | solution.py:356
  25.3 1.8 %collective-permute-start.5 = (f32[576,128]{1,0:T(8,128)S(1)}, f32[576,128]{1,0:T(8,128)S(1)}, u32[]{:S(2)}, u32[]{:S(2)}) collective-permute-start(f32[576,128]{1,0:T(8,128)S(1)} %collective-permute-done.4.refs_2_), channel_id=1, source_target_pairs={{0,1},{1,0},{2,3},{3,2},{4,5},{5,4},{6,7},{7,6},{8,9},{9,8},{10,11... | collective-permute-start | bytes 884744 | tf_op jit(solution)/shard_map/ppermute | solution.py:356
  35.7 7.3 %collective-permute-start.6 = (f32[2,32,256]{2,1,0:T(8,128)S(1)}, f32[2,32,256]{2,1,0:T(8,128)S(1)}, u32[]{:S(2)}, u32[]{:S(2)}) collective-permute-start(f32[2,32,256]{2,1,0:T(8,128)S(1)} %get-tuple-element.40), channel_id=1, source_target_pairs={{0,4},{1,5},{2,6},{3,7},{4,8},{5,9},{6,10},{7,11},{8,12},{9,13},{1... | collective-permute-start | bytes 196616 | tf_op jit(solution)/shard_map/ppermute | solution.py:356
  37.9 7.7 %collective-permute-start.7 = (f32[2,32,256]{2,1,0:T(8,128)S(1)}, f32[2,32,256]{2,1,0:T(8,128)S(1)}, u32[]{:S(2)}, u32[]{:S(2)}) collective-permute-start(f32[2,32,256]{2,1,0:T(8,128)S(1)} %get-tuple-element.41), channel_id=1, source_target_pairs={{0,8},{1,9},{2,10},{3,11},{4,12},{5,13},{6,14},{7,15},{8,0},{9,1},... | collective-permute-start | bytes 196616 | tf_op jit(solution)/shard_map/ppermute | solution.py:356
  40.5 5.7 %collective-permute-start.8 = (f32[2,32,256]{2,1,0:T(8,128)S(1)}, f32[2,32,256]{2,1,0:T(8,128)S(1)}, u32[]{:S(2)}, u32[]{:S(2)}) collective-permute-start(f32[2,32,256]{2,1,0:T(8,128)S(1)} %get-tuple-element.42), channel_id=1, source_target_pairs={{0,12},{1,13},{2,14},{3,15},{4,0},{5,1},{6,2},{7,3},{8,4},{9,5},{1... | collective-permute-start | bytes 196616 | tf_op jit(solution)/shard_map/ppermute | solution.py:356
  48.4 1.9 %collective-permute-start.9 = (f32[2,2,27,8,128]{4,3,2,1,0:T(8,128)S(1)}, f32[2,2,27,8,128]{4,3,2,1,0:T(8,128)S(1)}, u32[]{:S(2)}, u32[]{:S(2)}) collective-permute-start(f32[2,2,27,8,128]{4,3,2,1,0:T(8,128)S(1)} %get-tuple-element.50), channel_id=1, source_target_pairs={{0,1},{1,0},{2,3},{3,2},{4,5},{5,4},{6,7},{7,6},{8,9},{9,8},{10,11... | collective-permute-start | bytes 1327112 | tf_op jit(solution)/shard_map/ppermute | solution.py:356
  50.3 6.7 %collective-permute-start.10 = (f32[27,8,128]{2,1,0:T(8,128)S(1)}, f32[27,8,128]{2,1,0:T(8,128)S(1)}, u32[]{:S(2)}, u32[]{:S(2)}) collective-permute-start(f32[27,8,128]{2,1,0:T(8,128)S(1)} %get-tuple-element.55), channel_id=1, source_target_pairs={{0,2},{1,3},{2,0},{3,1},{4,6},{5,7},{6,4},{7,5},{8,10},{9,11},{10,... | collective-permute-start | bytes 331784 | tf_op jit(solution)/shard_map/ppermute | solution.py:356
  51.9 6.8 %collective-permute-start.12 = (f32[27,8,128]{2,1,0:T(8,128)S(1)}, f32[27,8,128]{2,1,0:T(8,128)S(1)}, u32[]{:S(2)}, u32[]{:S(2)}) collective-permute-start(f32[27,8,128]{2,1,0:T(8,128)S(1)} %get-tuple-element.56), channel_id=1, source_target_pairs={{0,18},{1,19},{2,16},{3,17},{4,22},{5,23},{6,20},{7,21},{8,26},{9,... | collective-permute-start | bytes 331784 | tf_op jit(solution)/shard_map/ppermute | solution.py:356
  53.3 5.8 %collective-permute-start.11 = (f32[27,8,128]{2,1,0:T(8,128)S(1)}, f32[27,8,128]{2,1,0:T(8,128)S(1)}, u32[]{:S(2)}, u32[]{:S(2)}) collective-permute-start(f32[27,8,128]{2,1,0:T(8,128)S(1)} %get-tuple-element.57), channel_id=1, source_target_pairs={{0,16},{1,17},{2,18},{3,19},{4,20},{5,21},{6,22},{7,23},{8,24},{9,... | collective-permute-start | bytes 331784 | tf_op jit(solution)/shard_map/ppermute | solution.py:356
  59.2 8.2 %collective-permute-start.14 = (f32[18,8,128]{2,1,0:T(8,128)S(1)}, f32[18,8,128]{2,1,0:T(8,128)S(1)}, u32[]{:S(2)}, u32[]{:S(2)}) collective-permute-start(f32[18,8,128]{2,1,0:T(8,128)S(1)} %get-tuple-element.63), channel_id=1, source_target_pairs={{0,8},{1,9},{2,10},{3,11},{4,12},{5,13},{6,14},{7,15},{8,0},{9,1},... | collective-permute-start | bytes 221192 | tf_op jit(solution)/shard_map/ppermute | solution.py:356
  59.9 7.4 %collective-permute-start.13 = (f32[18,8,128]{2,1,0:T(8,128)S(1)}, f32[18,8,128]{2,1,0:T(8,128)S(1)}, u32[]{:S(2)}, u32[]{:S(2)}) collective-permute-start(f32[18,8,128]{2,1,0:T(8,128)S(1)} %get-tuple-element.63), channel_id=1, source_target_pairs={{0,4},{1,5},{2,6},{3,7},{4,8},{5,9},{6,10},{7,11},{8,12},{9,13},{1... | collective-permute-start | bytes 221192 | tf_op jit(solution)/shard_map/ppermute | solution.py:356
  62.2 5.6 %collective-permute-start.15 = (f32[18,8,128]{2,1,0:T(8,128)S(1)}, f32[18,8,128]{2,1,0:T(8,128)S(1)}, u32[]{:S(2)}, u32[]{:S(2)}) collective-permute-start(f32[18,8,128]{2,1,0:T(8,128)S(1)} %get-tuple-element.63), channel_id=1, source_target_pairs={{0,12},{1,13},{2,14},{3,15},{4,0},{5,1},{6,2},{7,3},{8,4},{9,5},{1... | collective-permute-start | bytes 221192 | tf_op jit(solution)/shard_map/ppermute | solution.py:356
  63.8 5.4 %collective-permute-start.17 = (f32[9,8,128]{2,1,0:T(8,128)S(1)}, f32[9,8,128]{2,1,0:T(8,128)S(1)}, u32[]{:S(2)}, u32[]{:S(2)}) collective-permute-start(f32[9,8,128]{2,1,0:T(8,128)S(1)} %get-tuple-element.61), channel_id=1, source_target_pairs={{0,2},{1,3},{2,0},{3,1},{4,6},{5,7},{6,4},{7,5},{8,10},{9,11},{10,... | collective-permute-start | bytes 110600 | tf_op jit(solution)/shard_map/ppermute | solution.py:356
  67.8 9.5 %collective-permute-start.16 = (f32[4,18,8,128]{3,2,1,0:T(8,128)S(1)}, f32[4,18,8,128]{3,2,1,0:T(8,128)S(1)}, u32[]{:S(2)}, u32[]{:S(2)}) collective-permute-start(f32[4,18,8,128]{3,2,1,0:T(8,128)S(1)} %get-tuple-element.59), channel_id=1, source_target_pairs={{0,2},{1,3},{2,0},{3,1},{4,6},{5,7},{6,4},{7,5},{8,10},{9,11},{10,... | collective-permute-start | bytes 884744 | tf_op jit(solution)/shard_map/ppermute | solution.py:356
  69.2 7.4 %collective-permute-start.19 = (f32[2,9,8,128]{3,2,1,0:T(8,128)S(1)}, f32[2,9,8,128]{3,2,1,0:T(8,128)S(1)}, u32[]{:S(2)}, u32[]{:S(2)}) collective-permute-start(f32[2,9,8,128]{3,2,1,0:T(8,128)S(1)} %get-tuple-element.65), channel_id=1, source_target_pairs={{0,8},{1,9},{2,10},{3,11},{4,12},{5,13},{6,14},{7,15},{8,0},{9,1},... | collective-permute-start | bytes 221192 | tf_op jit(solution)/shard_map/ppermute | solution.py:356
  69.8 6.8 %collective-permute-start.18 = (f32[2,9,8,128]{3,2,1,0:T(8,128)S(1)}, f32[2,9,8,128]{3,2,1,0:T(8,128)S(1)}, u32[]{:S(2)}, u32[]{:S(2)}) collective-permute-start(f32[2,9,8,128]{3,2,1,0:T(8,128)S(1)} %get-tuple-element.65), channel_id=1, source_target_pairs={{0,4},{1,5},{2,6},{3,7},{4,8},{5,9},{6,10},{7,11},{8,12},{9,13},{1... | collective-permute-start | bytes 221192 | tf_op jit(solution)/shard_map/ppermute | solution.py:356
  72.3 4.9 %collective-permute-start.20 = (f32[2,9,8,128]{3,2,1,0:T(8,128)S(1)}, f32[2,9,8,128]{3,2,1,0:T(8,128)S(1)}, u32[]{:S(2)}, u32[]{:S(2)}) collective-permute-start(f32[2,9,8,128]{3,2,1,0:T(8,128)S(1)} %get-tuple-element.65), channel_id=1, source_target_pairs={{0,12},{1,13},{2,14},{3,15},{4,0},{5,1},{6,2},{7,3},{8,4},{9,5},{1... | collective-permute-start | bytes 221192 | tf_op jit(solution)/shard_map/ppermute | solution.py:356
  77.3 2.5 %collective-permute-start.21 = (f32[2,4,18,8,128]{4,3,2,1,0:T(8,128)S(1)}, f32[2,4,18,8,128]{4,3,2,1,0:T(8,128)S(1)}, u32[]{:S(2)}, u32[]{:S(2)}) collective-permute-start(f32[2,4,18,8,128]{4,3,2,1,0:T(8,128)S(1)} %pad_maximum_fusion.early_ref), channel_id=1, source_target_pairs={{0,1},{1,0},{2,3},{3,2},{4,5},{5,4},{6,7},{7,6},{8,9},{9,8},{10,11... | collective-permute-start | bytes 1769480 | tf_op jit(solution)/shard_map/ppermute | solution.py:356
  77.4 2.4 %collective-permute-start.22 = (f32[4,2,9,8,128]{4,3,2,1,0:T(8,128)S(1)}, f32[4,2,9,8,128]{4,3,2,1,0:T(8,128)S(1)}, u32[]{:S(2)}, u32[]{:S(2)}) collective-permute-start(f32[4,2,9,8,128]{4,3,2,1,0:T(8,128)S(1)} %pad_maximum_fusion.2.late_ref), channel_id=1, source_target_pairs={{0,1},{1,0},{2,3},{3,2},{4,5},{5,4},{6,7},{7,6},{8,9},{9,8},{10,11... | collective-permute-start | bytes 884744 | tf_op jit(solution)/shard_map/ppermute | solution.py:356
